TPU v7x, 32 devices: a whole 2x2x4 slice. The times are simulated.
32 devices in a mesh: dp: 2 (over x), ctx: 8 (over z, y), tensor: 2 (over core).
Axes of the slice: x: 2, y: 2, z: 4, core: 2. Of those that a mesh axis runs over, the one named last changes fastest.
Arguments:
- input_spikes: int32 [512, 4096], P(None, ('dp', 'ctx')), may hold values from 0 to 65535
- query_spikes: int32 [512, 4096], P('tensor', ('dp', 'ctx')), may hold values from 0 to 65535
- key_spikes: int32 [512, 4096], P('tensor', ('dp', 'ctx')), may hold values from 0 to 65535
- values: bfloat16 [4096, 8192], P(('dp', 'ctx'), 'tensor'), may hold values from -6 to 6
- query_slope: bfloat16 [4096, 8192], P(('dp', 'ctx'), 'tensor'), may hold values from 0.25 to 2
- key_slope: bfloat16 [4096, 8192], P(('dp', 'ctx'), 'tensor'), may hold values from 0.25 to 2
- grad_out: bfloat16 [4096, 8192], P(('dp', 'ctx'), 'tensor'), may hold values from -6 to 6
- log_gate: float32 [64, 4096], P('tensor', ('dp', 'ctx')), may hold values from -0.8 to 0
- pattern: int32 [128, 16], P('tensor'), may hold values from 0 to 127, all different within a row
Outputs:
- query_grad: bfloat16 [4096, 8192], P(('dp', 'ctx'), 'tensor')
- key_grad: bfloat16 [4096, 8192], P(('dp', 'ctx'), 'tensor')
- value_grad: float32 [16, 128, 4096], P('ctx', 'tensor')
Inputs may be any that keep to these rules, and one draw needn't show every extreme that they name: `pattern`: each column block names 16 different row blocks.
All inputs are finite; a program needn't handle non-finite values.
Results may differ from a plain program's by a relative error of at most 0.0073.
Values sent between devices are 32-bit elements; how exact they have to be, the bound alone decides.
No kernel may reach another device: no remote copies, remote signals or barrier semaphores. Data moves between devices by JAX's collectives and lax.ppermute only.
A program may use at most 192 MiB of HBM per device.

v0:
```python
import jax
import jax.numpy as jnp
from jax import lax
from jax.sharding import PartitionSpec as P

D = 8192
HEAD = 128
BLK = 64
SEL = 16


highest = lax.Precision.HIGHEST


def entering(value, axis, combine, identity, reverse):
    devices, place = (lax.axis_size(axis), lax.axis_index(axis))
    everything = jax.tree.map(lambda part: lax.all_gather(part, axis), value)
    start = jax.tree.map(
        lambda part, zero: jnp.broadcast_to(jnp.asarray(zero, part.dtype), part.shape),
        value,
        identity,
    )

    def turn(k, before):
        at = devices - 1 - k if reverse else k
        reached = at > place if reverse else at < place
        new = combine(before, jax.tree.map(lambda part: part[at], everything))
        return jax.tree.map(lambda a, b: jnp.where(reached, a, b), new, before)

    return lax.fori_loop(0, devices, turn, start)


def dims_of(left_dim, right_dim):
    return (((left_dim,), (right_dim,)), ((), ()))


def unpack_flags(packed):
    shifts = jnp.arange(16, dtype=jnp.int32)
    flags = jnp.bitwise_and(jnp.right_shift(packed[:, None, :], shifts[None, :, None]), 1)
    return flags.reshape(packed.shape[0] * 16, packed.shape[1]).astype(jnp.bfloat16)


def decay_matrix(cumulative):
    spread = cumulative[:, None] - cumulative[None, :]
    places = jnp.arange(cumulative.shape[0])
    causal = places[:, None] >= places[None, :]
    return jnp.where(causal, jnp.exp(jnp.minimum(spread, 0.0)), 0.0)


def first_phase(query_cols, key_cols, head_values, cumulative):
    decays = decay_matrix(cumulative)
    intersection = lax.dot_general(
        query_cols, key_cols, dims_of(0, 0), preferred_element_type=jnp.float32
    )
    weights = intersection * decays
    weights_low = weights.astype(jnp.bfloat16)
    local_num = jnp.dot(weights_low, head_values, preferred_element_type=jnp.float32)
    local_den = jnp.sum(weights, axis=1)
    tail_decay = jnp.exp(cumulative[-1] - cumulative)
    key_float = key_cols.astype(jnp.float32) * tail_decay[None, :]
    state_sum = jnp.dot(key_float, head_values.astype(jnp.float32), precision=highest)
    key_sum = jnp.sum(key_float, axis=1)
    return (weights_low, local_num, local_den, jnp.exp(cumulative[-1]), state_sum, key_sum)


def second_phase(
    query_cols,
    key_cols,
    head_values,
    head_grad,
    cumulative,
    weights_low,
    local_num,
    local_den,
    state_in,
    keys_in,
):
    decays = decay_matrix(cumulative)
    lead_decay = jnp.exp(cumulative)
    query_float = query_cols.astype(jnp.float32)
    carried_num = lax.dot_general(query_float, state_in, dims_of(0, 0), precision=highest)
    numerator = local_num + lead_decay[:, None] * carried_num
    denominator = 1.0 + local_den + lead_decay * jnp.dot(keys_in, query_float, precision=highest)
    output = numerator / denominator[:, None]
    grad_float = head_grad.astype(jnp.float32)
    scaled = grad_float / denominator[:, None]
    norm_grad = -jnp.sum(grad_float * output, axis=1) / denominator
    scaled_low = scaled.astype(jnp.bfloat16)
    cross_term = lax.dot_general(
        scaled_low, head_values, dims_of(1, 1), preferred_element_type=jnp.float32
    )
    mixed_low = ((cross_term + norm_grad[:, None]) * decays).astype(jnp.bfloat16)
    carried_query = (
        lax.dot_general(scaled, state_in, dims_of(1, 1), precision=highest)
        + norm_grad[:, None] * keys_in[None, :]
    )
    grad_query = (
        lax.dot_general(mixed_low, key_cols, dims_of(1, 1), preferred_element_type=jnp.float32)
        + lead_decay[:, None] * carried_query
    )
    grad_key = lax.dot_general(
        mixed_low, query_cols, dims_of(0, 1), preferred_element_type=jnp.float32
    )
    grad_value = lax.dot_general(
        weights_low, scaled_low, dims_of(0, 0), preferred_element_type=jnp.float32
    )
    adjoint_sum = jnp.dot(query_float * lead_decay[None, :], scaled, precision=highest)
    adjoint_vec = jnp.dot(query_float, lead_decay * norm_grad, precision=highest)
    return (grad_query, grad_key, grad_value, adjoint_sum, adjoint_vec)


def third_phase(
    key_cols, head_values, cumulative, grad_key_local, grad_value_local, adjoint, adjoint_vec
):
    tail_decay = jnp.exp(cumulative[-1] - cumulative)[:, None]
    value_float = head_values.astype(jnp.float32)
    key_float = key_cols.astype(jnp.float32)
    grad_key = grad_key_local + tail_decay * (
        lax.dot_general(value_float, adjoint, dims_of(1, 1), precision=highest)
        + adjoint_vec[None, :]
    )
    grad_value = grad_value_local + tail_decay * lax.dot_general(
        key_float, adjoint, dims_of(0, 0), precision=highest
    )
    return (grad_key, grad_value)


def combine_forward(earlier_part, later_part):
    total_early, state_early, keys_early = earlier_part
    total_late, state_late, keys_late = later_part
    return (
        total_early * total_late,
        total_late[:, None, None] * state_early + state_late,
        total_late[:, None] * keys_early + keys_late,
    )


def combine_backward(earlier_part, later_part):
    total_early, adjoint_early, vector_early = earlier_part
    total_late, adjoint_late, vector_late = later_part
    return (
        total_early * total_late,
        adjoint_late + total_late[:, None, None] * adjoint_early,
        vector_late + total_late[:, None] * vector_early,
    )


def run_first(block_items):
    return first_phase(*block_items)


def run_second(block_items):
    return second_phase(*block_items)


def per_device(
    input_spikes,
    query_spikes,
    key_spikes,
    values,
    query_slope,
    key_slope,
    grad_out,
    log_gate,
    pattern,
):
    tokens_here = values.shape[0]
    heads_here = values.shape[1] // HEAD
    query_cols = unpack_flags(query_spikes).reshape(heads_here, HEAD, tokens_here)
    key_cols = unpack_flags(key_spikes).reshape(heads_here, HEAD, tokens_here)
    head_values = values.reshape(tokens_here, heads_here, HEAD).transpose(1, 0, 2)
    head_grads = grad_out.reshape(tokens_here, heads_here, HEAD).transpose(1, 0, 2)
    cumulative = jnp.cumsum(log_gate, axis=1)
    weights_low, local_num, local_den, totals, state_sum, key_sum = lax.map(
        run_first, (query_cols, key_cols, head_values, cumulative)
    )
    identity_state = (
        jnp.ones((heads_here,), jnp.float32),
        jnp.zeros((heads_here, HEAD, HEAD), jnp.float32),
        jnp.zeros((heads_here, HEAD), jnp.float32),
    )
    carried_state = entering(
        (totals, state_sum, key_sum), "ctx", combine_forward, identity_state, False
    )
    grad_query, grad_key_local, grad_value_local, adjoint_sum, adjoint_vec = lax.map(
        run_second,
        (
            query_cols,
            key_cols,
            head_values,
            head_grads,
            cumulative,
            weights_low,
            local_num,
            local_den,
            carried_state[1],
            carried_state[2],
        ),
    )
    carried_adjoint = entering(
        (totals, adjoint_sum, adjoint_vec), "ctx", combine_backward, identity_state, True
    )
    grad_key, grad_value = jax.vmap(third_phase)(
        key_cols,
        head_values,
        cumulative,
        grad_key_local,
        grad_value_local,
        carried_adjoint[1],
        carried_adjoint[2],
    )
    width_here = heads_here * HEAD
    flat_query = grad_query.transpose(1, 0, 2).reshape(tokens_here, width_here)
    flat_key = grad_key.transpose(1, 0, 2).reshape(tokens_here, width_here)
    query_grad = (query_slope.astype(jnp.float32) * flat_query).astype(jnp.bfloat16)
    key_grad = (key_slope.astype(jnp.float32) * flat_key).astype(jnp.bfloat16)
    column_blocks = pattern.shape[0]
    value_low = grad_value.transpose(1, 0, 2).reshape(tokens_here, width_here).astype(jnp.bfloat16)
    value_blocks = value_low.reshape(tokens_here, column_blocks, BLK)
    input_cols = unpack_flags(input_spikes)
    row_share = SEL // lax.axis_size("ctx")
    halves = input_cols.reshape(D // BLK, 2, BLK // 2, tokens_here)
    row_order = jnp.arange(lax.axis_size(("dp", "ctx")) * row_share, dtype=jnp.int32)
    half_index = row_order // SEL
    chosen = jnp.take(pattern, row_order % SEL, axis=1).T
    gathered = halves[chosen, half_index[:, None]]
    partial_value = jnp.einsum(
        "snat,tnb->snab", gathered, value_blocks, preferred_element_type=jnp.float32
    )
    reduced = lax.psum_scatter(
        partial_value.reshape(
            lax.axis_size(("dp", "ctx")) * row_share, column_blocks, BLK * BLK // 2
        ),
        ("dp", "ctx"),
        scatter_dimension=0,
        tiled=True,
    )
    value_grad = lax.all_gather(reduced, "dp", axis=2, tiled=True)
    return (query_grad, key_grad, value_grad)


def solution(mesh):
    in_specs = (
        P(None, ("dp", "ctx")),
        P("tensor", ("dp", "ctx")),
        P("tensor", ("dp", "ctx")),
        P(("dp", "ctx"), "tensor"),
        P(("dp", "ctx"), "tensor"),
        P(("dp", "ctx"), "tensor"),
        P(("dp", "ctx"), "tensor"),
        P("tensor", ("dp", "ctx")),
        P("tensor", None),
    )
    out_specs = (P(("dp", "ctx"), "tensor"), P(("dp", "ctx"), "tensor"), P("ctx", "tensor", None))
    return jax.shard_map(
        per_device, mesh=mesh, in_specs=in_specs, out_specs=out_specs, check_vma=False
    )
```

profile of v0, /device:TPU:24, one launch (start us, length us, event | category | flops | bytes accessed | tf_op | source)
XLA Modules:
  0.0 1647.0 jit_solution(58877603333213448)
XLA Ops:
  8.9 3.3 copy.53
  20.5 237.0 %while.72 = (s32[]{:T(128)}, bf16[32,256,256]{1,2,0:T(8,128)(2,1)}, f32[32,256,128]{2,1,0:T(8,128)}, f32[32,256]{1,0:T(8,128)S(1)}, f32[32]{0:T(128)S(1)}, /*ind...) while((s32[]{:T(128)}, bf16[32,256,256]{1,2,0:T(8,128)(2,1)}, ...), condition=%wide.region_5.6_spmd, body=%wide.region_2.5_spmd.sunk | while | flops 84574080 | bytes 1523417 | solution.py:174
  258.8 4.1 copy.50
  264.2 18.8 %all-reduce = f32[256]{0:T(256)S(1)} all-reduce(f32[256]{0:T(256)S(1)} %dynamic-update-slice), channel_id=2, replica_groups=mesh['dp'=2,'ctx'=8,'tensor'=2] {'ctx'}, use_global_device_ids=true, to_apply=%add | all-reduce | flops 256 | bytes 2048
  283.1 32.0 %all-gather.2 = f32[256,128]{1,0:T(8,128)S(1)} all-gather(f32[32,128]{1,0:T(8,128)S(1)} %get-tuple-element.456), channel_id=4, replica_groups=mesh['dp'=2,'ctx'=8,'tensor'=2] {'ctx'}, dimensions={0}, use_global_device_ids=true | all-gather | bytes 147456 | tf_op jit(solution)/shard_map/all_gather | solution.py:17
  315.1 170.6 %all-gather.11.cloned.1.call-done = f32[256,128,128]{2,1,0:T(8,128)} async-done(((f32[32,128,128]{2,1,0:T(8,128)}), f32[256,128,128]{2,1,0:T(8,128)}) %all-gather.11.cloned.1.call-update) | async-done | bytes 16777232 | tf_op jit(solution)/shard_map/all_gather | solution.py:17
  485.7 17.6 %while.74 = (s32[]{:T(128)}, f32[32,128,128]{2,1,0:T(8,128)S(1)}, f32[32,128]{1,0:T(8,128)S(1)}, s32[]{:T(128)}, f32[8,32]{1,0:T(8,128)S(1)}, /*index=5*/f32[8,3...) while((s32[]{:T(128)}, f32[32,128,128]{2,1,0:T(8,128)S(1)}, ...), condition=%wide.region_7.8_spmd.clone, body=%wide.region_6.7_spmd.clone.sunk | while | flops 2113540 | bytes 6341255 | solution.py:30
  504.9 429.8 %while.73 = (s32[]{:T(128)}, f32[32,256,128]{1,2,0:T(8,128)}, f32[32,256,128]{1,2,0:T(8,128)}, f32[32,256,128]{1,2,0:T(8,128)}, f32[32,128,128]{2,1,0:T(8,128)},...) while((s32[]{:T(128)}, f32[32,256,128]{1,2,0:T(8,128)}, ...), condition=%wide.region_10.11_spmd, body=%wide.region_8.10_spmd.sunk | while | flops 220071168 | bytes 2862273 | solution.py:185
  937.0 3.7 and_convert_fusion
  940.7 30.3 %gather_fusion.1 = bf16[2048,32,256]{2,1,0:T(8,128)(2,1)} fusion(bf16[128,2,32,256]{3,2,1,0:T(8,128)(2,1)} %and_convert_fusion, s32[2048]{0:T(1024)S(1)} %reshape.226), kind=kCustom, calls=%fused_computation.1 | custom fusion | bytes 67125248 | tf_op jit(solution)/shard_map/gather | solution.py:226
  971.3 31.0 %all-gather.4 = f32[256,128]{1,0:T(8,128)S(1)} all-gather(f32[32,128]{1,0:T(8,128)S(1)} %get-tuple-element.464), channel_id=6, replica_groups=mesh['dp'=2,'ctx'=8,'tensor'=2] {'ctx'}, dimensions={0}, use_global_device_ids=true | all-gather | bytes 147456 | tf_op jit(solution)/shard_map/all_gather | solution.py:17
  1002.3 159.6 %all-gather.13.cloned.1.call-done = f32[256,128,128]{2,1,0:T(8,128)} async-done(((f32[32,128,128]{2,1,0:T(8,128)}), f32[256,128,128]{2,1,0:T(8,128)}) %all-gather.13.cloned.1.call-update) | async-done | bytes 16777232 | tf_op jit(solution)/shard_map/all_gather | solution.py:17
  1161.9 17.7 %while.75 = (s32[]{:T(128)}, f32[32,128,128]{2,1,0:T(8,128)S(1)}, f32[32,128]{1,0:T(8,128)S(1)}, s32[]{:T(128)}, f32[8,32,128,128]{3,2,1,0:T(8,128)}, /*index=5*...) while((s32[]{:T(128)}, f32[32,128,128]{2,1,0:T(8,128)S(1)}, ...), condition=%wide.region_12.13_spmd.clone, body=%wide.region_11.12_spmd.clone.sunk | while | flops 2113544 | bytes 6341317 | solution.py:30
  1179.6 6.3 add_convert_fusion
  1185.9 23.8 %fusion.82 = f32[32,64,32,64]{3,2,0,1:T(8,128)} fusion(bf16[256,64,64,1]{0,2,3,1:T(8,128)(2,1)} %bitcast.312, bf16[32,64,32,256]{3,2,1,0:T(8,128)(2,1)} %bitcast.305), kind=kOutput, calls=%fused_computation.115 | convolution fusion | flops 2147483648 | bytes 52428800 | tf_op jit(solution)/shard_map/snat,tnb->snab/dot_general | solution.py:227
  1209.6 28.9 %reshape.216 = f32[32,64,2048]{2,0,1:T(8,128)} reshape(f32[32,64,32,64]{3,2,0,1:T(8,128)} %fusion.82) | data formatting | bytes 33554432 | tf_op jit(solution)/shard_map/reshape | solution.py:231
  1238.5 17.7 %copy.68 = f32[32,64,2048]{2,1,0:T(8,128)} copy(f32[32,64,2048]{2,0,1:T(8,128)} %reshape.216) | data formatting | bytes 33554432 | tf_op jit(solution)/shard_map/reshape | solution.py:231
  1256.5 346.4 %reduce-scatter.2.cloned.1.call-done = f32[2,64,2048]{2,1,0:T(8,128)} async-done(((f32[32,64,2048]{2,1,0:T(8,128)}), f32[2,64,2048]{2,1,0:T(8,128)}) %reduce-scatter.2.cloned.1.call-update) | async-done | bytes 1048592 | tf_op jit(solution)/shard_map/reduce_scatter | solution.py:230
  1602.9 5.6 copy.74
  1608.5 7.3 bitcast_add_fusion.4
  1615.8 5.8 copy.64
  1621.6 7.4 multiply_convert_fusion
  1629.0 8.4 all-gather.9.cloned.1.call-done
  1637.4 3.1 copy.168
  (951 shorter events, 693.9 us)
Async XLA Ops:
  7.2 0.8 copy-start
  7.2 478.5 %all-gather.11.cloned.1.call-start = ((), (), s32[]{:S(2)}) async-start(), calls=%async_computation.3 | async-start | bytes 18874368 | tf_op jit(solution)/shard_map/all_gather | solution.py:17
  12.2 2.9 copy-start.2
  12.2 2.9 copy-start.7
  15.1 1.0 copy-start.8
  257.4 1.3 copy-start.3
  257.5 904.4 %all-gather.13.cloned.1.call-start = ((), (), s32[]{:S(2)}) async-start(), calls=%async_computation.4 | async-start | bytes 18874368 | tf_op jit(solution)/shard_map/all_gather | solution.py:17
  258.8 4.1 copy-start.9
  934.7 0.7 copy-start.4
  934.7 1.6 copy-start.6
  934.8 668.1 %reduce-scatter.2.cloned.1.call-start = ((), (), s32[]{:S(2)}) async-start(), calls=%async_computation.1 | async-start | bytes 17825792 | tf_op jit(solution)/shard_map/reduce_scatter | solution.py:230
  1256.2 381.2 %all-gather.9.cloned.1.call-start = ((), (), s32[]{:S(2)}) async-start(), calls=%async_computation.2 | async-start | bytes 3145728 | tf_op jit(solution)/shard_map/all_gather | solution.py:238
  1615.8 5.8 copy-start.5
  1637.4 3.1 copy-start.1
Sparse Core Ops, SparseCore 0:
  257.6 228.0 all-gather.10
  934.9 226.9 all-gather.12
  1256.3 346.4 reduce-scatter.1
  1604.2 33.1 all-gather.8
where the time goes:
time: 1670 us; the launch traced here: 1650 us
  waiting for transfers between devices  685 us (41%)
  matrix products  593 us (36%)
  local copies, waits for them, and re-layouts  172 us (10%)
  blocking collectives  81.8 us (5%)
  other arithmetic  76.3 us (5%)
  loops' own time  24.6 us (1%)
    reduce_scatter x1, waiting for transfers between devices, per_device(): lax.psum_scatter(partial_value.reshape(lax.axis_size(('dp', 'ctx')) * row...  346 us
    all_gather x2, waiting for transfers between devices, entering(): everything = jax.tree.map(lambda part: lax.all_gather(part, axis), value)  330 us
    all_gather x2, blocking collectives, entering(): everything = jax.tree.map(lambda part: lax.all_gather(part, axis), value)  63 us
    dot_general x32, matrix products, second_phase(): jnp.dot(query_float * lead_decay[None, :], scaled, precision=highest)  57.3 us
    dot_general x32, matrix products, second_phase(): lax.dot_general(weights_low, scaled_low, dims_of(0, 0), preferred_element...  56.3 us
    dot_general x32, matrix products, first_phase(): jnp.dot(weights_low, head_values, preferred_element_type=jnp.float32)  55.3 us
    dot_general x32, matrix products, first_phase(): lax.dot_general(query_cols, key_cols, dims_of(0, 0), preferred_element_ty...  55.2 us
    dot_general x32, matrix products, second_phase(): lax.dot_general(mixed_low, key_cols, dims_of(1, 1), preferred_element_typ...  54.3 us
  transfers between devices with their start and end apart: 4, of which 4 were waited for; matrix products, arithmetic and copies ran while one was open for 4% of the time, Pallas kernels for 0%

commit v1 on v0

v1 whole, which is shorter than its diff:
```python
import jax
import jax.numpy as jnp
from jax import lax
from jax.experimental import pallas as pl
from jax.experimental.pallas import tpu as pltpu
from jax.sharding import PartitionSpec as P

HEAD = 128
WORDS = HEAD // 16
BLK = 64
HALF = BLK // 2
SEL = 16
QUAD = 4

F32 = jnp.float32
BF16 = jnp.bfloat16
VMEM_LIMIT = 48 * 1024 * 1024


def params():
    return pltpu.CompilerParams(vmem_limit_bytes=VMEM_LIMIT)


def cost(flops, nbytes):
    return pl.CostEstimate(flops=int(flops), bytes_accessed=int(nbytes), transcendentals=0)


def nn(a, b):
    return lax.dot_general(a, b, (((1,), (0,)), ((), ())), preferred_element_type=F32)


def nt(a, b):
    return lax.dot_general(a, b, (((1,), (1,)), ((), ())), preferred_element_type=F32)


def tn(a, b):
    return lax.dot_general(a, b, (((0,), (0,)), ((), ())), preferred_element_type=F32)


def split(a):
    high = a.astype(BF16)
    return high, (a - high.astype(F32)).astype(BF16)


def fold(a):
    return a[:, :HEAD] + a[:, HEAD:]


def unpack(words):
    tokens = words.shape[1]
    spread = jnp.broadcast_to(words[:, None, :], (WORDS, 16, tokens))
    shifts = lax.broadcasted_iota(jnp.int32, (WORDS, 16, tokens), 1)
    bits = jnp.bitwise_and(jnp.right_shift(spread, shifts), 1)
    return bits.reshape(HEAD, tokens).astype(F32)


def causal(shape, token_axis):
    return lax.broadcasted_iota(jnp.int32, shape, token_axis) >= lax.broadcasted_iota(
        jnp.int32, shape, 1 - token_axis
    )


def lanes(i):
    return slice(i * HEAD, (i + 1) * HEAD)


def rows_of(vector):
    high, low = split(vector)
    low2 = (vector - high.astype(F32) - low.astype(F32)).astype(BF16)
    n = vector.shape[1]
    return jnp.concatenate([high, low, low2, jnp.zeros((13, n), BF16)], axis=0)


def key_sums_kernel(heads, kw, cum, out):
    for i in range(heads):
        row = cum[0, i : i + 1, :]
        tail = jnp.exp(row[:, -1:] - row)
        k = unpack(kw[i * WORDS : (i + 1) * WORDS, :]).astype(BF16)
        out[0, i : i + 1, :] = jnp.sum(nt(rows_of(tail), k), axis=0, keepdims=True)


def summary_kernel(heads, qw, kw, v, cum, y_out, wt_out, den_out, qt_out, kt_out):
    tokens = v.shape[0]
    cols = jnp.transpose(cum[0])
    after = causal((tokens, tokens), 1)
    for i in range(heads):
        row = cum[0, i : i + 1, :]
        col = cols[:, i : i + 1]
        q = unpack(qw[i * WORDS : (i + 1) * WORDS, :])
        k = unpack(kw[i * WORDS : (i + 1) * WORDS, :])
        qt = jnp.transpose(q).astype(BF16)
        kt = jnp.transpose(k).astype(BF16)
        q = q.astype(BF16)
        qt_out[:, lanes(i)] = qt
        kt_out[:, lanes(i)] = kt
        tailed = k * jnp.exp(row[:, -1:] - row)
        high, low = split(tailed)
        value = v[:, lanes(i)]
        y_out[i] = nn(high, value) + nn(low, value)
        decay = jnp.where(after, jnp.exp(jnp.minimum(row - col, 0.0)), 0.0)
        w = nn(kt, q) * decay
        wt_out[i] = w.astype(BF16)
        den_out[0, i : i + 1, :] = jnp.sum(w, axis=0, keepdims=True)


def adjoint_kernel(heads, qw, do, cum, den_local, z0, wt, den_out, x_out, dv_out):
    tokens = do.shape[0]
    rows = []
    qs = []
    for i in range(heads):
        row = cum[0, i : i + 1, :]
        q = unpack(qw[i * WORDS : (i + 1) * WORDS, :]).astype(BF16)
        qs.append(q)
        carried = jnp.sum(nn(rows_of(z0[0, i : i + 1, :]), q), axis=0, keepdims=True)
        rows.append(1.0 + den_local[0, i : i + 1, :] + jnp.exp(row) * carried)
    rows = rows + [jnp.ones((1, tokens), F32)] * (8 - heads)
    den = jnp.concatenate(rows, axis=0)
    den_out[0] = den
    inverse = jnp.transpose(1.0 / den)
    leads = jnp.exp(jnp.transpose(cum[0]))
    for i in range(heads):
        g = do[:, lanes(i)].astype(F32) * inverse[:, i : i + 1]
        x_out[i] = fold(nn(qs[i], jnp.concatenate(split(g * leads[:, i : i + 1]), axis=1)))
        dv_out[0, :, lanes(i)] = nn(wt[i], g.astype(BF16))


def value_kernel(heads, c, kt, dv_local, cum, out):
    cols = jnp.transpose(cum[0])
    for i in range(heads):
        col = cols[:, i : i + 1]
        tail = jnp.exp(col[-1:, :] - col)
        carried = fold(nn(kt[:, lanes(i)], jnp.concatenate(split(c[i]), axis=1)))
        dv = dv_local[0, :, lanes(i)] + tail * carried
        out[0, :, lanes(i)] = dv.astype(BF16).astype(F32)


def token_kernel(heads, s0, c, z0, qt, kt, v, do, den, cum, slope, dq_out, dk_out, xv_out):
    tokens = v.shape[0]
    cols = jnp.transpose(cum[0])
    inverses = jnp.transpose(1.0 / den[0])
    before = causal((tokens, tokens), 0)
    for i in range(heads):
        row = cum[0, i : i + 1, :]
        col = cols[:, i : i + 1]
        inverse = inverses[:, i : i + 1]
        lead = jnp.exp(col)
        tail = jnp.exp(col[-1:, :] - col)
        q = qt[:, lanes(i)]
        k = kt[:, lanes(i)]
        value = v[:, lanes(i)]
        grad = do[:, lanes(i)].astype(F32)
        decay = jnp.where(before, jnp.exp(jnp.minimum(col - row, 0.0)), 0.0)
        w = (nt(q, k) * decay).astype(BF16)
        state = split(s0[i])
        carried = fold(nn(q, jnp.concatenate(state, axis=1)))
        o = (nn(w, value) + lead * carried) * inverse
        h = -jnp.sum(grad * o, axis=1, keepdims=True) * inverse
        g = (grad * inverse).astype(BF16)
        r = ((nt(g, value) + h) * decay).astype(BF16)
        back = fold(nt(g, jnp.concatenate(state, axis=0))) + h * z0[0, i : i + 1, :]
        dq = nn(r, k) + lead * back
        dq_out[:, lanes(i)] = (slope[:, lanes(i)].astype(F32) * dq).astype(BF16)
        carried = fold(nt(value, jnp.concatenate(split(c[i]), axis=0)))
        dk_out[:, lanes(i)] = tn(r, q) + tail * carried
        xv_out[0, i : i + 1, :] = jnp.sum(q.astype(F32) * (lead * h), axis=0, keepdims=True)


def key_kernel(heads, dk, cv, cum, slope, out):
    cols = jnp.transpose(cum[0])
    for i in range(heads):
        col = cols[:, i : i + 1]
        tail = jnp.exp(col[-1:, :] - col)
        total = dk[:, lanes(i)] + tail * cv[0, i : i + 1, :]
        out[:, lanes(i)] = (slope[:, lanes(i)].astype(F32) * total).astype(BF16)


def block_kernel(pattern, *refs):
    spikes, grads, out, flags = refs[:QUAD], refs[QUAD : 2 * QUAD], refs[2 * QUAD], refs[2 * QUAD + 1]
    tokens = grads[0].shape[0]
    step = pl.program_id(0)
    shifts = 2 * lax.broadcasted_iota(jnp.int32, (8, tokens), 0)
    low = lax.broadcasted_iota(jnp.int32, (tokens, HEAD), 1) < BLK
    for side in range(2):
        total = None
        for source in range(QUAD):
            grad = grads[source][...]
            turned = jnp.concatenate([grad[:, BLK:], grad[:, :BLK]], axis=1)
            even, odd = (grad, turned) if side == 0 else (turned, grad)
            right = jnp.concatenate(
                [jnp.where(low, even, 0.0).astype(BF16), jnp.where(low, 0.0, odd).astype(BF16)], axis=0
            )
            for s in range(SEL):
                first = pattern[2 * step + side, s] * (BLK // 16)
                for parity in range(2):
                    parts = []
                    for word in range(BLK // 16):
                        line = spikes[source][pl.ds(first + word, 1), :]
                        spread = jnp.broadcast_to(line, (8, tokens))
                        parts.append(jnp.bitwise_and(jnp.right_shift(spread, shifts + parity), 1))
                    bits = jnp.concatenate(parts, axis=0).astype(F32).astype(BF16)
                    flags[s * HALF : (s + 1) * HALF, parity * tokens : (parity + 1) * tokens] = bits
            part = nn(flags[...], right)
            total = part if total is None else total + part
        out[:, side] = total.reshape(SEL, HALF, HEAD)


def per_device(
    input_spikes,
    query_spikes,
    key_spikes,
    values,
    query_slope,
    key_slope,
    grad_out,
    log_gate,
    pattern,
):
    tokens, width = values.shape
    heads_here = width // HEAD
    heads = heads_here // QUAD
    nctx, ndp = lax.axis_size("ctx"), lax.axis_size("dp")
    nz = nctx // 2
    x, place = lax.axis_index("dp"), lax.axis_index("ctx")
    y, z = place % 2, place // 2

    gate_sums = jnp.cumsum(log_gate, axis=1)
    totals = jnp.exp(gate_sums[:, -1])
    cum = gate_sums.reshape(QUAD, heads, tokens)
    cum = jnp.pad(cum, ((0, 0), (0, 8 - heads), (0, 0)))

    word_spec = pl.BlockSpec((heads * WORDS, tokens), lambda j: (j, 0))
    flat_spec = pl.BlockSpec((tokens, heads * HEAD), lambda j: (0, j))
    quad_spec = pl.BlockSpec((1, tokens, heads * HEAD), lambda j: (j, 0, 0))
    cum_spec = pl.BlockSpec((1, 8, tokens), lambda j: (j, 0, 0))
    vec_spec = pl.BlockSpec((1, 8, HEAD), lambda j: (j, 0, 0))
    state_spec = pl.BlockSpec((heads, HEAD, HEAD), lambda j: (j, 0, 0))
    wt_spec = pl.BlockSpec((heads, tokens, tokens), lambda j: (j, 0, 0))

    def shape(*dims, kind=F32):
        return jax.ShapeDtypeStruct(dims, kind)

    flat16 = shape(tokens, width, kind=BF16)
    flat32 = shape(tokens, width)
    quad32 = shape(QUAD, tokens, heads * HEAD)
    states = shape(heads_here, HEAD, HEAD)
    vecs = shape(QUAD, 8, HEAD)
    cums = shape(QUAD, 8, tokens)
    unit = 2 * tokens * tokens * HEAD * heads_here
    mib = 1 << 20

    def call(kernel, in_specs, out_specs, out_shape, estimate, *args):
        def body(*refs):
            kernel(heads, *refs)

        body.__name__ = kernel.__name__
        return pl.pallas_call(
            body,
            grid=(QUAD,),
            in_specs=in_specs,
            out_specs=out_specs,
            out_shape=out_shape,
            compiler_params=params(),
            cost_estimate=estimate,
            name=kernel.__name__,
        )(*args)

    def swap(value, dx, dy):
        pairs = [
            (d * nctx + c, (d ^ dx) * nctx + (c ^ dy)) for d in range(ndp) for c in range(nctx)
        ]
        return lax.ppermute(value, ("dp", "ctx"), pairs)

    def along(value, delta):
        pairs = [
            (c, c + 2 * delta) for c in range(nctx) if 0 <= c + 2 * delta < nctx
        ]
        return lax.ppermute(value, "ctx", pairs)

    def vec(a):
        return jnp.pad(a.reshape(QUAD, heads, HEAD), ((0, 0), (0, 8 - heads), (0, 0)))

    def unvec(a):
        return a[:, :heads].reshape(heads_here, HEAD)

    def everyone(value):
        parts = [value]
        for k in range(1, nctx):
            parts.append(lax.ppermute(value, "ctx", [(c, (c + k) % nctx) for c in range(nctx)]))
        return parts

    key_sum = call(
        key_sums_kernel, [word_spec, cum_spec], vec_spec, vecs, cost(unit // 16, mib), key_spikes, cum
    )
    message = jnp.concatenate(
        [unvec(key_sum), jnp.broadcast_to(totals[:, None], (heads_here, HEAD))], axis=0
    )
    messages = everyone(message)

    state_sum, wt, den_local, qt, kt = call(
        summary_kernel,
        [word_spec, word_spec, flat_spec, cum_spec],
        [state_spec, wt_spec, cum_spec, flat_spec, flat_spec],
        [states, shape(heads_here, tokens, tokens, kind=BF16), cums, flat16, flat16],
        cost(3 * unit, 14 * mib),
        query_spikes,
        key_spikes,
        values,
        cum,
    )

    z0 = jnp.zeros((heads_here, HEAD), F32)
    for k in range(nctx - 1, 0, -1):
        part = messages[k]
        z0 = jnp.where(place >= k, part[heads_here:] * z0 + part[:heads_here], z0)
    z0 = vec(z0)
    relative = jnp.stack([part[heads_here:, 0] for part in messages])
    decays = jnp.take(relative, (place - jnp.arange(nctx)) % nctx, axis=0)
    pair_decays = decays[0::2] * decays[1::2]

    den, adjoint_sum, dv_local = call(
        adjoint_kernel,
        [word_spec, flat_spec, cum_spec, cum_spec, vec_spec, wt_spec],
        [cum_spec, state_spec, quad_spec],
        [cums, states, quad32],
        cost(3 * unit, 14 * mib),
        query_spikes,
        grad_out,
        cum,
        den_local,
        z0,
        wt,
    )

    half = heads_here // 2
    mine, other = y * half, (1 - y) * half

    def cut(value, start):
        return lax.dynamic_slice_in_dim(value, start, half, 0)

    def decay_at(at):
        row = lax.dynamic_index_in_dim(pair_decays, jnp.clip(at, 0, nz - 1), 0, keepdims=False)
        return cut(row, mine)[:, None, None]

    first_decay = cut(lax.dynamic_index_in_dim(decays, 2 * z, 0, keepdims=False), mine)[:, None, None]
    second_decay = cut(lax.dynamic_index_in_dim(decays, 2 * z + 1, 0, keepdims=False), mine)[:, None, None]

    def carried(value, forward):
        own = cut(value, mine)
        got = swap(cut(value, other), 0, 1)
        first = jnp.where(y == 0, own, got)
        second = jnp.where(y == 0, got, own)
        both = second_decay * first + second if forward else first + first_decay * second
        sign = 1 if forward else -1
        arrived = [along(both, sign * delta) for delta in range(1, nz)]
        reach = arrived[-1]
        for delta in range(nz - 2, 0, -1):
            reach = decay_at(z - sign * delta) * reach + arrived[delta - 1]
        if forward:
            for_first, for_second = reach, first_decay * reach + first
        else:
            for_first, for_second = second + second_decay * reach, reach
        keep = jnp.where(y == 0, for_first, for_second)
        got = swap(jnp.where(y == 0, for_second, for_first), 0, 1)
        return jnp.concatenate([jnp.where(y == 0, keep, got), jnp.where(y == 0, got, keep)], axis=0)

    adjoint = carried(adjoint_sum, False)
    state = carried(state_sum, True)

    value_low = call(
        value_kernel,
        [state_spec, flat_spec, quad_spec, cum_spec],
        quad_spec,
        quad32,
        cost(unit // 2, 12 * mib),
        adjoint,
        kt,
        dv_local,
        cum,
    )

    quad = 2 * x + y
    offsets = [(0, 0), (0, 1), (1, 0), (1, 1)]

    def quarter(dx, dy):
        part = lax.dynamic_index_in_dim(value_low, 2 * (x ^ dx) + (y ^ dy), 0, keepdims=False)
        return part if (dx, dy) == (0, 0) else swap(part, dx, dy)

    grads = [quarter(*offset) for offset in offsets]
    spikes = [input_spikes] + [swap(input_spikes, *offset) for offset in offsets[1:]]

    dq, dk, xv = call(
        token_kernel,
        [state_spec, state_spec, vec_spec] + [flat_spec] * 4 + [cum_spec, cum_spec, flat_spec],
        [flat_spec, flat_spec, vec_spec],
        [flat16, flat32, vecs],
        cost(6 * unit, 20 * mib),
        state,
        adjoint,
        z0,
        qt,
        kt,
        values,
        grad_out,
        den,
        cum,
        query_slope,
    )
    vectors = everyone(unvec(xv))
    cv = jnp.zeros((heads_here, HEAD), F32)
    for k in range(nctx - 1, 0, -1):
        part = vectors[nctx - k]
        at = jnp.clip(place + k, 0, nctx - 1)
        decay = lax.dynamic_index_in_dim(decays, at, 0, keepdims=False)[:, None]
        cv = jnp.where(place + k < nctx, part + decay * cv, cv)
    key_grad = call(
        key_kernel,
        [flat_spec, vec_spec, cum_spec, flat_spec],
        flat_spec,
        flat16,
        cost(1, 8 * mib),
        dk,
        vec(cv),
        cum,
        key_slope,
    )

    columns = pattern.shape[0] // QUAD
    own_pattern = lax.dynamic_slice_in_dim(pattern, quad * columns, columns, 0)
    partial_value = pl.pallas_call(
        block_kernel,
        grid_spec=pltpu.PrefetchScalarGridSpec(
            num_scalar_prefetch=1,
            grid=(columns // 2,),
            in_specs=[pl.BlockSpec(input_spikes.shape, lambda j, p: (0, 0))] * QUAD
            + [pl.BlockSpec((tokens, HEAD), lambda j, p: (0, j))] * QUAD,
            out_specs=pl.BlockSpec((SEL, 2, HALF, HEAD), lambda j, p: (0, j, 0, 0)),
            scratch_shapes=[pltpu.VMEM((SEL * HALF, 2 * tokens), BF16)],
        ),
        out_shape=shape(SEL, columns, HALF, HEAD),
        compiler_params=params(),
        cost_estimate=cost(2 * unit, 10 * mib),
        name="block_kernel",
    )(own_pattern, *spikes, *grads)

    share = SEL // nz
    pieces = partial_value.reshape(nz, share, columns, HALF, HEAD)

    def piece(at):
        return lax.dynamic_index_in_dim(pieces, jnp.clip(at, 0, nz - 1), 0, keepdims=False)

    up = down = None
    for step in range(nz - 1):
        send_up = piece(nz - 1 - step + z)
        send_down = piece(step - (nz - 1 - z))
        if step:
            send_up, send_down = send_up + up, send_down + down
        up = lax.ppermute(
            send_up, "ctx", [(c, c + 2) for c in range(nctx - 2) if c // 2 <= step]
        )
        down = lax.ppermute(
            send_down, "ctx", [(c, c - 2) for c in range(2, nctx) if nz - 1 - c // 2 <= step]
        )
    summed = piece(z) + up + down

    def rows(dx, dy):
        part = lax.dynamic_slice_in_dim(summed, (y ^ dy) * (share // 2), share // 2, 0)
        return part if (dx, dy) == (0, 0) else swap(part, dx, dy)

    parts = [rows(*offset) for offset in offsets]
    parts = [jnp.where(y == 0, parts[i], parts[i ^ 1]) for i in range(QUAD)]
    parts = [jnp.where(x == 0, parts[i], parts[i ^ 2]) for i in range(QUAD)]
    value_grad = jnp.concatenate(parts, axis=1).reshape(share // 2, QUAD * columns, BLK * BLK)
    return (dq, key_grad, value_grad)


def solution(mesh):
    in_specs = (
        P(None, ("dp", "ctx")),
        P("tensor", ("dp", "ctx")),
        P("tensor", ("dp", "ctx")),
        P(("dp", "ctx"), "tensor"),
        P(("dp", "ctx"), "tensor"),
        P(("dp", "ctx"), "tensor"),
        P(("dp", "ctx"), "tensor"),
        P("tensor", ("dp", "ctx")),
        P("tensor", None),
    )
    out_specs = (P(("dp", "ctx"), "tensor"), P(("dp", "ctx"), "tensor"), P("ctx", "tensor", None))
    return jax.shard_map(
        per_device, mesh=mesh, in_specs=in_specs, out_specs=out_specs, check_vma=False
    )
```

time: 1670 us -> 509 us (0.30); the launches traced: 1650 us -> 505 us
  matrix products: 593 us -> 0 us
  waiting for transfers between devices: 685 us -> 250 us
  local copies, waits for them, and re-layouts: 172 us -> 27 us
  starting transfers between devices: 0.38 us -> 129 us
  blocking collectives: 81.8 us -> 0 us
  Pallas kernels: 0 us -> 64.4 us
  other arithmetic: 76.3 us -> 33.1 us
  loops' own time: 24.6 us -> 0 us
    dot_general x387 -> x0, matrix products: 593 us -> none  [the longest x32 57.3 us: second_phase(): jnp.dot(query_float * lead_decay[None, :], scaled, precision=highest)]
    reduce_scatter x1 -> x0, waiting for transfers between devices: 346 us -> none  [per_device(): lax.psum_scatter(partial_value.reshape(lax.axis_size(('dp', 'ctx')) * row...]
    all_gather x3 -> x0, waiting for transfers between devices: 339 us -> none  [the longest x2 330 us: entering(): everything = jax.tree.map(lambda part: lax.all_gather(part, axis), value)]
    ppermute x0 -> x39, waiting for transfers between devices: none -> 250 us  [the longest x6 123 us: along(): return lax.ppermute(value, 'ctx', pairs)]
    ppermute x0 -> x39, starting transfers between devices: none -> 129 us  [the longest x3 75.9 us: per_device(): lax.ppermute(send_down, 'ctx', [(c, c - 2) for c in range(2, nctx) if nz...]
    pallas_call x0 -> x7, Pallas kernels: none -> 64.4 us  [the longest x6 47.6 us: call(): pl.pallas_call(body, grid=(QUAD,), in_specs=in_specs, out_specs=out_specs...]
    all_gather x2 -> x0, blocking collectives: 63 us -> none  [entering(): everything = jax.tree.map(lambda part: lax.all_gather(part, axis), value)]
    reshape x5 -> x4, local copies, waits for them, and re-layouts: 58 us -> 1.72 us  [the longest x1 1.53 us: per_device(): jnp.concatenate(parts, axis=1)]
  transfers between devices with their start and end apart: 4 -> 39, of which waited for: 4 -> 19; matrix products, arithmetic and copies ran while one was open for 4% -> 7% of each run, Pallas kernels for 0% -> 8%
where the time goes in v1:
time: 509 us; the launch traced here: 505 us
  waiting for transfers between devices  250 us (49%)
  starting transfers between devices  129 us (25%)
  Pallas kernels  64.4 us (13%)
  other arithmetic  33.1 us (7%)
  local copies, waits for them, and re-layouts  27 us (5%)
    ppermute x6, waiting for transfers between devices, along(): return lax.ppermute(value, 'ctx', pairs)  123 us
    ppermute x13, waiting for transfers between devices, swap(): return lax.ppermute(value, ('dp', 'ctx'), pairs)  101 us
    ppermute x3, starting transfers between devices, per_device(): lax.ppermute(send_down, 'ctx', [(c, c - 2) for c in range(2, nctx) if nz...  75.9 us
    pallas_call x6, Pallas kernels, call(): pl.pallas_call(body, grid=(QUAD,), in_specs=in_specs, out_specs=out_specs...  47.6 us
    ppermute x14, starting transfers between devices, everyone(): lax.ppermute(value, 'ctx', [(c, (c + k) % nctx) for c in range(nctx)])  20 us
    ppermute x13, starting transfers between devices, swap(): return lax.ppermute(value, ('dp', 'ctx'), pairs)  17 us
    pallas_call x1, Pallas kernels, per_device(): pl.pallas_call(block_kernel, grid_spec=pltpu.PrefetchScalarGridSpec(num_s...  16.8 us
    ppermute x14, waiting for transfers between devices, everyone(): lax.ppermute(value, 'ctx', [(c, (c + k) % nctx) for c in range(nctx)])  16.2 us
  transfers between devices with their start and end apart: 39, of which 19 were waited for; matrix products, arithmetic and copies ran while one was open for 7% of the time, Pallas kernels for 8%

profile of v1, /device:TPU:24, one launch (start us, length us, event | category | flops | bytes accessed | tf_op | source)
XLA Modules:
  0.0 504.7 jit_solution(5846868192873126465)
XLA Ops:
  14.4 8.0 %summary_kernel.1 = (f32[32,128,128]{2,1,0:T(8,128)S(1)}, bf16[32,256,256]{2,1,0:T(8,128)(2,1)}, f32[4,8,256]{2,1,0:T(8,128)S(1)}, bf16[256,4096]{1,0:T(8,128)(2,1)S(1)}, bf16[256,4096]{1,0:T(8,128)(2,1)}) custom-call(s32[256,256]{1,0:T(8,128)S(1)} %copy-done.10, s32[256,256]{1,0:T(8,128)S(1)} %copy-done.13, bf16[256,4096]{1,0:T(8,128)(2,1)} %refs_5_.1, ...), custom_call_target="tpu_custom_call" | custom-call | flops 1610612736 | bytes 14680064 | tf_op jit(solution)/shard_map/summary_kernel/pallas_call | solution.py:256
  31.9 7.7 %adjoint_kernel.1 = (f32[4,8,256]{2,1,0:T(8,128)S(1)}, f32[32,128,128]{2,1,0:T(8,128)S(1)}, f32[4,256,1024]{2,1,0:T(8,128)}) custom-call(s32[256,256]{1,0:T(8,128)S(1)} %copy-done.11, bf16[256,4096]{1,0:T(8,128)(2,1)S(1)} %copy-done.2, f32[4,8,256]{2,1,0:T(8,128)S(1)} %reduce_window_sum.21.refs_1_.refs_3_.refs_2_.refs_8_, ...), custom_call_target="tpu_custom_call" | custom-call | flops 1610612736 | bytes 14680064 | tf_op jit(solution)/shard_map/adjoint_kernel/pallas_call | solution.py:256
  49.4 16.1 %collective-permute-done.12 = f32[16,128,128]{2,1,0:T(8,128)S(1)} collective-permute-done((f32[16,128,128]{2,1,0:T(8,128)}, f32[16,128,128]{2,1,0:T(8,128)S(1)}, u32[]{:S(2)}, u32[]{:S(2)}) %collective-permute-start.12) | collective-permute-done | bytes 1048608 | tf_op jit(solution)/shard_map/ppermute | solution.py:271
  70.2 4.0 collective-permute-start.14
  79.3 13.8 %collective-permute-done.15 = f32[16,128,128]{2,1,0:T(8,128)} collective-permute-done((f32[16,128,128]{2,1,0:T(8,128)}, f32[16,128,128]{2,1,0:T(8,128)}, u32[]{:S(2)}, u32[]{:S(2)}) %collective-permute-start.15) | collective-permute-done | bytes 1048608 | tf_op jit(solution)/shard_map/ppermute | solution.py:277
  93.1 22.5 %collective-permute-done.14 = f32[16,128,128]{2,1,0:T(8,128)} collective-permute-done((f32[16,128,128]{2,1,0:T(8,128)}, f32[16,128,128]{2,1,0:T(8,128)}, u32[]{:S(2)}, u32[]{:S(2)}) %collective-permute-start.14) | collective-permute-done | bytes 1048608 | tf_op jit(solution)/shard_map/ppermute | solution.py:277
  115.6 18.1 %collective-permute-done.13 = f32[16,128,128]{2,1,0:T(8,128)} collective-permute-done((f32[16,128,128]{2,1,0:T(8,128)}, f32[16,128,128]{2,1,0:T(8,128)}, u32[]{:S(2)}, u32[]{:S(2)}) %collective-permute-start.13) | collective-permute-done | bytes 1048608 | tf_op jit(solution)/shard_map/ppermute | solution.py:277
  133.7 3.9 fusion.1
  139.6 24.4 %collective-permute-done.16 = f32[16,128,128]{2,1,0:T(8,128)} collective-permute-done((f32[16,128,128]{2,1,0:T(8,128)}, f32[16,128,128]{2,1,0:T(8,128)}, u32[]{:S(2)}, u32[]{:S(2)}) %collective-permute-start.16) | collective-permute-done | bytes 1048608 | tf_op jit(solution)/shard_map/ppermute | solution.py:271
  164.0 3.7 broadcast_select_fusion.1
  170.6 5.9 %value_kernel.1 = f32[4,256,1024]{2,1,0:T(8,128)} custom-call(f32[32,128,128]{2,1,0:T(8,128)S(1)} %pad_maximum_fusion.1.refs_1_.refs_0_, bf16[256,4096]{1,0:T(8,128)(2,1)S(1)} %copy-done.7, f32[4,256,1024]{2,1,0:T(8,128)} %get-tuple-element.24.refs_2_, f32[4,8,256]{2,1,0:T(8,128)S(1)} %reduce_window_sum.21.refs_1_.refs_3_.refs_2_.refs_8_), custom_call_target="tpu_custom_call" | custom-call | flops 268435456 | bytes 12582912 | tf_op jit(solution)/shard_map/value_kernel/pallas_call | solution.py:256
  176.5 4.0 dynamic-slice_bitcast_fusion.2
  186.2 48.5 %collective-permute-done.25.refs_2_ = s32[512,256]{1,0:T(8,128)} collective-permute-done((s32[512,256]{1,0:T(8,128)}, s32[512,256]{1,0:T(8,128)}, u32[]{:S(2)}, u32[]{:S(2)}) %collective-permute-start.25) | collective-permute-done | bytes 524320 | tf_op jit(solution)/shard_map/ppermute | solution.py:271
  234.7 6.8 %collective-permute-done.26.refs_3_ = s32[512,256]{1,0:T(8,128)} collective-permute-done((s32[512,256]{1,0:T(8,128)}, s32[512,256]{1,0:T(8,128)}, u32[]{:S(2)}, u32[]{:S(2)}) %collective-permute-start.26) | collective-permute-done | bytes 524320 | tf_op jit(solution)/shard_map/ppermute | solution.py:271
  241.5 16.8 %block_kernel.1 = f32[16,16,32,128]{3,2,1,0:T(8,128)} custom-call(s32[16,16]{1,0:T(8,128)S(1)} %copy.53.pattern, s32[512,256]{1,0:T(8,128)} %refs_0_.7, s32[512,256]{1,0:T(8,128)} %collective-permute-done.24.refs_1_, s32[512,256]{1,0:T(8,128)} %collective-permute-done.25.refs_2_, s32[512,256]{1,0:T(8,128)} %collective-permute-done.26.refs_3_, ...), custom_call_target="tpu_custom_call" | custom-call | flops 1073741824 | bytes 10485760 | tf_op jit(solution)/shard_map/block_kernel/pallas_call | solution.py:429
  261.9 25.1 %collective-permute-start.33 = (f32[4,16,32,128]{3,2,1,0:T(8,128)}, f32[4,16,32,128]{3,2,1,0:T(8,128)}, u32[]{:S(2)}, u32[]{:S(2)}) collective-permute-start(f32[4,16,32,128]{3,2,1,0:T(8,128)} %get-tuple-element.36), channel_id=1, source_target_pairs={{12,8},{14,10},{13,9},{15,11},{28,24},{30,26},{29,25},{31,27}} | collective-permute-start | bytes 3145736 | tf_op jit(solution)/shard_map/ppermute | solution.py:460
  298.6 4.0 bitcast_add_fusion.3
  302.6 45.2 %collective-permute-start.34 = (f32[4,16,32,128]{3,2,1,0:T(8,128)}, f32[4,16,32,128]{3,2,1,0:T(8,128)}, u32[]{:S(2)}, u32[]{:S(2)}) collective-permute-start(f32[4,16,32,128]{3,2,1,0:T(8,128)} %get-tuple-element.34), channel_id=1, source_target_pairs={{8,4},{10,6},{12,8},{14,10},{9,5},{11,7},{13,9},{15,11},{24,20},{2... | collective-permute-start | bytes 3145736 | tf_op jit(solution)/shard_map/ppermute | solution.py:460
  347.8 68.7 %collective-permute-done.9 = f32[16,128,128]{2,1,0:T(8,128)} collective-permute-done((f32[16,128,128]{2,1,0:T(8,128)S(1)}, f32[16,128,128]{2,1,0:T(8,128)}, u32[]{:S(2)}, u32[]{:S(2)}) %collective-permute-start.9) | collective-permute-done | bytes 1048608 | tf_op jit(solution)/shard_map/ppermute | solution.py:277
  425.7 5.5 %collective-permute-start.35 = (f32[4,16,32,128]{3,2,1,0:T(8,128)}, f32[4,16,32,128]{3,2,1,0:T(8,128)}, u32[]{:S(2)}, u32[]{:S(2)}) collective-permute-start(f32[4,16,32,128]{3,2,1,0:T(8,128)} %bitcast_add_fusion.1), channel_id=1, source_target_pairs={{4,0},{6,2},{8,4},{10,6},{12,8},{14,10},{5,1},{7,3},{9,5},{11,7},{... | collective-permute-start | bytes 3145736 | tf_op jit(solution)/shard_map/ppermute | solution.py:460
  431.3 5.5 %collective-permute-done.11 = f32[16,128,128]{2,1,0:T(8,128)S(1)} collective-permute-done((f32[16,128,128]{2,1,0:T(8,128)}, f32[16,128,128]{2,1,0:T(8,128)S(1)}, u32[]{:S(2)}, u32[]{:S(2)}) %collective-permute-start.11) | collective-permute-done | bytes 1048608 | tf_op jit(solution)/shard_map/ppermute | solution.py:271
  439.4 5.6 %collective-permute-done.35 = f32[4,16,32,128]{3,2,1,0:T(8,128)} collective-permute-done((f32[4,16,32,128]{3,2,1,0:T(8,128)}, f32[4,16,32,128]{3,2,1,0:T(8,128)}, u32[]{:S(2)}, u32[]{:S(2)}) %collective-permute-start.35) | collective-permute-done | bytes 1048608 | tf_op jit(solution)/shard_map/ppermute | solution.py:460
  451.6 19.5 %token_kernel.1 = (bf16[256,4096]{1,0:T(8,128)(2,1)}, f32[256,4096]{1,0:T(8,128)}, f32[4,8,128]{2,1,0:T(8,128)S(1)}) custom-call(f32[32,128,128]{2,1,0:T(8,128)S(1)} %pad_maximum_fusion.refs_0_, f32[32,128,128]{2,1,0:T(8,128)S(1)} %pad_maximum_fusion.1.refs_1_.refs_0_, f32[4,8,128]{2,1,0:T(8,128)S(1)} %bitcast.85, bf16[256,4096]{1,0:T(8,128)(2,1)} %copy-done.9, ...), custom_call_target="tpu_custom_call" | custom-call | flops 3221225472 | bytes 20971520 | tf_op jit(solution)/shard_map/token_kernel/pallas_call | solution.py:256
  496.2 5.2 %key_kernel.1 = bf16[256,4096]{1,0:T(8,128)(2,1)} custom-call(f32[256,4096]{1,0:T(8,128)} %get-tuple-element.22.refs_0_, f32[4,8,128]{2,1,0:T(8,128)S(1)} %bitcast.86, f32[4,8,256]{2,1,0:T(8,128)S(1)} %reduce_window_sum.21.refs_1_.refs_3_.refs_2_.refs_8_, bf16[256,4096]{1,0:T(8,128)(2,1)S(1)} %copy-done.8), custom_call_target="tpu_custom_call" | custom-call | flops 1 | bytes 8388608 | tf_op jit(solution)/shard_map/key_kernel/pallas_call | solution.py:256
  (159 shorter events, 115.3 us)
Async XLA Ops:
  5.1 20.5 %collective-permute-start = (f32[64,128]{0,1:T(8,128)S(1)}, f32[64,128]{0,1:T(8,128)S(1)}, u32[]{:S(2)}, u32[]{:S(2)}) collective-permute-start(f32[64,128]{0,1:T(8,128)S(1)} %pad_maximum_fusion.3), channel_id=1, source_target_pairs={{0,2},{2,4},{4,6},{6,8},{8,10},{10,12},{12,14},{14,0},{1,3},{3,5},... | collective-permute-start | bytes 98312 | tf_op jit(solution)/shard_map/ppermute | solution.py:288
  6.7 19.3 %collective-permute-start.1 = (f32[64,128]{0,1:T(8,128)S(1)}, f32[64,128]{0,1:T(8,128)S(1)}, u32[]{:S(2)}, u32[]{:S(2)}) collective-permute-start(f32[64,128]{0,1:T(8,128)S(1)} %pad_maximum_fusion.3), channel_id=1, source_target_pairs={{0,4},{2,6},{4,8},{6,10},{8,12},{10,14},{12,0},{14,2},{1,5},{3,7},... | collective-permute-start | bytes 98312 | tf_op jit(solution)/shard_map/ppermute | solution.py:288
  6.9 21.0 %collective-permute-start.2 = (f32[64,128]{0,1:T(8,128)S(1)}, f32[64,128]{0,1:T(8,128)S(1)}, u32[]{:S(2)}, u32[]{:S(2)}) collective-permute-start(f32[64,128]{0,1:T(8,128)S(1)} %pad_maximum_fusion.3), channel_id=1, source_target_pairs={{0,6},{2,8},{4,10},{6,12},{8,14},{10,0},{12,2},{14,4},{1,7},{3,9},... | collective-permute-start | bytes 98312 | tf_op jit(solution)/shard_map/ppermute | solution.py:288
  42.1 23.4 %collective-permute-start.12 = (f32[16,128,128]{2,1,0:T(8,128)}, f32[16,128,128]{2,1,0:T(8,128)S(1)}, u32[]{:S(2)}, u32[]{:S(2)}) collective-permute-start(f32[16,128,128]{2,1,0:T(8,128)} %constant_dynamic-slice_fusion.10), channel_id=1, source_target_pairs={{0,2},{2,0},{4,6},{6,4},{8,10},{10,8},{12,14},{14,12},{16,18},{18,... | collective-permute-start | bytes 3145736 | tf_op jit(solution)/shard_map/ppermute | solution.py:271
  67.9 25.2 %collective-permute-start.15 = (f32[16,128,128]{2,1,0:T(8,128)}, f32[16,128,128]{2,1,0:T(8,128)}, u32[]{:S(2)}, u32[]{:S(2)}) collective-permute-start(f32[16,128,128]{2,1,0:T(8,128)} %multiply_add_fusion.2), channel_id=1, source_target_pairs={{4,0},{6,2},{8,4},{10,6},{12,8},{14,10},{5,1},{7,3},{9,5},{11,7},{... | collective-permute-start | bytes 3145736 | tf_op jit(solution)/shard_map/ppermute | solution.py:277
  70.2 45.5 %collective-permute-start.14 = (f32[16,128,128]{2,1,0:T(8,128)}, f32[16,128,128]{2,1,0:T(8,128)}, u32[]{:S(2)}, u32[]{:S(2)}) collective-permute-start(f32[16,128,128]{2,1,0:T(8,128)} %multiply_add_fusion.2), channel_id=1, source_target_pairs={{8,0},{10,2},{12,4},{14,6},{9,1},{11,3},{13,5},{15,7},{24,16},{26,... | collective-permute-start | bytes 3145736 | tf_op jit(solution)/shard_map/ppermute | solution.py:277
  74.2 59.5 %collective-permute-start.13 = (f32[16,128,128]{2,1,0:T(8,128)}, f32[16,128,128]{2,1,0:T(8,128)}, u32[]{:S(2)}, u32[]{:S(2)}) collective-permute-start(f32[16,128,128]{2,1,0:T(8,128)} %multiply_add_fusion.2), channel_id=1, source_target_pairs={{12,0},{14,2},{13,1},{15,3},{28,16},{30,18},{29,17},{31,19}} | collective-permute-start | bytes 3145736 | tf_op jit(solution)/shard_map/ppermute | solution.py:277
  77.6 62.0 %collective-permute-start.7 = (f32[16,128,128]{2,1,0:T(8,128)}, f32[16,128,128]{2,1,0:T(8,128)}, u32[]{:S(2)}, u32[]{:S(2)}) collective-permute-start(f32[16,128,128]{2,1,0:T(8,128)} %constant_dynamic-slice_fusion.11), channel_id=1, source_target_pairs={{0,2},{2,0},{4,6},{6,4},{8,10},{10,8},{12,14},{14,12},{16,18},{18,... | collective-permute-start | bytes 3145736 | tf_op jit(solution)/shard_map/ppermute | solution.py:271
  137.6 26.4 %collective-permute-start.16 = (f32[16,128,128]{2,1,0:T(8,128)}, f32[16,128,128]{2,1,0:T(8,128)}, u32[]{:S(2)}, u32[]{:S(2)}) collective-permute-start(f32[16,128,128]{2,1,0:T(8,128)} %get-tuple-element.27), channel_id=1, source_target_pairs={{0,2},{2,0},{4,6},{6,4},{8,10},{10,8},{12,14},{14,12},{16,18},{18,... | collective-permute-start | bytes 3145736 | tf_op jit(solution)/shard_map/ppermute | solution.py:271
  139.0 46.4 %collective-permute-start.24 = (s32[512,256]{1,0:T(8,128)}, s32[512,256]{1,0:T(8,128)}, u32[]{:S(2)}, u32[]{:S(2)}) collective-permute-start(s32[512,256]{1,0:T(8,128)} %refs_0_.7), channel_id=1, source_target_pairs={{0,2},{2,0},{4,6},{6,4},{8,10},{10,8},{12,14},{14,12},{16,18},{18,... | collective-permute-start | bytes 1572872 | tf_op jit(solution)/shard_map/ppermute | solution.py:271
  180.5 61.0 %collective-permute-start.27 = (f32[256,1024]{1,0:T(8,128)}, f32[256,1024]{1,0:T(8,128)}, u32[]{:S(2)}, u32[]{:S(2)}) collective-permute-start(f32[256,1024]{1,0:T(8,128)} %get-tuple-element.39), channel_id=1, source_target_pairs={{0,2},{2,0},{4,6},{6,4},{8,10},{10,8},{12,14},{14,12},{16,18},{18,... | collective-permute-start | bytes 3145736 | tf_op jit(solution)/shard_map/ppermute | solution.py:271
  181.1 60.4 %collective-permute-start.28 = (f32[256,1024]{1,0:T(8,128)}, f32[256,1024]{1,0:T(8,128)}, u32[]{:S(2)}, u32[]{:S(2)}) collective-permute-start(f32[256,1024]{1,0:T(8,128)} %get-tuple-element.38), channel_id=1, source_target_pairs={{0,16},{2,18},{4,20},{6,22},{8,24},{10,26},{12,28},{14,30},{16,0},... | collective-permute-start | bytes 3145736 | tf_op jit(solution)/shard_map/ppermute | solution.py:271
  182.5 59.0 %collective-permute-start.29 = (f32[256,1024]{1,0:T(8,128)}, f32[256,1024]{1,0:T(8,128)}, u32[]{:S(2)}, u32[]{:S(2)}) collective-permute-start(f32[256,1024]{1,0:T(8,128)} %get-tuple-element.37), channel_id=1, source_target_pairs={{0,18},{2,16},{4,22},{6,20},{8,26},{10,24},{12,30},{14,28},{16,2},... | collective-permute-start | bytes 3145736 | tf_op jit(solution)/shard_map/ppermute | solution.py:271
  184.0 50.7 %collective-permute-start.25 = (s32[512,256]{1,0:T(8,128)}, s32[512,256]{1,0:T(8,128)}, u32[]{:S(2)}, u32[]{:S(2)}) collective-permute-start(s32[512,256]{1,0:T(8,128)} %refs_0_.7), channel_id=1, source_target_pairs={{0,16},{2,18},{4,20},{6,22},{8,24},{10,26},{12,28},{14,30},{16,0},... | collective-permute-start | bytes 1572872 | tf_op jit(solution)/shard_map/ppermute | solution.py:271
  185.5 56.0 %collective-permute-start.26 = (s32[512,256]{1,0:T(8,128)}, s32[512,256]{1,0:T(8,128)}, u32[]{:S(2)}, u32[]{:S(2)}) collective-permute-start(s32[512,256]{1,0:T(8,128)} %refs_0_.7), channel_id=1, source_target_pairs={{0,18},{2,16},{4,22},{6,20},{8,26},{10,24},{12,30},{14,28},{16,2},... | collective-permute-start | bytes 1572872 | tf_op jit(solution)/shard_map/ppermute | solution.py:271
  261.0 26.0 %collective-permute-start.30 = (f32[4,16,32,128]{3,2,1,0:T(8,128)S(1)}, f32[4,16,32,128]{3,2,1,0:T(8,128)S(1)}, u32[]{:S(2)}, u32[]{:S(2)}) collective-permute-start(f32[4,16,32,128]{3,2,1,0:T(8,128)S(1)} %get-tuple-element.35), channel_id=1, source_target_pairs={{0,4},{2,6},{1,5},{3,7},{16,20},{18,22},{17,21},{19,23}} | collective-permute-start | bytes 3145736 | tf_op jit(solution)/shard_map/ppermute | solution.py:457
  261.9 36.7 %collective-permute-start.33 = (f32[4,16,32,128]{3,2,1,0:T(8,128)}, f32[4,16,32,128]{3,2,1,0:T(8,128)}, u32[]{:S(2)}, u32[]{:S(2)}) collective-permute-start(f32[4,16,32,128]{3,2,1,0:T(8,128)} %get-tuple-element.36), channel_id=1, source_target_pairs={{12,8},{14,10},{13,9},{15,11},{28,24},{30,26},{29,25},{31,27}} | collective-permute-start | bytes 3145736 | tf_op jit(solution)/shard_map/ppermute | solution.py:460
  291.1 56.7 %collective-permute-start.10 = (f32[16,128,128]{2,1,0:T(8,128)S(1)}, f32[16,128,128]{2,1,0:T(8,128)}, u32[]{:S(2)}, u32[]{:S(2)}) collective-permute-start(f32[16,128,128]{2,1,0:T(8,128)S(1)} %copy-done.14), channel_id=1, source_target_pairs={{0,4},{2,6},{4,8},{6,10},{8,12},{10,14},{1,5},{3,7},{5,9},{7,11},{... | collective-permute-start | bytes 3145736 | tf_op jit(solution)/shard_map/ppermute | solution.py:277
  292.4 124.1 %collective-permute-start.9 = (f32[16,128,128]{2,1,0:T(8,128)S(1)}, f32[16,128,128]{2,1,0:T(8,128)}, u32[]{:S(2)}, u32[]{:S(2)}) collective-permute-start(f32[16,128,128]{2,1,0:T(8,128)S(1)} %copy-done.14), channel_id=1, source_target_pairs={{0,8},{2,10},{4,12},{6,14},{1,9},{3,11},{5,13},{7,15},{16,24},{18,... | collective-permute-start | bytes 3145736 | tf_op jit(solution)/shard_map/ppermute | solution.py:277
  293.7 122.8 %collective-permute-start.8 = (f32[16,128,128]{2,1,0:T(8,128)S(1)}, f32[16,128,128]{2,1,0:T(8,128)}, u32[]{:S(2)}, u32[]{:S(2)}) collective-permute-start(f32[16,128,128]{2,1,0:T(8,128)S(1)} %copy-done.14), channel_id=1, source_target_pairs={{0,12},{2,14},{1,13},{3,15},{16,28},{18,30},{17,29},{19,31}} | collective-permute-start | bytes 3145736 | tf_op jit(solution)/shard_map/ppermute | solution.py:277
  302.6 120.4 %collective-permute-start.34 = (f32[4,16,32,128]{3,2,1,0:T(8,128)}, f32[4,16,32,128]{3,2,1,0:T(8,128)}, u32[]{:S(2)}, u32[]{:S(2)}) collective-permute-start(f32[4,16,32,128]{3,2,1,0:T(8,128)} %get-tuple-element.34), channel_id=1, source_target_pairs={{8,4},{10,6},{12,8},{14,10},{9,5},{11,7},{13,9},{15,11},{24,20},{2... | collective-permute-start | bytes 3145736 | tf_op jit(solution)/shard_map/ppermute | solution.py:460
  448.1 53.4 %collective-permute-start.36 = (f32[2,16,32,128]{3,2,1,0:T(8,128)}, f32[2,16,32,128]{3,2,1,0:T(8,128)S(1)}, u32[]{:S(2)}, u32[]{:S(2)}) collective-permute-start(f32[2,16,32,128]{3,2,1,0:T(8,128)} %get-tuple-element.46), channel_id=1, source_target_pairs={{0,2},{2,0},{4,6},{6,4},{8,10},{10,8},{12,14},{14,12},{16,18},{18,... | collective-permute-start | bytes 1572872 | tf_op jit(solution)/shard_map/ppermute | solution.py:271
  448.1 53.4 %collective-permute-start.38 = (f32[2,16,32,128]{3,2,1,0:T(8,128)}, f32[2,16,32,128]{3,2,1,0:T(8,128)}, u32[]{:S(2)}, u32[]{:S(2)}) collective-permute-start(f32[2,16,32,128]{3,2,1,0:T(8,128)} %get-tuple-element.46), channel_id=1, source_target_pairs={{0,18},{2,16},{4,22},{6,20},{8,26},{10,24},{12,30},{14,28},{16,2},... | collective-permute-start | bytes 1572872 | tf_op jit(solution)/shard_map/ppermute | solution.py:271
  450.3 51.2 %collective-permute-start.37 = (f32[2,16,32,128]{3,2,1,0:T(8,128)S(1)}, f32[2,16,32,128]{3,2,1,0:T(8,128)}, u32[]{:S(2)}, u32[]{:S(2)}) collective-permute-start(f32[2,16,32,128]{3,2,1,0:T(8,128)S(1)} %get-tuple-element.45), channel_id=1, source_target_pairs={{0,16},{2,18},{4,20},{6,22},{8,24},{10,26},{12,28},{14,30},{16,0},... | collective-permute-start | bytes 1572872 | tf_op jit(solution)/shard_map/ppermute | solution.py:271
  (34 other events, 421.2 us)

commit v2 on v1

v2 whole, which is shorter than its diff:
```python
import jax
import jax.numpy as jnp
from jax import lax
from jax.experimental import pallas as pl
from jax.experimental.pallas import tpu as pltpu
from jax.sharding import PartitionSpec as P

HEAD = 128
WORDS = HEAD // 16
BLK = 64
HALF = BLK // 2
SEL = 16
QUAD = 4
CHUNKS = 2

F32 = jnp.float32
BF16 = jnp.bfloat16
VMEM_LIMIT = 48 * 1024 * 1024


def params():
    return pltpu.CompilerParams(vmem_limit_bytes=VMEM_LIMIT)


def cost(flops, nbytes):
    return pl.CostEstimate(flops=int(flops), bytes_accessed=int(nbytes), transcendentals=0)


def nn(a, b):
    return lax.dot_general(a, b, (((1,), (0,)), ((), ())), preferred_element_type=F32)


def nt(a, b):
    return lax.dot_general(a, b, (((1,), (1,)), ((), ())), preferred_element_type=F32)


def tn(a, b):
    return lax.dot_general(a, b, (((0,), (0,)), ((), ())), preferred_element_type=F32)


def split(a):
    high = a.astype(BF16)
    return high, (a - high.astype(F32)).astype(BF16)


def fold(a):
    return a[:, :HEAD] + a[:, HEAD:]


def unpack(words):
    tokens = words.shape[1]
    spread = jnp.broadcast_to(words[:, None, :], (WORDS, 16, tokens))
    shifts = lax.broadcasted_iota(jnp.int32, (WORDS, 16, tokens), 1)
    bits = jnp.bitwise_and(jnp.right_shift(spread, shifts), 1)
    return bits.reshape(HEAD, tokens).astype(F32)


def causal(shape, token_axis):
    return lax.broadcasted_iota(jnp.int32, shape, token_axis) >= lax.broadcasted_iota(
        jnp.int32, shape, 1 - token_axis
    )


def lanes(i):
    return slice(i * HEAD, (i + 1) * HEAD)


def rows_of(vector):
    high, low = split(vector)
    low2 = (vector - high.astype(F32) - low.astype(F32)).astype(BF16)
    n = vector.shape[1]
    return jnp.concatenate([high, low, low2, jnp.zeros((13, n), BF16)], axis=0)


def key_sums_kernel(heads, kw, cum, out):
    for i in range(heads):
        row = cum[0, i : i + 1, :]
        tail = jnp.exp(row[:, -1:] - row)
        k = unpack(kw[i * WORDS : (i + 1) * WORDS, :]).astype(BF16)
        out[0, i : i + 1, :] = jnp.sum(nt(rows_of(tail), k), axis=0, keepdims=True)


def summary_kernel(heads, qw, kw, v, cum, y_out, wt_out, den_out, qt_out, kt_out):
    tokens = v.shape[0]
    cols = jnp.transpose(cum[0])
    after = causal((tokens, tokens), 1)
    for i in range(heads):
        row = cum[0, i : i + 1, :]
        col = cols[:, i : i + 1]
        q = unpack(qw[i * WORDS : (i + 1) * WORDS, :])
        k = unpack(kw[i * WORDS : (i + 1) * WORDS, :])
        qt = jnp.transpose(q).astype(BF16)
        kt = jnp.transpose(k).astype(BF16)
        q = q.astype(BF16)
        qt_out[:, lanes(i)] = qt
        kt_out[:, lanes(i)] = kt
        tailed = k * jnp.exp(row[:, -1:] - row)
        high, low = split(tailed)
        value = v[:, lanes(i)]
        y_out[i] = nn(high, value) + nn(low, value)
        decay = jnp.where(after, jnp.exp(jnp.minimum(row - col, 0.0)), 0.0)
        w = nn(kt, q) * decay
        wt_out[i] = w.astype(BF16)
        den_out[0, i : i + 1, :] = jnp.sum(w, axis=0, keepdims=True)


def adjoint_kernel(start, heads, qw, do, cum, den_local, z0, wt, den_out, x_out, dv_out):
    tokens = do.shape[0]
    rows = []
    qs = []
    for i in range(heads):
        at = start + i
        row = cum[0, at : at + 1, :]
        q = unpack(qw[i * WORDS : (i + 1) * WORDS, :]).astype(BF16)
        qs.append(q)
        carried = jnp.sum(nn(rows_of(z0[0, at : at + 1, :]), q), axis=0, keepdims=True)
        rows.append(1.0 + den_local[0, at : at + 1, :] + jnp.exp(row) * carried)
    rows = rows + [jnp.ones((1, tokens), F32)] * (8 - heads)
    den = jnp.concatenate(rows, axis=0)
    den_out[0] = den
    inverse = jnp.transpose(1.0 / den)
    leads = jnp.exp(jnp.transpose(cum[0]))
    for i in range(heads):
        g = do[:, lanes(i)].astype(F32) * inverse[:, i : i + 1]
        lead = leads[:, start + i : start + i + 1]
        x_out[0, i] = fold(nn(qs[i], jnp.concatenate(split(g * lead), axis=1)))
        dv_out[0, :, lanes(i)] = nn(wt[i], g.astype(BF16))


def output_kernel(chunk, heads, s0, qt, kt, v, do, cum, *refs):
    dens, (h_out, xv_out) = refs[:-2], refs[-2:]
    tokens = v.shape[0]
    cols = jnp.transpose(cum[0])
    inverses = [jnp.transpose(1.0 / den[0]) for den in dens]
    before = causal((tokens, tokens), 0)
    for i in range(heads):
        row = cum[0, i : i + 1, :]
        col = cols[:, i : i + 1]
        inverse = inverses[i // chunk][:, i % chunk : i % chunk + 1]
        lead = jnp.exp(col)
        q = qt[:, lanes(i)]
        grad = do[:, lanes(i)].astype(F32)
        decay = jnp.where(before, jnp.exp(jnp.minimum(col - row, 0.0)), 0.0)
        w = (nt(q, kt[:, lanes(i)]) * decay).astype(BF16)
        carried = fold(nn(q, jnp.concatenate(split(s0[i]), axis=1)))
        o = (nn(w, v[:, lanes(i)]) + lead * carried) * inverse
        h = -jnp.sum(grad * o, axis=1, keepdims=True) * inverse
        h_out[0, :, i : i + 1] = h
        xv_out[0, i : i + 1, :] = jnp.sum(q.astype(F32) * (lead * h), axis=0, keepdims=True)


def token_kernel(chunk, heads, turn, s0, c, z0, qt, kt, v, do, cum, slope, h_in, *refs):
    dens, (dq_out, dk_out) = refs[:-2], refs[-2:]
    tokens = v.shape[0]
    cols = jnp.transpose(cum[0])
    inverses = [jnp.transpose(1.0 / den[0]) for den in dens]
    before = causal((tokens, tokens), 0)
    for i in range(heads):
        row = cum[0, i : i + 1, :]
        col = cols[:, i : i + 1]
        inverse = inverses[i // chunk][:, i % chunk : i % chunk + 1]
        lead = jnp.exp(col)
        tail = jnp.exp(col[-1:, :] - col)
        value = v[:, lanes(i)]
        decay = jnp.where(before, jnp.exp(jnp.minimum(col - row, 0.0)), 0.0)
        h = h_in[0, :, i : i + 1]
        g = (do[:, lanes(i)].astype(F32) * inverse).astype(BF16)
        r = ((nt(g, value) + h) * decay).astype(BF16)
        back = fold(nt(g, jnp.concatenate(split(s0[i]), axis=0))) + h * z0[0, i : i + 1, :]
        dq = nn(r, kt[:, lanes(i)]) + lead * back
        dq_out[:, lanes(i)] = (slope[:, lanes(i)].astype(F32) * dq).astype(BF16)
        carried = fold(nt(value, jnp.concatenate(split(c[0, i]), axis=0)))
        dk_out[:, lanes(i)] = tn(r, qt[:, lanes(i)]) + tail * carried


def key_kernel(heads, dk, cv, cum, slope, out):
    cols = jnp.transpose(cum[0])
    for i in range(heads):
        col = cols[:, i : i + 1]
        tail = jnp.exp(col[-1:, :] - col)
        total = dk[:, lanes(i)] + tail * cv[0, i : i + 1, :]
        out[:, lanes(i)] = (slope[:, lanes(i)].astype(F32) * total).astype(BF16)


def block_kernel(start, pattern, *refs):
    spikes, grads, words, cums, adjoints = (refs[QUAD * i : QUAD * (i + 1)] for i in range(5))
    out, flags = refs[5 * QUAD :]
    tokens = grads[0].shape[0]
    step = pl.program_id(0)
    shifts = 2 * lax.broadcasted_iota(jnp.int32, (8, tokens), 0)
    low = lax.broadcasted_iota(jnp.int32, (tokens, HEAD), 1) < BLK
    values = []
    for source in range(QUAD):
        row = cums[source][pl.ds(start + step, 1), :]
        k = unpack(words[source][...].astype(jnp.int32)) * jnp.exp(row[:, -1:] - row)
        carried = fold(tn(k.astype(BF16), jnp.concatenate(split(adjoints[source][0]), axis=1)))
        values.append((grads[source][...] + carried).astype(BF16).astype(F32))
    for side in range(2):
        total = None
        for source in range(QUAD):
            grad = values[source]
            turned = jnp.concatenate([grad[:, BLK:], grad[:, :BLK]], axis=1)
            even, odd = (grad, turned) if side == 0 else (turned, grad)
            right = jnp.concatenate(
                [jnp.where(low, even, 0.0).astype(BF16), jnp.where(low, 0.0, odd).astype(BF16)], axis=0
            )
            for s in range(SEL):
                first = pattern[2 * (start + step) + side, s] * (BLK // 16)
                for parity in range(2):
                    parts = []
                    for word in range(BLK // 16):
                        line = spikes[source][pl.ds(first + word, 1), :]
                        spread = jnp.broadcast_to(line, (8, tokens))
                        parts.append(jnp.bitwise_and(jnp.right_shift(spread, shifts + parity), 1))
                    bits = jnp.concatenate(parts, axis=0).astype(F32).astype(BF16)
                    flags[s * HALF : (s + 1) * HALF, parity * tokens : (parity + 1) * tokens] = bits
            part = nn(flags[...], right)
            total = part if total is None else total + part
        out[:, side] = total.reshape(SEL, HALF, HEAD)


def per_device(
    input_spikes,
    query_spikes,
    key_spikes,
    values,
    query_slope,
    key_slope,
    grad_out,
    log_gate,
    pattern,
):
    tokens, width = values.shape
    heads_here = width // HEAD
    heads = heads_here // QUAD
    chunk = heads // CHUNKS
    nctx, ndp = lax.axis_size("ctx"), lax.axis_size("dp")
    nz = nctx // 2
    x, place = lax.axis_index("dp"), lax.axis_index("ctx")
    y, z = place % 2, place // 2
    quad = 2 * x + y
    offsets = [(0, 0), (0, 1), (1, 0), (1, 1)]

    gate_sums = jnp.cumsum(log_gate, axis=1)
    totals = jnp.exp(gate_sums[:, -1])
    cum = gate_sums.reshape(QUAD, heads, tokens)
    cum = jnp.pad(cum, ((0, 0), (0, 8 - heads), (0, 0)))

    def spec(block, index):
        return pl.BlockSpec(block, lambda j, *refs: index(j))

    word_spec = spec((heads * WORDS, tokens), lambda j: (j, 0))
    flat_spec = spec((tokens, heads * HEAD), lambda j: (0, j))
    cum_spec = spec((1, 8, tokens), lambda j: (j, 0, 0))
    vec_spec = spec((1, 8, HEAD), lambda j: (j, 0, 0))
    state_spec = spec((heads, HEAD, HEAD), lambda j: (j, 0, 0))
    wt_spec = spec((heads, tokens, tokens), lambda j: (j, 0, 0))
    col_spec = spec((1, tokens, 8), lambda j: (j, 0, 0))

    def shape(*dims, kind=F32):
        return jax.ShapeDtypeStruct(dims, kind)

    flat16 = shape(tokens, width, kind=BF16)
    flat32 = shape(tokens, width)
    states = shape(heads_here, HEAD, HEAD)
    vecs = shape(QUAD, 8, HEAD)
    cums = shape(QUAD, 8, tokens)
    unit = 2 * tokens * tokens * HEAD * heads_here
    mib = 1 << 20

    def call(name, kernel, in_specs, out_specs, out_shape, estimate, *args):
        def body(*refs):
            kernel(*refs)

        body.__name__ = name
        return pl.pallas_call(
            body,
            grid=(QUAD,),
            in_specs=in_specs,
            out_specs=out_specs,
            out_shape=out_shape,
            compiler_params=params(),
            cost_estimate=estimate,
            name=name,
        )(*args)

    def swap(value, dx, dy):
        pairs = [
            (d * nctx + c, (d ^ dx) * nctx + (c ^ dy)) for d in range(ndp) for c in range(nctx)
        ]
        return lax.ppermute(value, ("dp", "ctx"), pairs)

    def along(value, delta, only=None):
        pairs = [
            (c, c + 2 * delta)
            for c in range(nctx)
            if 0 <= c + 2 * delta < nctx and (only is None or c // 2 == only)
        ]
        return lax.ppermute(value, "ctx", pairs)

    def vec(a):
        return jnp.pad(a.reshape(QUAD, heads, HEAD), ((0, 0), (0, 8 - heads), (0, 0)))

    def unvec(a):
        return a[:, :heads].reshape(heads_here, HEAD)

    def ordered(own, got):
        return jnp.where(y == 0, own, got), jnp.where(y == 0, got, own)

    def at_group(value, dx, dy):
        return lax.dynamic_index_in_dim(value, 2 * (x ^ dx) + (y ^ dy), 0, keepdims=False)

    spread_totals = jnp.broadcast_to(totals[:, None], (heads_here, HEAD))

    def carried_vectors(vector, forward):
        message = jnp.concatenate([vector, spread_totals], axis=0)
        first, second = ordered(message, swap(message, 0, 1))
        first_decay, second_decay = first[heads_here:], second[heads_here:]
        first, second = first[:heads_here], second[:heads_here]
        both = second_decay * first + second if forward else first + first_decay * second
        message = jnp.concatenate([both, first_decay * second_decay], axis=0)
        sign = 1 if forward else -1
        arrived = [along(message, sign * delta) for delta in range(1, nz)]
        reach = arrived[-1][:heads_here]
        for part in arrived[-2::-1]:
            reach = part[heads_here:] * reach + part[:heads_here]
        if forward:
            return jnp.where(y == 0, reach, first_decay * reach + first)
        return jnp.where(y == 0, second + second_decay * reach, reach)

    key_sum = call(
        "key_sums_kernel",
        lambda *refs: key_sums_kernel(heads, *refs),
        [word_spec, cum_spec],
        vec_spec,
        vecs,
        cost(unit // 16, mib),
        key_spikes,
        cum,
    )
    z0 = vec(carried_vectors(unvec(key_sum), True))

    state_sum, wt, den_local, qt, kt = call(
        "summary_kernel",
        lambda *refs: summary_kernel(heads, *refs),
        [word_spec, word_spec, flat_spec, cum_spec],
        [state_spec, wt_spec, cum_spec, flat_spec, flat_spec],
        [states, shape(heads_here, tokens, tokens, kind=BF16), cums, flat16, flat16],
        cost(3 * unit, 14 * mib),
        query_spikes,
        key_spikes,
        values,
        cum,
    )

    dens, adjoint_sums, value_parts = [], [], []
    for n in range(CHUNKS):
        den, adjoint_sum, value_part = call(
            "adjoint_kernel",
            lambda *refs, n=n: adjoint_kernel(n * chunk, chunk, *refs),
            [
                spec((chunk * WORDS, tokens), lambda j, n=n: (j * CHUNKS + n, 0)),
                spec((tokens, chunk * HEAD), lambda j, n=n: (0, j * CHUNKS + n)),
                cum_spec,
                cum_spec,
                vec_spec,
                spec((chunk, tokens, tokens), lambda j, n=n: (j * CHUNKS + n, 0, 0)),
            ],
            [
                cum_spec,
                spec((1, chunk, HEAD, HEAD), lambda j: (j, 0, 0, 0)),
                spec((1, tokens, chunk * HEAD), lambda j: (j, 0, 0)),
            ],
            [cums, shape(QUAD, chunk, HEAD, HEAD), shape(QUAD, tokens, chunk * HEAD)],
            cost(3 * unit // CHUNKS, 14 * mib // CHUNKS),
            query_spikes,
            grad_out,
            cum,
            den_local,
            z0,
            wt,
        )
        dens.append(den)
        adjoint_sums.append(adjoint_sum)
        value_parts.append(value_part)

    def plane(value):
        return [at_group(value, 0, 0)] + [
            swap(at_group(value, *offset), *offset) for offset in offsets[1:]
        ]

    key_words = jnp.concatenate(
        [key_spikes.reshape(QUAD, heads * WORDS, tokens).astype(F32), cum], axis=1
    )
    key_words = plane(key_words)
    spikes = [input_spikes] + [swap(input_spikes, *offset) for offset in offsets[1:]]

    def pair_of(parts, dx):
        return ordered(parts[2 * dx], parts[2 * dx + 1])

    adjoints = []
    for n in range(CHUNKS):
        parts = plane(adjoint_sums[n])
        gates = [
            jnp.exp(part[heads * WORDS + n * chunk : heads * WORDS + (n + 1) * chunk, -1:])[:, :, None]
            for part in key_words
        ]
        pairs = [pair_of(parts, dx) for dx in range(2)]
        decays = [pair_of(gates, dx) for dx in range(2)]
        both = jnp.stack([pairs[dx][0] + decays[dx][0] * pairs[dx][1] for dx in range(2)])
        decay = jnp.stack([decays[dx][0] * decays[dx][1] for dx in range(2)])
        reach = None
        for hop in range(nz - 1, 0, -1):
            send = both if reach is None else both + decay * reach
            got = along(send, -1, hop)
            reach = got if reach is None else reach + got
        found = []
        for dx in range(2):
            for_second = reach[dx]
            for_first = pairs[dx][1] + decays[dx][1] * for_second
            found += list(ordered(for_first, for_second))
        adjoints.append(found)

    half = heads_here // 2
    mine, other = y * half, (1 - y) * half

    def cut(value, start):
        return lax.dynamic_slice_in_dim(value, start, half, 0)

    first, second = ordered(cut(state_sum, mine), swap(cut(state_sum, other), 0, 1))
    first_decay, second_decay = ordered(spread_totals, swap(spread_totals, 0, 1))
    first_decay = cut(first_decay, mine)[:, :1, None]
    second_decay = cut(second_decay, mine)[:, :1, None]
    both = second_decay * first + second
    reach = None
    for hop in range(nz - 1):
        send = both if reach is None else both + second_decay * first_decay * reach
        got = along(send, 1, hop)
        reach = got if reach is None else reach + got
    keep, send = ordered(reach, first_decay * reach + first)
    state = jnp.concatenate(ordered(keep, swap(send, 0, 1)), axis=0)

    columns = pattern.shape[0] // QUAD
    own_pattern = lax.dynamic_slice_in_dim(pattern, quad * columns, columns, 0)
    share = SEL // nz
    columns = columns // CHUNKS
    results = []
    for n in range(CHUNKS):
        grads = plane(value_parts[n])
        partial_value = pl.pallas_call(
            lambda *refs, n=n: block_kernel(n * chunk, *refs),
            grid_spec=pltpu.PrefetchScalarGridSpec(
                num_scalar_prefetch=1,
                grid=(chunk,),
                in_specs=[spec(input_spikes.shape, lambda j: (0, 0))] * QUAD
                + [spec((tokens, HEAD), lambda j: (0, j))] * QUAD
                + [spec((WORDS, tokens), lambda j, n=n: (j + n * chunk, 0))] * QUAD
                + [spec((8, tokens), lambda j: (heads, 0))] * QUAD
                + [spec((1, HEAD, HEAD), lambda j: (j, 0, 0))] * QUAD,
                out_specs=spec((SEL, 2, HALF, HEAD), lambda j: (0, j, 0, 0)),
                scratch_shapes=[pltpu.VMEM((SEL * HALF, 2 * tokens), BF16)],
            ),
            out_shape=shape(SEL, columns, HALF, HEAD),
            compiler_params=params(),
            cost_estimate=cost(3 * unit // CHUNKS, 16 * mib // CHUNKS),
            name="block_kernel",
        )(own_pattern, *spikes, *grads, *key_words, *key_words, *adjoints[n])

        pieces = partial_value.reshape(nz, share, columns, HALF, HEAD)

        def piece(at):
            return lax.dynamic_index_in_dim(pieces, jnp.clip(at, 0, nz - 1), 0, keepdims=False)

        up = down = None
        for step in range(nz - 1):
            send_up = piece(nz - 1 - step + z)
            send_down = piece(step - (nz - 1 - z))
            if step:
                send_up, send_down = send_up + up, send_down + down
            up = lax.ppermute(
                send_up, "ctx", [(c, c + 2) for c in range(nctx - 2) if c // 2 <= step]
            )
            down = lax.ppermute(
                send_down, "ctx", [(c, c - 2) for c in range(2, nctx) if nz - 1 - c // 2 <= step]
            )
        summed = piece(z) + up + down

        def rows(dx, dy):
            part = lax.dynamic_slice_in_dim(summed, (y ^ dy) * (share // 2), share // 2, 0)
            return part if (dx, dy) == (0, 0) else swap(part, dx, dy)

        parts = [rows(*offset) for offset in offsets]
        parts = [jnp.where(y == 0, parts[i], parts[i ^ 1]) for i in range(QUAD)]
        parts = [jnp.where(x == 0, parts[i], parts[i ^ 2]) for i in range(QUAD)]
        results.append(jnp.stack(parts, axis=1))
    value_grad = jnp.stack(results, axis=2).reshape(share // 2, pattern.shape[0], BLK * BLK)

    h, xv = call(
        "output_kernel",
        lambda *refs: output_kernel(chunk, heads, *refs),
        [state_spec] + [flat_spec] * 4 + [cum_spec] * (1 + CHUNKS),
        [col_spec, vec_spec],
        [shape(QUAD, tokens, 8), vecs],
        cost(3 * unit, 12 * mib),
        state,
        qt,
        kt,
        values,
        grad_out,
        cum,
        *dens,
    )
    cv = vec(carried_vectors(unvec(xv), False))
    returned = [
        jnp.concatenate(
            [
                adjoints[n][i] if i == 0 else swap(adjoints[n][i], *offsets[i])
                for n in range(CHUNKS)
            ],
            axis=0,
        )
        for i in range(QUAD)
    ]
    dq, dk = pl.pallas_call(
        lambda *refs: token_kernel(chunk, heads, *refs),
        grid_spec=pltpu.PrefetchScalarGridSpec(
            num_scalar_prefetch=1,
            grid=(QUAD,),
            in_specs=[
                state_spec,
                pl.BlockSpec((1, heads, HEAD, HEAD), lambda j, turn: (j ^ turn[0], 0, 0, 0)),
                vec_spec,
            ]
            + [flat_spec] * 4
            + [cum_spec, flat_spec, col_spec]
            + [cum_spec] * CHUNKS,
            out_specs=[flat_spec, flat_spec],
        ),
        out_shape=[flat16, flat32],
        compiler_params=params(),
        cost_estimate=cost(5 * unit, 20 * mib),
        name="token_kernel",
    )(
        quad.astype(jnp.int32).reshape(1),
        state,
        jnp.stack(returned),
        z0,
        qt,
        kt,
        values,
        grad_out,
        cum,
        query_slope,
        h,
        *dens,
    )
    key_grad = call(
        "key_kernel",
        lambda *refs: key_kernel(heads, *refs),
        [flat_spec, vec_spec, cum_spec, flat_spec],
        flat_spec,
        flat16,
        cost(1, 8 * mib),
        dk,
        cv,
        cum,
        key_slope,
    )
    return (dq, key_grad, value_grad)


def solution(mesh):
    in_specs = (
        P(None, ("dp", "ctx")),
        P("tensor", ("dp", "ctx")),
        P("tensor", ("dp", "ctx")),
        P(("dp", "ctx"), "tensor"),
        P(("dp", "ctx"), "tensor"),
        P(("dp", "ctx"), "tensor"),
        P(("dp", "ctx"), "tensor"),
        P("tensor", ("dp", "ctx")),
        P("tensor", None),
    )
    out_specs = (P(("dp", "ctx"), "tensor"), P(("dp", "ctx"), "tensor"), P("ctx", "tensor", None))
    return jax.shard_map(
        per_device, mesh=mesh, in_specs=in_specs, out_specs=out_specs, check_vma=False
    )
```

time: 509 us -> 355 us (0.70)
  waiting for transfers between devices: 250 us -> 121 us
  starting transfers between devices: 129 us -> 106 us
  other arithmetic: 33.1 us -> 19.5 us
  Pallas kernels: 64.4 us -> 77.7 us
    ppermute x6 -> x15, waiting for transfers between devices: 123 us -> 16.2 us  [along(): return lax.ppermute(value, 'ctx', pairs)]
    ppermute x3 -> x6, starting transfers between devices: 75.9 us -> 43 us  [per_device(): lax.ppermute(send_down, 'ctx', [(c, c - 2) for c in range(2, nctx) if nz...]
    ppermute x13 -> x35, starting transfers between devices: 17 us -> 41.7 us  [swap(): return lax.ppermute(value, ('dp', 'ctx'), pairs)]
    ppermute x14 -> x0, starting transfers between devices: 20 us -> none  [everyone(): lax.ppermute(value, 'ctx', [(c, (c + k) % nctx) for c in range(nctx)])]
    pallas_call x1 -> x3, Pallas kernels: 16.8 us -> 36.4 us  [the longest x2 20.5 us: per_device(): pl.pallas_call(lambda *refs, n=n: block_kernel(n * chunk, *refs), grid_sp...]
    ppermute x14 -> x0, waiting for transfers between devices: 16.2 us -> none  [everyone(): lax.ppermute(value, 'ctx', [(c, (c + k) % nctx) for c in range(nctx)])]
    select_n x11, other arithmetic: 16.9 us -> 3.84 us  [the longest x9 1.95 us: ordered(): return (jnp.where(y == 0, own, got), jnp.where(y == 0, got, own))]
    ppermute x13 -> x35, waiting for transfers between devices: 101 us -> 92 us  [swap(): return lax.ppermute(value, ('dp', 'ctx'), pairs)]
  transfers between devices with their start and end apart: 39 -> 62, of which waited for: 19 -> 20; matrix products, arithmetic and copies ran while one was open for 7% -> 9% of each run, Pallas kernels for 8% -> 15%
where the time goes in v2:
time: 355 us; the launch traced here: 353 us
  waiting for transfers between devices  121 us (34%)
  starting transfers between devices  106 us (30%)
  Pallas kernels  77.7 us (22%)
  local copies, waits for them, and re-layouts  27.3 us (8%)
  other arithmetic  19.5 us (5%)
    ppermute x35, waiting for transfers between devices, swap(): return lax.ppermute(value, ('dp', 'ctx'), pairs)  92 us
    ppermute x6, starting transfers between devices, per_device(): lax.ppermute(send_down, 'ctx', [(c, c - 2) for c in range(2, nctx) if nz...  43 us
    ppermute x35, starting transfers between devices, swap(): return lax.ppermute(value, ('dp', 'ctx'), pairs)  41.7 us
    pallas_call x6, Pallas kernels, call(): pl.pallas_call(body, grid=(QUAD,), in_specs=in_specs, out_specs=out_specs...  41.3 us
    pallas_call x2, Pallas kernels, per_device(): pl.pallas_call(lambda *refs, n=n: block_kernel(n * chunk, *refs), grid_sp...  20.5 us
    ppermute x15, starting transfers between devices, along(): return lax.ppermute(value, 'ctx', pairs)  16.3 us
    ppermute x15, waiting for transfers between devices, along(): return lax.ppermute(value, 'ctx', pairs)  16.2 us
    pallas_call x1, Pallas kernels, per_device(): pl.pallas_call(lambda *refs: token_kernel(chunk, heads, *refs), grid_spec...  15.9 us
  transfers between devices with their start and end apart: 62, of which 20 were waited for; matrix products, arithmetic and copies ran while one was open for 9% of the time, Pallas kernels for 15%

profile of v2, /device:TPU:24, one launch (start us, length us, event | category | flops | bytes accessed | tf_op | source)
XLA Modules:
  0.0 353.5 jit_solution(9356516846223913350)
XLA Ops:
  11.4 7.8 %summary_kernel.1 = (f32[32,128,128]{2,1,0:T(8,128)S(1)}, bf16[32,256,256]{2,1,0:T(8,128)(2,1)}, f32[4,8,256]{2,1,0:T(8,128)S(1)}, bf16[256,4096]{1,0:T(8,128)(2,1)S(1)}, bf16[256,4096]{1,0:T(8,128)(2,1)}) custom-call(s32[256,256]{1,0:T(8,128)S(1)} %copy-done.10, s32[256,256]{1,0:T(8,128)S(1)} %copy-done.13, bf16[256,4096]{1,0:T(8,128)(2,1)} %refs_6_.1, ...), custom_call_target="tpu_custom_call" | custom-call | flops 1610612736 | bytes 14680064 | tf_op jit(solution)/shard_map/summary_kernel/pallas_call | solution.py:276
  41.5 5.1 %adjoint_kernel.3 = (f32[4,8,256]{2,1,0:T(8,128)S(1)}, f32[4,4,128,128]{3,2,1,0:T(8,128)S(1)}, f32[4,256,512]{2,1,0:T(8,128)S(1)}) custom-call(s32[256,256]{1,0:T(8,128)S(1)} %copy-done.11, bf16[256,4096]{1,0:T(8,128)(2,1)S(1)} %copy-done.2, f32[4,8,256]{2,1,0:T(8,128)S(1)} %reduce_window_sum.21.refs_3_.refs_1_.refs_2_.refs_5_.refs_8_, ...), custom_call_target="tpu_custom_call" | custom-call | flops 805306368 | bytes 7340032 | tf_op jit(solution)/shard_map/adjoint_kernel/pallas_call | solution.py:276
  46.6 4.9 %adjoint_kernel.2 = (f32[4,8,256]{2,1,0:T(8,128)S(1)}, f32[4,4,128,128]{3,2,1,0:T(8,128)S(1)}, f32[4,256,512]{2,1,0:T(8,128)S(1)}) custom-call(s32[256,256]{1,0:T(8,128)S(1)} %copy-done.11, bf16[256,4096]{1,0:T(8,128)(2,1)S(1)} %copy-done.2, f32[4,8,256]{2,1,0:T(8,128)S(1)} %reduce_window_sum.21.refs_3_.refs_1_.refs_2_.refs_5_.refs_8_, ...), custom_call_target="tpu_custom_call" | custom-call | flops 805306368 | bytes 7340032 | tf_op jit(solution)/shard_map/adjoint_kernel/pallas_call | solution.py:276
  52.2 2.5 collective-permute-start.21
  56.4 4.4 %collective-permute-done.20 = f32[4,128,128]{2,1,0:T(8,128)S(1)} collective-permute-done((f32[4,128,128]{2,1,0:T(8,128)S(1)}, f32[4,128,128]{2,1,0:T(8,128)S(1)}, u32[]{:S(2)}, u32[]{:S(2)}) %collective-permute-start.20) | collective-permute-done | bytes 262176 | tf_op jit(solution)/shard_map/ppermute | solution.py:291
  62.4 5.1 %collective-permute-done.21 = f32[4,128,128]{2,1,0:T(8,128)S(1)} collective-permute-done((f32[4,128,128]{2,1,0:T(8,128)S(1)}, f32[4,128,128]{2,1,0:T(8,128)S(1)}, u32[]{:S(2)}, u32[]{:S(2)}) %collective-permute-start.21) | collective-permute-done | bytes 262176 | tf_op jit(solution)/shard_map/ppermute | solution.py:291
  73.7 9.4 %collective-permute-done.12 = f32[4,128,128]{2,1,0:T(8,128)S(1)} collective-permute-done((f32[4,128,128]{2,1,0:T(8,128)S(1)}, f32[4,128,128]{2,1,0:T(8,128)S(1)}, u32[]{:S(2)}, u32[]{:S(2)}) %collective-permute-start.12) | collective-permute-done | bytes 262176 | tf_op jit(solution)/shard_map/ppermute | solution.py:291
  90.1 7.2 %collective-permute-done.16 = f32[2,4,128,128]{3,2,1,0:T(8,128)S(1)} collective-permute-done((f32[2,4,128,128]{3,2,1,0:T(8,128)S(1)}, f32[2,4,128,128]{3,2,1,0:T(8,128)S(1)}, u32[]{:S(2)}, u32[]{:S(2)}) %collective-permute-start.16) | collective-permute-done | bytes 524320 | tf_op jit(solution)/shard_map/ppermute | solution.py:299
  104.8 25.1 %collective-permute-done.1 = f32[16,128,128]{2,1,0:T(8,128)S(1)} collective-permute-done((f32[16,128,128]{2,1,0:T(8,128)S(1)}, f32[16,128,128]{2,1,0:T(8,128)S(1)}, u32[]{:S(2)}, u32[]{:S(2)}) %collective-permute-start.1) | collective-permute-done | bytes 1048608 | tf_op jit(solution)/shard_map/ppermute | solution.py:291
  133.0 13.8 %collective-permute-done.50.refs_6_ = f32[256,512]{1,0:T(8,128)S(1)} collective-permute-done((f32[256,512]{1,0:T(8,128)S(1)}, f32[256,512]{1,0:T(8,128)S(1)}, u32[]{:S(2)}, u32[]{:S(2)}) %collective-permute-start.50) | collective-permute-done | bytes 524320 | tf_op jit(solution)/shard_map/ppermute | solution.py:291
  149.6 10.3 %block_kernel.3 = f32[16,8,32,128]{3,2,1,0:T(8,128)} custom-call(s32[16,16]{1,0:T(8,128)S(1)} %copy-done.16, s32[512,256]{1,0:T(8,128)S(1)} %copy-done.8, s32[512,256]{1,0:T(8,128)S(1)} %collective-permute-done.35.refs_2_, s32[512,256]{1,0:T(8,128)S(1)} %collective-permute-done.36.refs_3_, s32[512,256]{1,0:T(8,128)S(1)} %collective-permute-done.37.refs_4_, ...), custom_call_target="tpu_custom_call" | custom-call | flops 805306368 | bytes 8388608 | tf_op jit(solution)/shard_map/block_kernel/pallas_call | solution.py:450
  169.6 10.2 %block_kernel.2 = f32[16,8,32,128]{3,2,1,0:T(8,128)} custom-call(s32[16,16]{1,0:T(8,128)S(1)} %copy-done.16, s32[512,256]{1,0:T(8,128)S(1)} %copy-done.8, s32[512,256]{1,0:T(8,128)S(1)} %collective-permute-done.35.refs_2_, s32[512,256]{1,0:T(8,128)S(1)} %collective-permute-done.36.refs_3_, s32[512,256]{1,0:T(8,128)S(1)} %collective-permute-done.37.refs_4_, ...), custom_call_target="tpu_custom_call" | custom-call | flops 805306368 | bytes 8388608 | tf_op jit(solution)/shard_map/block_kernel/pallas_call | solution.py:450
  199.3 5.7 %collective-permute-done.44 = f32[4,8,32,128]{3,2,1,0:T(8,128)S(1)} collective-permute-done((f32[4,8,32,128]{3,2,1,0:T(8,128)S(1)}, f32[4,8,32,128]{3,2,1,0:T(8,128)S(1)}, u32[]{:S(2)}, u32[]{:S(2)}) %collective-permute-start.44) | collective-permute-done | bytes 524320 | tf_op jit(solution)/shard_map/ppermute | solution.py:483
  205.0 4.4 %collective-permute-start.57 = (f32[4,8,32,128]{3,2,1,0:T(8,128)S(1)}, f32[4,8,32,128]{3,2,1,0:T(8,128)S(1)}, u32[]{:S(2)}, u32[]{:S(2)}) collective-permute-start(f32[4,8,32,128]{3,2,1,0:T(8,128)S(1)} %get-tuple-element.65), channel_id=1, source_target_pairs={{8,4},{10,6},{12,8},{14,10},{9,5},{11,7},{13,9},{15,11},{24,20},{2... | collective-permute-start | bytes 1572872 | tf_op jit(solution)/shard_map/ppermute | solution.py:483
  211.0 25.6 %collective-permute-start.45 = (f32[4,8,32,128]{3,2,1,0:T(8,128)S(1)}, f32[4,8,32,128]{3,2,1,0:T(8,128)S(1)}, u32[]{:S(2)}, u32[]{:S(2)}) collective-permute-start(f32[4,8,32,128]{3,2,1,0:T(8,128)S(1)} %get-tuple-element.57), channel_id=1, source_target_pairs={{8,4},{10,6},{12,8},{14,10},{9,5},{11,7},{13,9},{15,11},{24,20},{2... | collective-permute-start | bytes 1572872 | tf_op jit(solution)/shard_map/ppermute | solution.py:483
  238.2 4.6 %collective-permute-start.58 = (f32[4,8,32,128]{3,2,1,0:T(8,128)S(1)}, f32[4,8,32,128]{3,2,1,0:T(8,128)S(1)}, u32[]{:S(2)}, u32[]{:S(2)}) collective-permute-start(f32[4,8,32,128]{3,2,1,0:T(8,128)S(1)} %bitcast_add_fusion.1), channel_id=1, source_target_pairs={{4,0},{6,2},{8,4},{10,6},{12,8},{14,10},{5,1},{7,3},{9,5},{11,7},{... | collective-permute-start | bytes 1572872 | tf_op jit(solution)/shard_map/ppermute | solution.py:483
  247.7 4.4 %collective-permute-start.46 = (f32[4,8,32,128]{3,2,1,0:T(8,128)S(1)}, f32[4,8,32,128]{3,2,1,0:T(8,128)S(1)}, u32[]{:S(2)}, u32[]{:S(2)}) collective-permute-start(f32[4,8,32,128]{3,2,1,0:T(8,128)S(1)} %bitcast_add_fusion.6), channel_id=1, source_target_pairs={{4,0},{6,2},{8,4},{10,6},{12,8},{14,10},{5,1},{7,3},{9,5},{11,7},{... | collective-permute-start | bytes 1572872 | tf_op jit(solution)/shard_map/ppermute | solution.py:483
  256.5 5.2 %collective-permute-done.4 = f32[16,128,128]{2,1,0:T(8,128)S(1)} collective-permute-done((f32[16,128,128]{2,1,0:T(8,128)S(1)}, f32[16,128,128]{2,1,0:T(8,128)S(1)}, u32[]{:S(2)}, u32[]{:S(2)}) %collective-permute-start.4) | collective-permute-done | bytes 1048608 | tf_op jit(solution)/shard_map/ppermute | solution.py:299
  263.6 3.8 %collective-permute-done.43 = f32[4,8,32,128]{3,2,1,0:T(8,128)S(1)} collective-permute-done((f32[4,8,32,128]{3,2,1,0:T(8,128)S(1)}, f32[4,8,32,128]{3,2,1,0:T(8,128)S(1)}, u32[]{:S(2)}, u32[]{:S(2)}) %collective-permute-start.43) | collective-permute-done | bytes 524320 | tf_op jit(solution)/shard_map/ppermute | solution.py:480
  272.8 23.0 %collective-permute-done.47 = f32[2,8,32,128]{3,2,1,0:T(8,128)S(1)} collective-permute-done((f32[2,8,32,128]{3,2,1,0:T(8,128)S(1)}, f32[2,8,32,128]{3,2,1,0:T(8,128)S(1)}, u32[]{:S(2)}, u32[]{:S(2)}) %collective-permute-start.47) | collective-permute-done | bytes 262176 | tf_op jit(solution)/shard_map/ppermute | solution.py:291
  299.7 16.9 %output_kernel.1 = (f32[4,256,8]{2,1,0:T(8,128)S(1)}, f32[4,8,128]{2,1,0:T(8,128)S(1)}) custom-call(f32[32,128,128]{2,1,0:T(8,128)S(1)} %pad_maximum_fusion.refs_0_.refs_1_, bf16[256,4096]{1,0:T(8,128)(2,1)S(1)} %copy-done.6, bf16[256,4096]{1,0:T(8,128)(2,1)} %get-tuple-element.24.refs_2_.refs_5_, bf16[256,4096]{1,0:T(8,128)(2,1)} %refs_6_.1, ...), custom_call_target="tpu_custom_call" | custom-call | flops 1610612736 | bytes 12582912 | tf_op jit(solution)/shard_map/output_kernel/pallas_call | solution.py:276
  321.7 2.7 reshape.370
  330.4 15.9 %token_kernel.1 = (bf16[256,4096]{1,0:T(8,128)(2,1)}, f32[256,4096]{1,0:T(8,128)}) custom-call(s32[1]{0:T(128)} %bitcast.refs_0_, f32[32,128,128]{2,1,0:T(8,128)S(1)} %pad_maximum_fusion.refs_0_.refs_1_, f32[4,8,128,128]{3,2,1,0:T(8,128)S(1)} %copy-done.7, f32[4,8,128]{2,1,0:T(8,128)S(1)} %bitcast.188, bf16[256,4096]{1,0:T(8,128)(2,1)} %copy-done.5, ...), custom_call_target="tpu_custom_call" | custom-call | flops 2684354560 | bytes 20971520 | tf_op jit(solution)/shard_map/token_kernel/pallas_call | solution.py:524
  348.2 5.2 %key_kernel.1 = bf16[256,4096]{1,0:T(8,128)(2,1)} custom-call(f32[256,4096]{1,0:T(8,128)} %get-tuple-element.29.refs_0_, f32[4,8,128]{2,1,0:T(8,128)S(1)} %bitcast.189, f32[4,8,256]{2,1,0:T(8,128)S(1)} %reduce_window_sum.21.refs_3_.refs_1_.refs_2_.refs_5_.refs_8_, bf16[256,4096]{1,0:T(8,128)(2,1)S(1)} %copy-done.9), custom_call_target="tpu_custom_call" | custom-call | flops 1 | bytes 8388608 | tf_op jit(solution)/shard_map/key_kernel/pallas_call | solution.py:276
  (267 shorter events, 128.4 us)
Async XLA Ops:
  8.4 43.8 %collective-permute-start.11 = (f32[72,256]{1,0:T(8,128)}, f32[72,256]{1,0:T(8,128)S(1)}, u32[]{:S(2)}, u32[]{:S(2)}) collective-permute-start(f32[72,256]{1,0:T(8,128)} %get-tuple-element.102), channel_id=1, source_target_pairs={{0,2},{2,0},{4,6},{6,4},{8,10},{10,8},{12,14},{14,12},{16,18},{18,... | collective-permute-start | bytes 221192 | tf_op jit(solution)/shard_map/ppermute | solution.py:291
  8.9 46.1 %collective-permute-start.14 = (f32[72,256]{1,0:T(8,128)}, f32[72,256]{1,0:T(8,128)S(1)}, u32[]{:S(2)}, u32[]{:S(2)}) collective-permute-start(f32[72,256]{1,0:T(8,128)} %get-tuple-element.104), channel_id=1, source_target_pairs={{0,16},{2,18},{4,20},{6,22},{8,24},{10,26},{12,28},{14,30},{16,0},... | collective-permute-start | bytes 221192 | tf_op jit(solution)/shard_map/ppermute | solution.py:291
  34.4 66.0 %collective-permute-start.35 = (s32[512,256]{1,0:T(8,128)S(1)}, s32[512,256]{1,0:T(8,128)S(1)}, u32[]{:S(2)}, u32[]{:S(2)}) collective-permute-start(s32[512,256]{1,0:T(8,128)S(1)} %copy-done.8), channel_id=1, source_target_pairs={{0,2},{2,0},{4,6},{6,4},{8,10},{10,8},{12,14},{14,12},{16,18},{18,... | collective-permute-start | bytes 1572872 | tf_op jit(solution)/shard_map/ppermute | solution.py:291
  55.0 46.6 %collective-permute-start.36 = (s32[512,256]{1,0:T(8,128)S(1)}, s32[512,256]{1,0:T(8,128)S(1)}, u32[]{:S(2)}, u32[]{:S(2)}) collective-permute-start(s32[512,256]{1,0:T(8,128)S(1)} %copy-done.8), channel_id=1, source_target_pairs={{0,16},{2,18},{4,20},{6,22},{8,24},{10,26},{12,28},{14,30},{16,0},... | collective-permute-start | bytes 1572872 | tf_op jit(solution)/shard_map/ppermute | solution.py:291
  86.9 43.0 %collective-permute-start.1 = (f32[16,128,128]{2,1,0:T(8,128)S(1)}, f32[16,128,128]{2,1,0:T(8,128)S(1)}, u32[]{:S(2)}, u32[]{:S(2)}) collective-permute-start(f32[16,128,128]{2,1,0:T(8,128)S(1)} %copy-done.25), channel_id=1, source_target_pairs={{0,2},{2,0},{4,6},{6,4},{8,10},{10,8},{12,14},{14,12},{16,18},{18,... | collective-permute-start | bytes 3145736 | tf_op jit(solution)/shard_map/ppermute | solution.py:291
  98.2 32.1 %collective-permute-start.24 = (f32[2,4,128,128]{3,2,1,0:T(8,128)S(1)}, f32[2,4,128,128]{3,2,1,0:T(8,128)S(1)}, u32[]{:S(2)}, u32[]{:S(2)}) collective-permute-start(f32[2,4,128,128]{3,2,1,0:T(8,128)S(1)} %get-tuple-element.47), channel_id=1, source_target_pairs={{4,0},{6,2},{5,1},{7,3},{20,16},{22,18},{21,17},{23,19}} | collective-permute-start | bytes 1572872 | tf_op jit(solution)/shard_map/ppermute | solution.py:299
  100.4 31.0 %collective-permute-start.37 = (s32[512,256]{1,0:T(8,128)S(1)}, s32[512,256]{1,0:T(8,128)S(1)}, u32[]{:S(2)}, u32[]{:S(2)}) collective-permute-start(s32[512,256]{1,0:T(8,128)S(1)} %copy-done.8), channel_id=1, source_target_pairs={{0,18},{2,16},{4,22},{6,20},{8,26},{10,24},{12,30},{14,28},{16,2},... | collective-permute-start | bytes 1572872 | tf_op jit(solution)/shard_map/ppermute | solution.py:291
  101.6 45.1 %collective-permute-start.50 = (f32[256,512]{1,0:T(8,128)S(1)}, f32[256,512]{1,0:T(8,128)S(1)}, u32[]{:S(2)}, u32[]{:S(2)}) collective-permute-start(f32[256,512]{1,0:T(8,128)S(1)} %get-tuple-element.70), channel_id=1, source_target_pairs={{0,2},{2,0},{4,6},{6,4},{8,10},{10,8},{12,14},{14,12},{16,18},{18,... | collective-permute-start | bytes 1572872 | tf_op jit(solution)/shard_map/ppermute | solution.py:291
  102.4 44.8 %collective-permute-start.51 = (f32[256,512]{1,0:T(8,128)S(1)}, f32[256,512]{1,0:T(8,128)S(1)}, u32[]{:S(2)}, u32[]{:S(2)}) collective-permute-start(f32[256,512]{1,0:T(8,128)S(1)} %get-tuple-element.69), channel_id=1, source_target_pairs={{0,16},{2,18},{4,20},{6,22},{8,24},{10,26},{12,28},{14,30},{16,0},... | collective-permute-start | bytes 1572872 | tf_op jit(solution)/shard_map/ppermute | solution.py:291
  130.4 31.7 %collective-permute-start.18 = (f32[2,4,128,128]{3,2,1,0:T(8,128)}, f32[2,4,128,128]{3,2,1,0:T(8,128)S(1)}, u32[]{:S(2)}, u32[]{:S(2)}) collective-permute-start(f32[2,4,128,128]{3,2,1,0:T(8,128)} %get-tuple-element.45), channel_id=1, source_target_pairs={{4,0},{6,2},{5,1},{7,3},{20,16},{22,18},{21,17},{23,19}} | collective-permute-start | bytes 1572872 | tf_op jit(solution)/shard_map/ppermute | solution.py:299
  131.4 33.5 %collective-permute-start.38 = (f32[256,512]{1,0:T(8,128)}, f32[256,512]{1,0:T(8,128)S(1)}, u32[]{:S(2)}, u32[]{:S(2)}) collective-permute-start(f32[256,512]{1,0:T(8,128)} %get-tuple-element.62), channel_id=1, source_target_pairs={{0,2},{2,0},{4,6},{6,4},{8,10},{10,8},{12,14},{14,12},{16,18},{18,... | collective-permute-start | bytes 1572872 | tf_op jit(solution)/shard_map/ppermute | solution.py:291
  148.9 35.2 %collective-permute-start.2 = (f32[16,128,128]{2,1,0:T(8,128)S(1)}, f32[16,128,128]{2,1,0:T(8,128)S(1)}, u32[]{:S(2)}, u32[]{:S(2)}) collective-permute-start(f32[16,128,128]{2,1,0:T(8,128)S(1)} %select_add_fusion), channel_id=1, source_target_pairs={{0,4},{2,6},{1,5},{3,7},{16,20},{18,22},{17,21},{19,23}} | collective-permute-start | bytes 3145736 | tf_op jit(solution)/shard_map/ppermute | solution.py:299
  188.1 22.9 %collective-permute-start.3 = (f32[16,128,128]{2,1,0:T(8,128)S(1)}, f32[16,128,128]{2,1,0:T(8,128)S(1)}, u32[]{:S(2)}, u32[]{:S(2)}) collective-permute-start(f32[16,128,128]{2,1,0:T(8,128)S(1)} %multiply_add_fusion.2), channel_id=1, source_target_pairs={{4,8},{6,10},{5,9},{7,11},{20,24},{22,26},{21,25},{23,27}} | collective-permute-start | bytes 3145736 | tf_op jit(solution)/shard_map/ppermute | solution.py:299
  196.1 42.1 %collective-permute-start.29 = (f32[4,128,128]{2,1,0:T(8,128)S(1)}, f32[4,128,128]{2,1,0:T(8,128)S(1)}, u32[]{:S(2)}, u32[]{:S(2)}) collective-permute-start(f32[4,128,128]{2,1,0:T(8,128)S(1)} %get-tuple-element.98.refs_20_), channel_id=1, source_target_pairs={{0,18},{2,16},{4,22},{6,20},{8,26},{10,24},{12,30},{14,28},{16,2},... | collective-permute-start | bytes 786440 | tf_op jit(solution)/shard_map/ppermute | solution.py:291
  198.4 44.5 %collective-permute-start.30 = (f32[4,128,128]{2,1,0:T(8,128)S(1)}, f32[4,128,128]{2,1,0:T(8,128)S(1)}, u32[]{:S(2)}, u32[]{:S(2)}) collective-permute-start(f32[4,128,128]{2,1,0:T(8,128)S(1)} %get-tuple-element.100.refs_20_), channel_id=1, source_target_pairs={{0,18},{2,16},{4,22},{6,20},{8,26},{10,24},{12,30},{14,28},{16,2},... | collective-permute-start | bytes 786440 | tf_op jit(solution)/shard_map/ppermute | solution.py:291
  205.0 31.8 %collective-permute-start.57 = (f32[4,8,32,128]{3,2,1,0:T(8,128)S(1)}, f32[4,8,32,128]{3,2,1,0:T(8,128)S(1)}, u32[]{:S(2)}, u32[]{:S(2)}) collective-permute-start(f32[4,8,32,128]{3,2,1,0:T(8,128)S(1)} %get-tuple-element.65), channel_id=1, source_target_pairs={{8,4},{10,6},{12,8},{14,10},{9,5},{11,7},{13,9},{15,11},{24,20},{2... | collective-permute-start | bytes 1572872 | tf_op jit(solution)/shard_map/ppermute | solution.py:483
  209.5 42.7 %collective-permute-start.55 = (f32[4,8,32,128]{3,2,1,0:T(8,128)S(1)}, f32[4,8,32,128]{3,2,1,0:T(8,128)S(1)}, u32[]{:S(2)}, u32[]{:S(2)}) collective-permute-start(f32[4,8,32,128]{3,2,1,0:T(8,128)S(1)} %get-tuple-element.64), channel_id=1, source_target_pairs={{0,4},{2,6},{4,8},{6,10},{8,12},{10,14},{1,5},{3,7},{5,9},{7,11},{... | collective-permute-start | bytes 1572872 | tf_op jit(solution)/shard_map/ppermute | solution.py:480
  211.0 36.6 %collective-permute-start.45 = (f32[4,8,32,128]{3,2,1,0:T(8,128)S(1)}, f32[4,8,32,128]{3,2,1,0:T(8,128)S(1)}, u32[]{:S(2)}, u32[]{:S(2)}) collective-permute-start(f32[4,8,32,128]{3,2,1,0:T(8,128)S(1)} %get-tuple-element.57), channel_id=1, source_target_pairs={{8,4},{10,6},{12,8},{14,10},{9,5},{11,7},{13,9},{15,11},{24,20},{2... | collective-permute-start | bytes 1572872 | tf_op jit(solution)/shard_map/ppermute | solution.py:483
  236.8 24.9 %collective-permute-start.4 = (f32[16,128,128]{2,1,0:T(8,128)S(1)}, f32[16,128,128]{2,1,0:T(8,128)S(1)}, u32[]{:S(2)}, u32[]{:S(2)}) collective-permute-start(f32[16,128,128]{2,1,0:T(8,128)S(1)} %get-tuple-element.51), channel_id=1, source_target_pairs={{8,12},{10,14},{9,13},{11,15},{24,28},{26,30},{25,29},{27,31}} | collective-permute-start | bytes 3145736 | tf_op jit(solution)/shard_map/ppermute | solution.py:299
  244.5 22.8 %collective-permute-start.43 = (f32[4,8,32,128]{3,2,1,0:T(8,128)S(1)}, f32[4,8,32,128]{3,2,1,0:T(8,128)S(1)}, u32[]{:S(2)}, u32[]{:S(2)}) collective-permute-start(f32[4,8,32,128]{3,2,1,0:T(8,128)S(1)} %get-tuple-element.56), channel_id=1, source_target_pairs={{0,4},{2,6},{4,8},{6,10},{8,12},{10,14},{1,5},{3,7},{5,9},{7,11},{... | collective-permute-start | bytes 1572872 | tf_op jit(solution)/shard_map/ppermute | solution.py:480
  267.3 30.2 %collective-permute-start.5 = (f32[16,128,128]{2,1,0:T(8,128)S(1)}, f32[16,128,128]{2,1,0:T(8,128)S(1)}, u32[]{:S(2)}, u32[]{:S(2)}) collective-permute-start(f32[16,128,128]{2,1,0:T(8,128)S(1)} %fusion), channel_id=1, source_target_pairs={{0,2},{2,0},{4,6},{6,4},{8,10},{10,8},{12,14},{14,12},{16,18},{18,... | collective-permute-start | bytes 3145736 | tf_op jit(solution)/shard_map/ppermute | solution.py:291
  269.1 26.7 %collective-permute-start.47 = (f32[2,8,32,128]{3,2,1,0:T(8,128)S(1)}, f32[2,8,32,128]{3,2,1,0:T(8,128)S(1)}, u32[]{:S(2)}, u32[]{:S(2)}) collective-permute-start(f32[2,8,32,128]{3,2,1,0:T(8,128)S(1)} %get-tuple-element.95), channel_id=1, source_target_pairs={{0,2},{2,0},{4,6},{6,4},{8,10},{10,8},{12,14},{14,12},{16,18},{18,... | collective-permute-start | bytes 786440 | tf_op jit(solution)/shard_map/ppermute | solution.py:291
  269.7 26.1 %collective-permute-start.49 = (f32[2,8,32,128]{3,2,1,0:T(8,128)S(1)}, f32[2,8,32,128]{3,2,1,0:T(8,128)S(1)}, u32[]{:S(2)}, u32[]{:S(2)}) collective-permute-start(f32[2,8,32,128]{3,2,1,0:T(8,128)S(1)} %get-tuple-element.95), channel_id=1, source_target_pairs={{0,18},{2,16},{4,22},{6,20},{8,26},{10,24},{12,30},{14,28},{16,2},... | collective-permute-start | bytes 786440 | tf_op jit(solution)/shard_map/ppermute | solution.py:291
  272.1 23.7 %collective-permute-start.48 = (f32[2,8,32,128]{3,2,1,0:T(8,128)S(1)}, f32[2,8,32,128]{3,2,1,0:T(8,128)S(1)}, u32[]{:S(2)}, u32[]{:S(2)}) collective-permute-start(f32[2,8,32,128]{3,2,1,0:T(8,128)S(1)} %get-tuple-element.94), channel_id=1, source_target_pairs={{0,16},{2,18},{4,20},{6,22},{8,24},{10,26},{12,28},{14,30},{16,0},... | collective-permute-start | bytes 786440 | tf_op jit(solution)/shard_map/ppermute | solution.py:291
  (75 other events, 1146.0 us)

commit v3 on v2

v3 whole, which is shorter than its diff:
```python
import jax
import jax.numpy as jnp
from jax import lax
from jax.experimental import pallas as pl
from jax.experimental.pallas import tpu as pltpu
from jax.sharding import PartitionSpec as P

HEAD = 128
WORDS = HEAD // 16
BLK = 64
HALF = BLK // 2
SEL = 16
QUAD = 4
CHUNKS = 2

F32 = jnp.float32
BF16 = jnp.bfloat16
VMEM_LIMIT = 62 * 1024 * 1024


def params():
    return pltpu.CompilerParams(vmem_limit_bytes=VMEM_LIMIT)


def cost(flops, nbytes):
    return pl.CostEstimate(flops=int(flops), bytes_accessed=int(nbytes), transcendentals=0)


def nn(a, b):
    return lax.dot_general(a, b, (((1,), (0,)), ((), ())), preferred_element_type=F32)


def nt(a, b):
    return lax.dot_general(a, b, (((1,), (1,)), ((), ())), preferred_element_type=F32)


def tn(a, b):
    return lax.dot_general(a, b, (((0,), (0,)), ((), ())), preferred_element_type=F32)


def split(a):
    high = a.astype(BF16)
    return high, (a - high.astype(F32)).astype(BF16)


def fold(a):
    return a[:, :HEAD] + a[:, HEAD:]


def unpack(words):
    tokens = words.shape[1]
    spread = jnp.broadcast_to(words[:, None, :], (WORDS, 16, tokens))
    shifts = lax.broadcasted_iota(jnp.int32, (WORDS, 16, tokens), 1)
    bits = jnp.bitwise_and(jnp.right_shift(spread, shifts), 1)
    return bits.reshape(HEAD, tokens).astype(F32)


def causal(shape, token_axis):
    return lax.broadcasted_iota(jnp.int32, shape, token_axis) >= lax.broadcasted_iota(
        jnp.int32, shape, 1 - token_axis
    )


def lanes(i):
    return slice(i * HEAD, (i + 1) * HEAD)


def rows_of(vector):
    high, low = split(vector)
    low2 = (vector - high.astype(F32) - low.astype(F32)).astype(BF16)
    n = vector.shape[1]
    return jnp.concatenate([high, low, low2, jnp.zeros((13, n), BF16)], axis=0)


def key_sums_kernel(heads, kw, cum, out):
    for i in range(heads):
        row = cum[0, i : i + 1, :]
        tail = jnp.exp(row[:, -1:] - row)
        k = unpack(kw[i * WORDS : (i + 1) * WORDS, :]).astype(BF16)
        out[0, i : i + 1, :] = jnp.sum(nt(rows_of(tail), k), axis=0, keepdims=True)


def state_kernel(heads, kw, v, cum, y_out, kt_out):
    for i in range(heads):
        row = cum[0, i : i + 1, :]
        k = unpack(kw[i * WORDS : (i + 1) * WORDS, :])
        kt_out[:, lanes(i)] = jnp.transpose(k).astype(BF16)
        high, low = split(k * jnp.exp(row[:, -1:] - row))
        value = v[:, lanes(i)]
        y_out[i] = nn(high, value) + nn(low, value)


def weight_kernel(heads, qw, kt, cum, wt_out, den_out, qt_out):
    tokens = kt.shape[0]
    cols = jnp.transpose(cum[0])
    after = causal((tokens, tokens), 1)
    for i in range(heads):
        row = cum[0, i : i + 1, :]
        col = cols[:, i : i + 1]
        q = unpack(qw[i * WORDS : (i + 1) * WORDS, :])
        qt_out[:, lanes(i)] = jnp.transpose(q).astype(BF16)
        decay = jnp.where(after, jnp.exp(jnp.minimum(row - col, 0.0)), 0.0)
        w = nn(kt[:, lanes(i)], q.astype(BF16)) * decay
        wt_out[i] = w.astype(BF16)
        den_out[0, i : i + 1, :] = jnp.sum(w, axis=0, keepdims=True)


def start_kernel(z, received, up, order, down_out, send_out):
    second = received[1, :, :HEAD, :]
    down = received[0, :, :HEAD, :] + received[0, :, HEAD : HEAD + 1, :] * second
    down_out[0] = down
    send_out[0] = jnp.where(z[0] == 0, up[0], down)


def local_kernel(heads, wt, v, out):
    for i in range(heads):
        out[:, lanes(i)] = tn(wt[i], v[:, lanes(i)])


def adjoint_kernel(start, heads, qw, do, cum, den_local, z0, wt, *refs):
    den_out, x_out, dv_out = refs[-3:]
    tokens = do.shape[0]
    rows = []
    qs = []
    for i in range(heads):
        at = start + i
        row = cum[0, at : at + 1, :]
        q = unpack(qw[i * WORDS : (i + 1) * WORDS, :]).astype(BF16)
        qs.append(q)
        carried = jnp.sum(nn(rows_of(z0[0, at : at + 1, :]), q), axis=0, keepdims=True)
        rows.append(1.0 + den_local[0, at : at + 1, :] + jnp.exp(row) * carried)
    rows = rows + [jnp.ones((1, tokens), F32)] * (8 - heads)
    den = jnp.concatenate(rows, axis=0)
    den_out[0] = den
    inverse = jnp.transpose(1.0 / den)
    leads = jnp.exp(jnp.transpose(cum[0]))
    for i in range(heads):
        g = do[:, lanes(i)].astype(F32) * inverse[:, i : i + 1]
        lead = leads[:, start + i : start + i + 1]
        x_out[0, i, :HEAD, :] = fold(nn(qs[i], jnp.concatenate(split(g * lead), axis=1)))
        x_out[0, i, HEAD:, :] = jnp.broadcast_to(lead[-1:, :], (8, HEAD))
        dv_out[0, 0, :, lanes(i)] = nn(wt[i], g.astype(BF16))


def output_kernel(chunk, heads, y, keep, got, local, qt, do, cum, *refs):
    dens, (h_out, xv_out) = refs[:-3], refs[-2:]
    cols = jnp.transpose(cum[0])
    inverses = [jnp.transpose(1.0 / den[0]) for den in dens]
    kept = pl.program_id(0) // 2 == y[0]
    for i in range(heads):
        col = cols[:, i : i + 1]
        inverse = inverses[i // chunk][:, i % chunk : i % chunk + 1]
        lead = jnp.exp(col)
        q = qt[:, lanes(i)]
        grad = do[:, lanes(i)].astype(F32)
        state = jnp.where(kept, keep[i], got[i])
        carried = fold(nn(q, jnp.concatenate(split(state), axis=1)))
        o = (local[:, lanes(i)] + lead * carried) * inverse
        h = -jnp.sum(grad * o, axis=1, keepdims=True) * inverse
        h_out[0, :, i : i + 1] = h
        xv_out[0, i : i + 1, :] = jnp.sum(q.astype(F32) * (lead * h), axis=0, keepdims=True)


def token_kernel(chunk, heads, y, quad, keep, got, z0, qt, kt, v, do, cum, slope, h_in, *refs):
    dens, adjoints, (dq_out, dk_out) = refs[:CHUNKS], refs[CHUNKS:-2], refs[-2:]
    offset = pl.program_id(0) ^ quad[0]
    tokens = v.shape[0]
    cols = jnp.transpose(cum[0])
    inverses = [jnp.transpose(1.0 / den[0]) for den in dens]
    before = causal((tokens, tokens), 0)
    kept = pl.program_id(0) // 2 == y[0]
    for i in range(heads):
        row = cum[0, i : i + 1, :]
        col = cols[:, i : i + 1]
        inverse = inverses[i // chunk][:, i % chunk : i % chunk + 1]
        lead = jnp.exp(col)
        tail = jnp.exp(col[-1:, :] - col)
        value = v[:, lanes(i)]
        decay = jnp.where(before, jnp.exp(jnp.minimum(col - row, 0.0)), 0.0)
        h = h_in[0, :, i : i + 1]
        g = (do[:, lanes(i)].astype(F32) * inverse).astype(BF16)
        r = ((nt(g, value) + h) * decay).astype(BF16)
        state = jnp.where(kept, keep[i], got[i])
        back = fold(nt(g, jnp.concatenate(split(state), axis=0))) + h * z0[0, i : i + 1, :]
        dq = nn(r, kt[:, lanes(i)]) + lead * back
        dq_out[:, lanes(i)] = (slope[:, lanes(i)].astype(F32) * dq).astype(BF16)
        adjoint = adjoints[QUAD * (i // chunk)][i % chunk]
        for at in range(1, QUAD):
            adjoint = jnp.where(offset == at, adjoints[QUAD * (i // chunk) + at][i % chunk], adjoint)
        carried = fold(nt(value, jnp.concatenate(split(adjoint), axis=0)))
        dk_out[:, lanes(i)] = tn(r, qt[:, lanes(i)]) + tail * carried


def key_kernel(heads, dk, cv, cum, slope, out):
    cols = jnp.transpose(cum[0])
    for i in range(heads):
        col = cols[:, i : i + 1]
        tail = jnp.exp(col[-1:, :] - col)
        total = dk[:, lanes(i)] + tail * cv[0, i : i + 1, :]
        out[:, lanes(i)] = (slope[:, lanes(i)].astype(F32) * total).astype(BF16)


def block_kernel(start, quad, core, pattern, *refs):
    keep_out, send_out, *adjoint_outs = refs[-6 - QUAD : -4]
    flags, lines, others, found = refs[-4:]
    pieces, (grads, parts, reach), other_pieces = refs[:QUAD], refs[QUAD : QUAD + 3], refs[QUAD + 3 : -7 - QUAD]
    tokens = grads.shape[2]
    key_rows = others.shape[1] - 8
    ncore = 1 + len(other_pieces)
    spike_rows = lines.shape[1] // ncore
    step = pl.program_id(0)
    shifts = 2 * lax.broadcasted_iota(jnp.int32, (8, tokens), 0)
    low = lax.broadcasted_iota(jnp.int32, (tokens, HEAD), 1) < BLK

    @pl.when(step == 0)
    def _():
        for i in range(QUAD):
            source = quad[0] ^ i
            others[source] = pieces[i][spike_rows:, :]
            for k in range(ncore):
                part = other_pieces[k - 1][i] if k else pieces[i][:spike_rows, :]
                rows = pl.multiple_of(lax.rem(core[0] + ncore - k, ncore) * spike_rows, spike_rows)
                lines[source, pl.ds(rows, spike_rows), :] = part.astype(jnp.int32)

    values = []
    for source in range(QUAD):
        if source % 2:
            adjoint = reach[source // 2, 0]
        else:
            adjoint = parts[source + 1, 0, :HEAD, :] + parts[source + 1, 0, HEAD : HEAD + 1, :] * reach[source // 2, 0]
        found[source] = adjoint
        row = others[source, pl.ds(key_rows + start + step, 1), :]
        words = others[source, pl.ds(pl.multiple_of((start + step) * WORDS, WORDS), WORDS), :]
        k = unpack(words.astype(jnp.int32)) * jnp.exp(row[:, -1:] - row)
        carried = fold(tn(k.astype(BF16), jnp.concatenate(split(adjoint), axis=1)))
        values.append((grads[source, 0] + carried).astype(BF16).astype(F32))
    for i in range(QUAD):
        adjoint_outs[i][0] = found[quad[0] ^ i]
    for side in range(2):
        total = None
        for source in range(QUAD):
            grad = values[source]
            turned = jnp.concatenate([grad[:, BLK:], grad[:, :BLK]], axis=1)
            even, odd = (grad, turned) if side == 0 else (turned, grad)
            right = jnp.concatenate(
                [jnp.where(low, even, 0.0).astype(BF16), jnp.where(low, 0.0, odd).astype(BF16)], axis=0
            )
            for s in range(SEL):
                first = pattern[2 * (start + step) + side, s] * (BLK // 16)
                for parity in range(2):
                    flag_parts = []
                    for word in range(BLK // 16):
                        line = lines[source, pl.ds(first + word, 1), :]
                        spread = jnp.broadcast_to(line, (8, tokens))
                        flag_parts.append(jnp.bitwise_and(jnp.right_shift(spread, shifts + parity), 1))
                    bits = jnp.concatenate(flag_parts, axis=0).astype(F32).astype(BF16)
                    flags[s * HALF : (s + 1) * HALF, parity * tokens : (parity + 1) * tokens] = bits
            part = nn(flags[...], right)
            total = part if total is None else total + part
        total = total.reshape(SEL, HALF, HEAD)
        keep_out[:, side] = total[: SEL // 2]
        send_out[:, side] = total[SEL // 2 :]


def finish_kernel(quad, *refs):
    parts, out = refs[:-1], refs[-1]
    rows = parts[0].shape[1]

    def place(source, offset):
        @pl.when(quad[0] ^ offset == source)
        def _():
            for n in range(CHUNKS):
                first = (source * CHUNKS + n) * rows
                for i in range(HALF):
                    out[0, first : first + rows, lanes(i)] = parts[n * QUAD + offset][0, :, i, :]

    for source in range(QUAD):
        for offset in range(QUAD):
            place(source, offset)


def per_device(
    input_spikes,
    query_spikes,
    key_spikes,
    values,
    query_slope,
    key_slope,
    grad_out,
    log_gate,
    pattern,
):
    tokens, width = values.shape
    heads_here = width // HEAD
    heads = heads_here // QUAD
    chunk = heads // CHUNKS
    nctx, ndp = lax.axis_size("ctx"), lax.axis_size("dp")
    nz = nctx // 2
    x, place = lax.axis_index("dp"), lax.axis_index("ctx")
    y, z = place % 2, place // 2
    quad = (2 * x + y).astype(jnp.int32).reshape(1)
    planes = [[d * nctx + 2 * c + i for d in range(ndp) for i in range(2)] for c in range(nz)]

    gate_sums = jnp.cumsum(log_gate, axis=1)
    totals = jnp.exp(gate_sums[:, -1])
    cum = gate_sums.reshape(QUAD, heads, tokens)
    cum = jnp.pad(cum, ((0, 0), (0, 8 - heads), (0, 0)))

    def spec(block, index):
        return pl.BlockSpec(block, lambda j, *refs: index(j))

    word_spec = spec((heads * WORDS, tokens), lambda j: (j, 0))
    flat_spec = spec((tokens, heads * HEAD), lambda j: (0, j))
    cum_spec = spec((1, 8, tokens), lambda j: (j, 0, 0))
    vec_spec = spec((1, 8, HEAD), lambda j: (j, 0, 0))
    state_spec = spec((heads, HEAD, HEAD), lambda j: (j, 0, 0))
    wt_spec = spec((heads, tokens, tokens), lambda j: (j, 0, 0))
    col_spec = spec((1, tokens, 8), lambda j: (j, 0, 0))

    def shape(*dims, kind=F32):
        return jax.ShapeDtypeStruct(dims, kind)

    flat16 = shape(tokens, width, kind=BF16)
    flat32 = shape(tokens, width)
    states = shape(heads_here, HEAD, HEAD)
    vecs = shape(QUAD, 8, HEAD)
    cums = shape(QUAD, 8, tokens)
    unit = 2 * tokens * tokens * HEAD * heads_here
    mib = 1 << 20

    def call(name, kernel, in_specs, out_specs, out_shape, estimate, *args, scalars=0, aliases={}):
        def body(*refs):
            kernel(*refs)

        body.__name__ = name
        return pl.pallas_call(
            body,
            grid_spec=pltpu.PrefetchScalarGridSpec(
                num_scalar_prefetch=scalars, grid=(QUAD,), in_specs=in_specs, out_specs=out_specs
            ),
            out_shape=out_shape,
            input_output_aliases=aliases,
            compiler_params=params(),
            cost_estimate=estimate,
            name=name,
        )(*args)

    def swap(value):
        return lax.ppermute(value, "ctx", [(c, c ^ 1) for c in range(nctx)])

    def across(value, offset):
        pairs = [
            (d * nctx + c, (d ^ (offset // 2)) * nctx + (c ^ (offset % 2)))
            for d in range(ndp)
            for c in range(nctx)
        ]
        return lax.ppermute(value, ("dp", "ctx"), pairs)

    def plane(value):
        return lax.all_to_all(value, ("dp", "ctx"), 0, 0, axis_index_groups=planes, tiled=True)

    def vec(a):
        return jnp.pad(a.reshape(QUAD, heads, HEAD), ((0, 0), (0, 8 - heads), (0, 0)))

    def unvec(a):
        return a[:, :heads].reshape(heads_here, HEAD)

    def ordered(own, got):
        return jnp.where(y == 0, own, got), jnp.where(y == 0, got, own)

    def carried_vectors(vector, forward):
        message = jnp.concatenate([vector, jnp.broadcast_to(totals[:, None], vector.shape)], axis=0)
        message = jnp.broadcast_to(message[None], (nctx,) + message.shape)
        parts = lax.all_to_all(message, "ctx", 0, 0, tiled=True)
        reach = jnp.zeros_like(vector)
        for at in range(nctx) if forward else range(nctx - 1, -1, -1):
            inside = at < place if forward else at > place
            reach = jnp.where(inside, parts[at, heads_here:] * reach + parts[at, :heads_here], reach)
        return reach, parts[:, heads_here:, 0]

    key_sum = call(
        "key_sums_kernel",
        lambda *refs: key_sums_kernel(heads, *refs),
        [word_spec, cum_spec],
        vec_spec,
        vecs,
        cost(1, 1),
        key_spikes,
        cum,
    )
    z0, decays = carried_vectors(unvec(key_sum), True)
    z0 = vec(z0)
    first_total = lax.dynamic_index_in_dim(decays, 2 * z, 0, keepdims=False)
    second_total = lax.dynamic_index_in_dim(decays, 2 * z + 1, 0, keepdims=False)

    ncore, core = lax.axis_size("tensor"), lax.axis_index("tensor")
    spike_rows = input_spikes.shape[0] // ncore
    spike_words = lax.dynamic_slice_in_dim(input_spikes, core * spike_rows, spike_rows, 0).astype(F32)
    spike_words = jnp.broadcast_to(spike_words[None], (QUAD,) + spike_words.shape)
    key_words = key_spikes.reshape(QUAD, heads * WORDS, tokens).astype(F32)
    key_words = jnp.concatenate([spike_words, key_words, cum], axis=1)
    pieces = []
    for i in range(QUAD):
        part = lax.dynamic_index_in_dim(key_words, quad[0] ^ i, 0, keepdims=False)
        pieces.append(across(part, i) if i else part)
    other_pieces = jnp.stack([piece[:spike_rows] for piece in pieces])
    other_pieces = [
        lax.ppermute(other_pieces, "tensor", [(c, (c + k) % ncore) for c in range(ncore)])
        for k in range(1, ncore)
    ]

    state_sum, kt = call(
        "state_kernel",
        lambda *refs: state_kernel(heads, *refs),
        [word_spec, flat_spec, cum_spec],
        [state_spec, flat_spec],
        [states, flat16],
        cost(1, 1),
        key_spikes,
        values,
        cum,
    )
    wt, den_local, qt = call(
        "weight_kernel",
        lambda *refs: weight_kernel(heads, *refs),
        [word_spec, flat_spec, cum_spec],
        [wt_spec, cum_spec, flat_spec],
        [shape(heads_here, tokens, tokens, kind=BF16), cums, flat16],
        cost(1, 1),
        query_spikes,
        kt,
        cum,
    )
    dens, adjoint_sums, value_parts = [], [], None
    anywhere = pl.BlockSpec(memory_space=pl.ANY)
    for n in range(CHUNKS):
        extra = pieces if n == 0 else [value_parts]
        den, adjoint_sum, value_parts = call(
            "adjoint_kernel",
            lambda *refs, n=n: adjoint_kernel(n * chunk, chunk, *refs),
            [
                spec((chunk * WORDS, tokens), lambda j, n=n: (j * CHUNKS + n, 0)),
                spec((tokens, chunk * HEAD), lambda j, n=n: (0, j * CHUNKS + n)),
                cum_spec,
                cum_spec,
                vec_spec,
                spec((chunk, tokens, tokens), lambda j, n=n: (j * CHUNKS + n, 0, 0)),
            ]
            + [anywhere] * len(extra),
            [
                cum_spec,
                spec((1, chunk, HEAD + 8, HEAD), lambda j: (j, 0, 0, 0)),
                spec((1, 1, tokens, chunk * HEAD), lambda j, n=n: (j, n, 0, 0)),
            ],
            [cums, shape(QUAD, chunk, HEAD + 8, HEAD), shape(QUAD, CHUNKS, tokens, chunk * HEAD)],
            cost(1, 1),
            query_spikes,
            grad_out,
            cum,
            den_local,
            z0,
            wt,
            *extra,
            aliases={6: 2} if n else {},
        )
        dens.append(den)
        adjoint_sums.append(adjoint_sum)

    local = call(
        "local_kernel",
        lambda wt, v, *refs: local_kernel(heads, wt, v, refs[-1]),
        [wt_spec, flat_spec] + [anywhere] * len([adjoint_sums[-1], *other_pieces]),
        flat_spec,
        flat32,
        cost(1, 1),
        wt,
        values,
        adjoint_sums[-1],
        *other_pieces,
    )

    half = heads_here // 2
    mine, other = y * half, (1 - y) * half

    def cut(value, start):
        return lax.dynamic_slice_in_dim(value, start, half, 0)

    first, second = ordered(cut(state_sum, mine), swap(cut(state_sum, other)))
    first_decay = cut(first_total, mine)[:, None, None]
    second_decay = cut(second_total, mine)[:, None, None]
    state_both = second_decay * first + second
    state_decay = second_decay * first_decay
    part_size = half // CHUNKS

    reaches, adjoint_parts = [], []
    for n in range(CHUNKS):
        received = plane(adjoint_sums[n])
        parts = received.reshape(2, 2, chunk, HEAD + 8, HEAD)
        gates = parts[:, :, :, HEAD : HEAD + 1, :1]
        down_decay = gates[:, 0] * gates[:, 1]
        size = (2, chunk, HEAD, HEAD)
        up = state_both[n * part_size : (n + 1) * part_size].reshape(size)
        size_spec = spec((1,) + size[1:], lambda j: (j, 0, 0, 0))
        down, send = pl.pallas_call(
            start_kernel,
            grid_spec=pltpu.PrefetchScalarGridSpec(
                num_scalar_prefetch=1,
                grid=(2,),
                in_specs=[
                    spec((2, chunk, HEAD + 8, HEAD), lambda j: (j, 0, 0, 0)),
                    size_spec,
                    anywhere,
                ],
                out_specs=[size_spec, size_spec],
            ),
            out_shape=[shape(*size), shape(*size)],
            compiler_params=params(),
            cost_estimate=cost(1, 1),
            name="start_kernel",
        )(z.astype(jnp.int32).reshape(1), received, up, local)
        up_decay = state_decay[n * part_size : (n + 1) * part_size].reshape(down_decay.shape)
        reach = None
        for hop in range(nz - 1):
            if reach is not None:
                send = jnp.where(z == hop, up, down) + jnp.where(z == hop, up_decay, down_decay) * reach
            pairs = []
            for c in range(nctx):
                if c // 2 == hop:
                    pairs.append((c, c + 2))
                elif c // 2 == nz - 1 - hop:
                    pairs.append((c, c - 2))
            got = lax.ppermute(send, "ctx", pairs)
            if reach is None:
                reach = got
                reach_up = jnp.where(z == hop + 1, got, 0.0)
                reach_down = jnp.where(z == nz - 2 - hop, got, 0.0)
            else:
                reach = got
                reach_up = jnp.where(z == hop + 1, got, reach_up)
                reach_down = jnp.where(z == nz - 2 - hop, got, reach_down)
        reaches.append(reach_up.reshape(part_size, HEAD, HEAD))
        adjoint_parts.append((received, reach_down))
    reach = jnp.concatenate(reaches, axis=0)
    keep, send = ordered(reach, first_decay * reach + first)
    state = [y.astype(jnp.int32).reshape(1), keep, swap(send)]

    columns = pattern.shape[0] // QUAD
    share = SEL // nz
    own_pattern = lax.dynamic_slice_in_dim(pattern, quad[0] * columns, columns, 0)
    order = jnp.arange(nz, dtype=jnp.int32)
    turned = sum((order // (nz >> (bit + 1))) % 2 << bit for bit in range(nz.bit_length() - 1))
    order = ((z ^ turned)[:, None] * share + jnp.arange(share, dtype=jnp.int32)[None, :]).reshape(SEL)
    own_pattern = jnp.take(own_pattern, order, axis=1)
    columns = columns // CHUNKS
    value_parts = plane(value_parts)
    results, adjoints = [], []
    for n in range(CHUNKS):
        half_spec = spec((SEL // 2, 2, HALF, HEAD), lambda j: (0, j, 0, 0))
        half_shape = shape(SEL // 2, columns, HALF, HEAD)
        after = adjoints[-1][0] if adjoints else adjoint_parts[n][1]
        summed, send, *adjoint = pl.pallas_call(
            lambda *refs, n=n: block_kernel(n * chunk, *refs),
            grid_spec=pltpu.PrefetchScalarGridSpec(
                num_scalar_prefetch=3,
                grid=(chunk,),
                in_specs=[spec(piece.shape, lambda j: (0, 0)) for piece in pieces]
                + [
                    spec((QUAD, 1, tokens, HEAD), lambda j, n=n: (0, n, 0, j)),
                    spec((QUAD, 1, HEAD + 8, HEAD), lambda j: (0, j, 0, 0)),
                    spec((2, 1, HEAD, HEAD), lambda j: (0, j, 0, 0)),
                ]
                + [spec(piece.shape, lambda j: (0, 0, 0)) for piece in other_pieces]
                + [anywhere],
                out_specs=[half_spec, half_spec] + [spec((1, HEAD, HEAD), lambda j: (j, 0, 0))] * QUAD,
                scratch_shapes=[
                    pltpu.VMEM((SEL * HALF, 2 * tokens), BF16),
                    pltpu.VMEM((QUAD, input_spikes.shape[0], tokens), jnp.int32),
                    pltpu.VMEM((QUAD, pieces[0].shape[0] - spike_rows, tokens), F32),
                    pltpu.VMEM((QUAD, HEAD, HEAD), F32),
                ],
            ),
            out_shape=[half_shape, half_shape] + [shape(chunk, HEAD, HEAD)] * QUAD,
            compiler_params=params(),
            cost_estimate=cost(1, 40 * mib),
            name="block_kernel",
        )(
            quad,
            core.astype(jnp.int32).reshape(1),
            own_pattern,
            *pieces,
            value_parts,
            *adjoint_parts[n],
            *other_pieces,
            after,
        )
        adjoints.append(adjoint)

        bit = 1
        while True:
            summed = summed + lax.ppermute(send, "ctx", [(c, c ^ (2 * bit)) for c in range(nctx)])
            bit *= 2
            if bit == nz:
                break
            rest = summed.shape[0] // 2
            summed, send = summed[:rest], summed[rest:]
        for i in range(QUAD):
            part = lax.dynamic_slice_in_dim(summed, (y ^ (i % 2)) * (share // 2), share // 2, 0)
            results.append(across(part, i) if i else part)
    part_spec = spec((1, columns, HALF, HEAD), lambda j: (j, 0, 0, 0))
    value_grad = pl.pallas_call(
        finish_kernel,
        grid_spec=pltpu.PrefetchScalarGridSpec(
            num_scalar_prefetch=1,
            grid=(share // 2,),
            in_specs=[part_spec] * (CHUNKS * QUAD),
            out_specs=spec((1, pattern.shape[0], BLK * BLK), lambda j: (j, 0, 0)),
        ),
        out_shape=shape(share // 2, pattern.shape[0], BLK * BLK),
        compiler_params=params(),
        cost_estimate=cost(1, 4 * mib),
        name="finish_kernel",
    )(quad, *results)

    part_spec = spec((heads, HEAD, HEAD), lambda j: (j % 2, 0, 0))
    h, xv = call(
        "output_kernel",
        lambda *refs: output_kernel(chunk, heads, *refs),
        [part_spec] * 2 + [flat_spec] * 3 + [cum_spec] * (1 + CHUNKS) + [anywhere],
        [col_spec, vec_spec],
        [shape(QUAD, tokens, 8), vecs],
        cost(1, 40 * mib),
        *state,
        local,
        qt,
        grad_out,
        cum,
        *dens,
        adjoints[-1][0],
        scalars=1,
    )
    cv = vec(carried_vectors(unvec(xv), False)[0])
    returned = [across(adjoint[i], i) if i else adjoint[i] for adjoint in adjoints for i in range(QUAD)]
    dq, dk = call(
        "token_kernel",
        lambda *refs: token_kernel(chunk, heads, *refs),
        [part_spec, part_spec, vec_spec]
        + [flat_spec] * 4
        + [cum_spec, flat_spec, col_spec]
        + [cum_spec] * CHUNKS
        + [spec((chunk, HEAD, HEAD), lambda j: (0, 0, 0))] * (CHUNKS * QUAD),
        [flat_spec, flat_spec],
        [flat16, flat32],
        cost(1, 60 * mib),
        state[0],
        quad,
        *state[1:],
        z0,
        qt,
        kt,
        values,
        grad_out,
        cum,
        query_slope,
        h,
        *dens,
        *returned,
        scalars=2,
    )
    key_grad = call(
        "key_kernel",
        lambda *refs: key_kernel(heads, *refs),
        [flat_spec, vec_spec, cum_spec, flat_spec],
        flat_spec,
        flat16,
        cost(1, 8 * mib),
        dk,
        cv,
        cum,
        key_slope,
    )
    return (dq, key_grad, value_grad)


def solution(mesh):
    in_specs = (
        P(None, ("dp", "ctx")),
        P("tensor", ("dp", "ctx")),
        P("tensor", ("dp", "ctx")),
        P(("dp", "ctx"), "tensor"),
        P(("dp", "ctx"), "tensor"),
        P(("dp", "ctx"), "tensor"),
        P(("dp", "ctx"), "tensor"),
        P("tensor", ("dp", "ctx")),
        P("tensor", None),
    )
    out_specs = (P(("dp", "ctx"), "tensor"), P(("dp", "ctx"), "tensor"), P("ctx", "tensor", None))
    return jax.shard_map(
        per_device, mesh=mesh, in_specs=in_specs, out_specs=out_specs, check_vma=False
    )
```

time: 355 us -> 304 us (0.86)
  starting transfers between devices: 106 us -> 65.2 us
  waiting for transfers between devices: 121 us -> 86 us
  Pallas kernels: 77.7 us -> 103 us
  local copies, waits for them, and re-layouts: 27.3 us -> 19.1 us
  other arithmetic: 19.5 us -> 25.2 us
    ppermute x62 -> x28, starting transfers between devices: 106 us -> 39.7 us  [the longest x15 22.5 us: across(): return lax.ppermute(value, ('dp', 'ctx'), pairs)]
    ppermute x62 -> x28, waiting for transfers between devices: 121 us -> 63.5 us  [the longest x6 32.7 us: per_device(): got = lax.ppermute(send, 'ctx', pairs)]
    all_to_all x0 -> x5, starting transfers between devices: none -> 25.5 us  [the longest x2 13 us: carried_vectors(): parts = lax.all_to_all(message, 'ctx', 0, 0, tiled=True)]
    all_to_all x0 -> x5, waiting for transfers between devices: none -> 22.5 us  [the longest x3 22.5 us: plane(): lax.all_to_all(value, ('dp', 'ctx'), 0, 0, axis_index_groups=planes, tile...]
    pallas_call x7 -> x12, Pallas kernels: 57.2 us -> 78.1 us  [the longest x9 69.9 us: call(): pl.pallas_call(body, grid_spec=pltpu.PrefetchScalarGridSpec(num_scalar_pr...]
    unnamed x75 -> x46, local copies, waits for them, and re-layouts: 13.1 us -> 3.9 us
    add x19 -> x10, other arithmetic: 4.34 us -> 12.6 us  [the longest x4 5.97 us: per_device(): jnp.where(z == hop, up, down)]
    another operation x21 -> x5, other arithmetic: 8.46 us -> 1.81 us  [the longest x1 1.04 us: per_device(): other_pieces = jnp.stack([piece[:spike_rows] for piece in pieces])]
  transfers between devices with their start and end apart: 62 -> 33, of which waited for: 20 -> 9; matrix products, arithmetic and copies ran while one was open for 9% -> 12% of each run, Pallas kernels for 15% -> 28%
where the time goes in v3:
time: 304 us; the launch traced here: 299 us
  Pallas kernels  103 us (34%)
  waiting for transfers between devices  86 us (28%)
  starting transfers between devices  65.2 us (21%)
  other arithmetic  25.2 us (8%)
  local copies, waits for them, and re-layouts  19.1 us (6%)
    pallas_call x9, Pallas kernels, call(): pl.pallas_call(body, grid_spec=pltpu.PrefetchScalarGridSpec(num_scalar_pr...  69.9 us
    ppermute x6, waiting for transfers between devices, per_device(): got = lax.ppermute(send, 'ctx', pairs)  32.7 us
    ppermute x4, waiting for transfers between devices, per_device(): lax.ppermute(send, 'ctx', [(c, c ^ 2 * bit) for c in range(nctx)])  30.8 us
    pallas_call x2, Pallas kernels, per_device(): pl.pallas_call(lambda *refs, n=n: block_kernel(n * chunk, *refs), grid_sp...  24.6 us
    all_to_all x3, waiting for transfers between devices, plane(): lax.all_to_all(value, ('dp', 'ctx'), 0, 0, axis_index_groups=planes, tile...  22.5 us
    ppermute x15, starting transfers between devices, across(): return lax.ppermute(value, ('dp', 'ctx'), pairs)  22.5 us
    all_to_all x2, starting transfers between devices, carried_vectors(): parts = lax.all_to_all(message, 'ctx', 0, 0, tiled=True)  13 us
    all_to_all x3, starting transfers between devices, plane(): lax.all_to_all(value, ('dp', 'ctx'), 0, 0, axis_index_groups=planes, tile...  12.5 us
  transfers between devices with their start and end apart: 33, of which 9 were waited for; matrix products, arithmetic and copies ran while one was open for 12% of the time, Pallas kernels for 28%

profile of v3, /device:TPU:24, one launch (start us, length us, event | category | flops | bytes accessed | tf_op | source)
XLA Modules:
  0.0 299.5 jit_solution(11859649164317027798)
XLA Ops:
  8.3 6.1 %all-to-all-start = ((f32[8,64,128]{2,1,0:T(8,128)}), f32[8,64,128]{2,1,0:T(8,128)S(1)}, u32[]{:S(2)}, u32[]{:S(2)}) async-start(f32[8,64,128]{2,1,0:T(8,128)} %broadcast_in_dim.29), calls=%async_computation | async-start | bytes 524288 | tf_op jit(solution)/shard_map/all_to_all | solution.py:374
  20.3 5.1 %state_kernel.1 = (f32[32,128,128]{2,1,0:T(8,128)}, bf16[256,4096]{1,0:T(8,128)(2,1)}) custom-call(s32[256,256]{1,0:T(8,128)} %refs_0_.6, bf16[256,4096]{1,0:T(8,128)(2,1)} %refs_7_.1, f32[4,8,256]{2,1,0:T(8,128)} %reduce_window_sum.20.refs_1_.refs_2_.refs_6_.refs_9_), custom_call_target="tpu_custom_call" | custom-call | flops 1 | bytes 1 | tf_op jit(solution)/shard_map/state_kernel/pallas_call | solution.py:336
  29.2 6.3 %weight_kernel.1 = (bf16[32,256,256]{2,1,0:T(8,128)(2,1)}, f32[4,8,256]{2,1,0:T(8,128)}, bf16[256,4096]{1,0:T(8,128)(2,1)}) custom-call(s32[256,256]{1,0:T(8,128)} %refs_0_.9, bf16[256,4096]{1,0:T(8,128)(2,1)} %get-tuple-element.35.refs_1_.refs_6_, f32[4,8,256]{2,1,0:T(8,128)} %reduce_window_sum.20.refs_1_.refs_2_.refs_6_.refs_9_), custom_call_target="tpu_custom_call" | custom-call | flops 1 | bytes 1 | tf_op jit(solution)/shard_map/weight_kernel/pallas_call | solution.py:336
  37.8 6.3 %adjoint_kernel.2 = (f32[4,8,256]{2,1,0:T(8,128)}, f32[4,4,136,128]{3,2,1,0:T(8,128)}, f32[4,2,256,512]{3,2,1,0:T(8,128)}) custom-call(s32[256,256]{1,0:T(8,128)} %refs_0_.9, bf16[256,4096]{1,0:T(8,128)(2,1)} %refs_8_.1, f32[4,8,256]{2,1,0:T(8,128)} %reduce_window_sum.20.refs_1_.refs_2_.refs_6_.refs_9_, f32[4,8,256]{2,1,0:T(8,128)} %get-tuple-element.36.refs_3_, ...), custom_call_target="tpu_custom_call" | custom-call | flops 1 | bytes 1 | tf_op jit(solution)/shard_map/adjoint_kernel/pallas_call | solution.py:336
  50.8 6.4 %adjoint_kernel.3 = (f32[4,8,256]{2,1,0:T(8,128)}, f32[4,4,136,128]{3,2,1,0:T(8,128)}, f32[4,2,256,512]{3,2,1,0:T(8,128)}) custom-call(s32[256,256]{1,0:T(8,128)} %refs_0_.9, bf16[256,4096]{1,0:T(8,128)(2,1)} %refs_8_.1, f32[4,8,256]{2,1,0:T(8,128)} %reduce_window_sum.20.refs_1_.refs_2_.refs_6_.refs_9_, ...), custom_call_target="tpu_custom_call", output_to_operand_aliasing={{2}: (6, {})} | custom-call | flops 1 | bytes 1 | tf_op jit(solution)/shard_map/adjoint_kernel/pallas_call | solution.py:336
  57.2 11.4 %all-to-all-done.1.received.refs_8_ = f32[4,4,136,128]{3,2,1,0:T(8,128)S(1)} async-done(((f32[4,4,136,128]{3,2,1,0:T(8,128)}), f32[4,4,136,128]{3,2,1,0:T(8,128)S(1)}, u32[]{:S(2)}, u32[]{:S(2)}) %all-to-all-start.1) | async-done | bytes 1114144 | tf_op jit(solution)/shard_map/all_to_all | solution.py:360
  69.6 4.0 %all-to-all-start.2 = ((f32[4,4,136,128]{3,2,1,0:T(8,128)}), f32[4,4,136,128]{3,2,1,0:T(8,128)S(1)}, u32[]{:S(2)}, u32[]{:S(2)}) async-start(f32[4,4,136,128]{3,2,1,0:T(8,128)} %get-tuple-element.40.refs_2_), calls=%async_computation.2 | async-start | bytes 2228224 | tf_op jit(solution)/shard_map/all_to_all | solution.py:360
  76.9 11.2 %all-to-all-done.2.received.refs_8_ = f32[4,4,136,128]{3,2,1,0:T(8,128)S(1)} async-done(((f32[4,4,136,128]{3,2,1,0:T(8,128)}), f32[4,4,136,128]{3,2,1,0:T(8,128)S(1)}, u32[]{:S(2)}, u32[]{:S(2)}) %all-to-all-start.2) | async-done | bytes 1114144 | tf_op jit(solution)/shard_map/all_to_all | solution.py:360
  89.1 4.9 %all-to-all-start.3 = ((f32[4,2,256,512]{3,2,1,0:T(8,128)}), f32[4,2,256,512]{3,2,1,0:T(8,128)}, u32[]{:S(2)}, u32[]{:S(2)}) async-start(f32[4,2,256,512]{3,2,1,0:T(8,128)} %get-tuple-element.48), calls=%async_computation.3 | async-start | bytes 8388608 | tf_op jit(solution)/shard_map/all_to_all | solution.py:360
  94.8 6.0 %local_kernel.1.order.refs_3_ = f32[256,4096]{1,0:T(8,128)} custom-call(bf16[32,256,256]{2,1,0:T(8,128)(2,1)} %get-tuple-element.37.refs_5_.refs_0_, bf16[256,4096]{1,0:T(8,128)(2,1)} %refs_7_.1, f32[4,4,136,128]{3,2,1,0:T(8,128)} %get-tuple-element.40.refs_2_, f32[4,256,256]{2,1,0:T(8,128)} %collective-permute-done.4.refs_3_.refs_10_), custom_call_target="tpu_custom_call" | custom-call | flops 1 | bytes 1 | tf_op jit(solution)/shard_map/local_kernel/pallas_call | solution.py:336
  111.2 7.6 %collective-permute-done.8 = f32[2,4,128,128]{3,2,1,0:T(8,128)S(1)} collective-permute-done((f32[2,4,128,128]{3,2,1,0:T(8,128)}, f32[2,4,128,128]{3,2,1,0:T(8,128)S(1)}, u32[]{:S(2)}, u32[]{:S(2)}) %collective-permute-start.8) | collective-permute-done | bytes 524320 | tf_op jit(solution)/shard_map/ppermute | solution.py:532
  121.2 7.0 %collective-permute-done.5 = f32[2,4,128,128]{3,2,1,0:T(8,128)S(1)} collective-permute-done((f32[2,4,128,128]{3,2,1,0:T(8,128)}, f32[2,4,128,128]{3,2,1,0:T(8,128)S(1)}, u32[]{:S(2)}, u32[]{:S(2)}) %collective-permute-start.5) | collective-permute-done | bytes 524320 | tf_op jit(solution)/shard_map/ppermute | solution.py:532
  138.9 8.8 %collective-permute-done.10 = f32[2,4,128,128]{3,2,1,0:T(8,128)S(1)} collective-permute-done((f32[2,4,128,128]{3,2,1,0:T(8,128)}, f32[2,4,128,128]{3,2,1,0:T(8,128)S(1)}, u32[]{:S(2)}, u32[]{:S(2)}) %collective-permute-start.10) | collective-permute-done | bytes 524320 | tf_op jit(solution)/shard_map/ppermute | solution.py:532
  149.7 9.3 %collective-permute-done.7 = f32[2,4,128,128]{3,2,1,0:T(8,128)S(1)} collective-permute-done((f32[2,4,128,128]{3,2,1,0:T(8,128)}, f32[2,4,128,128]{3,2,1,0:T(8,128)S(1)}, u32[]{:S(2)}, u32[]{:S(2)}) %collective-permute-start.7) | collective-permute-done | bytes 524320 | tf_op jit(solution)/shard_map/ppermute | solution.py:532
  160.9 12.3 %block_kernel.2 = (f32[8,8,32,128]{3,2,1,0:T(8,128)}, f32[8,8,32,128]{3,2,1,0:T(8,128)}, f32[4,128,128]{2,1,0:T(8,128)}, f32[4,128,128]{2,1,0:T(8,128)}, f32[4,128,128]{2,1,0:T(8,128)}, /*index=5*/f32[4,128,128]{2,1,0:T(8,128)}) custom-call(s32[1]{0:T(128)} %bitcast.1.refs_0_.refs_1_.quad, s32[1]{0:T(128)} %bitcast.35.refs_1_, ...), custom_call_target="tpu_custom_call" | custom-call | flops 1 | bytes 41943040 | tf_op jit(solution)/shard_map/block_kernel/pallas_call | solution.py:561
  177.9 12.3 %block_kernel.3 = (f32[8,8,32,128]{3,2,1,0:T(8,128)}, f32[8,8,32,128]{3,2,1,0:T(8,128)}, f32[4,128,128]{2,1,0:T(8,128)}, f32[4,128,128]{2,1,0:T(8,128)}, f32[4,128,128]{2,1,0:T(8,128)}, /*index=5*/f32[4,128,128]{2,1,0:T(8,128)}) custom-call(s32[1]{0:T(128)} %bitcast.1.refs_0_.refs_1_.quad, s32[1]{0:T(128)} %bitcast.35.refs_1_, ...), custom_call_target="tpu_custom_call" | custom-call | flops 1 | bytes 41943040 | tf_op jit(solution)/shard_map/block_kernel/pallas_call | solution.py:561
  192.2 13.1 %collective-permute-done.18 = f32[8,8,32,128]{3,2,1,0:T(8,128)} collective-permute-done((f32[8,8,32,128]{3,2,1,0:T(8,128)}, f32[8,8,32,128]{3,2,1,0:T(8,128)}, u32[]{:S(2)}, u32[]{:S(2)}) %collective-permute-start.18) | collective-permute-done | bytes 1048608 | tf_op jit(solution)/shard_map/ppermute | solution.py:600
  212.1 12.8 %output_kernel.1 = (f32[4,256,8]{2,1,0:T(8,128)}, f32[4,8,128]{2,1,0:T(8,128)}) custom-call(s32[1]{0:T(128)} %bitcast.refs_0_, f32[16,128,128]{2,1,0:T(8,128)} %get-tuple-element.70.refs_1_.refs_2_, f32[16,128,128]{2,1,0:T(8,128)} %collective-permute-done.11.refs_2_.refs_3_, f32[256,4096]{1,0:T(8,128)} %local_kernel.1.order.refs_3_, ...), custom_call_target="tpu_custom_call" | custom-call | flops 1 | bytes 41943040 | tf_op jit(solution)/shard_map/output_kernel/pallas_call | solution.py:336
  225.0 4.3 %collective-permute-done.23 = f32[8,8,32,128]{3,2,1,0:T(8,128)} collective-permute-done((f32[8,8,32,128]{3,2,1,0:T(8,128)}, f32[8,8,32,128]{3,2,1,0:T(8,128)}, u32[]{:S(2)}, u32[]{:S(2)}) %collective-permute-start.23) | collective-permute-done | bytes 1048608 | tf_op jit(solution)/shard_map/ppermute | solution.py:600
  234.2 7.0 %all-to-all-start.4 = ((f32[8,64,128]{2,1,0:T(8,128)}), f32[8,64,128]{2,1,0:T(8,128)S(1)}, u32[]{:S(2)}, u32[]{:S(2)}) async-start(f32[8,64,128]{2,1,0:T(8,128)} %broadcast_in_dim.58), calls=%async_computation.4 | async-start | bytes 524288 | tf_op jit(solution)/shard_map/all_to_all | solution.py:374
  244.9 13.4 %collective-permute-done.24 = f32[4,8,32,128]{3,2,1,0:T(8,128)} collective-permute-done((f32[4,8,32,128]{3,2,1,0:T(8,128)}, f32[4,8,32,128]{3,2,1,0:T(8,128)}, u32[]{:S(2)}, u32[]{:S(2)}) %collective-permute-start.24) | collective-permute-done | bytes 524320 | tf_op jit(solution)/shard_map/ppermute | solution.py:600
  271.5 17.7 %token_kernel.1 = (bf16[256,4096]{1,0:T(8,128)(2,1)}, f32[256,4096]{1,0:T(8,128)}) custom-call(s32[1]{0:T(128)} %bitcast.refs_0_, s32[1]{0:T(128)} %bitcast.1.refs_0_.refs_1_.quad, f32[16,128,128]{2,1,0:T(8,128)} %get-tuple-element.70.refs_1_.refs_2_, f32[16,128,128]{2,1,0:T(8,128)} %collective-permute-done.11.refs_2_.refs_3_, f32[4,8,128]{2,1,0:T(8,128)} %fusion.26.refs_4_, ...), custom_call_target="tpu_custom_call" | custom-call | flops 1 | bytes 62914560 | tf_op jit(solution)/shard_map/token_kernel/pallas_call | solution.py:336
  289.9 5.7 %key_kernel.1 = bf16[256,4096]{1,0:T(8,128)(2,1)} custom-call(f32[256,4096]{1,0:T(8,128)} %get-tuple-element.59.refs_0_, f32[4,8,128]{2,1,0:T(8,128)} %fusion.3.refs_1_, f32[4,8,256]{2,1,0:T(8,128)} %reduce_window_sum.20.refs_1_.refs_2_.refs_6_.refs_9_, bf16[256,4096]{1,0:T(8,128)(2,1)} %refs_3_.1), custom_call_target="tpu_custom_call" | custom-call | flops 1 | bytes 8388608 | tf_op jit(solution)/shard_map/key_kernel/pallas_call | solution.py:336
  295.6 3.7 %finish_kernel.1 = f32[2,64,4096]{2,1,0:T(8,128)} custom-call(s32[1]{0:T(128)} %bitcast.1.refs_0_.refs_1_.quad, f32[2,8,32,128]{3,2,1,0:T(8,128)} %copy-done.11, f32[2,8,32,128]{3,2,1,0:T(8,128)} %collective-permute-done.20.refs_1_, f32[2,8,32,128]{3,2,1,0:T(8,128)} %collective-permute-done.21.refs_2_, f32[2,8,32,128]{3,2,1,0:T(8,128)} %copy-done.17, ...), custom_call_target="tpu_custom_call" | custom-call | flops 1 | bytes 4194304 | tf_op jit(solution)/shard_map/finish_kernel/pallas_call | solution.py:610
  (167 shorter events, 95.8 us)
Async XLA Ops:
  8.3 28.1 %all-to-all-start = ((f32[8,64,128]{2,1,0:T(8,128)}), f32[8,64,128]{2,1,0:T(8,128)S(1)}, u32[]{:S(2)}, u32[]{:S(2)}) async-start(f32[8,64,128]{2,1,0:T(8,128)} %broadcast_in_dim.29), calls=%async_computation | async-start | bytes 524288 | tf_op jit(solution)/shard_map/all_to_all | solution.py:374
  16.8 20.3 %collective-permute-start.3 = (f32[328,256]{1,0:T(8,128)}, f32[328,256]{1,0:T(8,128)S(1)}, u32[]{:S(2)}, u32[]{:S(2)}) collective-permute-start(f32[328,256]{1,0:T(8,128)} %get-tuple-element.75), channel_id=1, source_target_pairs={{0,18},{2,16},{4,22},{6,20},{8,26},{10,24},{12,30},{14,28},{16,2},... | collective-permute-start | bytes 1007624 | tf_op jit(solution)/shard_map/ppermute | solution.py:357
  27.8 46.3 %collective-permute-start = (f32[16,128,128]{2,1,0:T(8,128)}, f32[16,128,128]{2,1,0:T(8,128)}, u32[]{:S(2)}, u32[]{:S(2)}) collective-permute-start(f32[16,128,128]{2,1,0:T(8,128)} %constant_dynamic-slice_fusion.6), channel_id=1, source_target_pairs={{0,2},{2,0},{4,6},{6,4},{8,10},{10,8},{12,14},{14,12},{1,3},{3,1},... | collective-permute-start | bytes 3145736 | tf_op jit(solution)/shard_map/ppermute | solution.py:349
  44.1 24.5 %all-to-all-start.1 = ((f32[4,4,136,128]{3,2,1,0:T(8,128)}), f32[4,4,136,128]{3,2,1,0:T(8,128)S(1)}, u32[]{:S(2)}, u32[]{:S(2)}) async-start(f32[4,4,136,128]{3,2,1,0:T(8,128)} %get-tuple-element.38), calls=%async_computation.1 | async-start | bytes 2228224 | tf_op jit(solution)/shard_map/all_to_all | solution.py:360
  50.8 44.0 %collective-permute-start.4 = (f32[4,256,256]{2,1,0:T(8,128)}, f32[4,256,256]{2,1,0:T(8,128)}, u32[]{:S(2)}, u32[]{:S(2)}) collective-permute-start(f32[4,256,256]{2,1,0:T(8,128)} %pad_maximum_fusion.1), channel_id=1, source_target_pairs={{0,1},{1,0},{2,3},{3,2},{4,5},{5,4},{6,7},{7,6},{8,9},{9,8},{10,11... | collective-permute-start | bytes 3145736 | tf_op jit(solution)/shard_map/ppermute | solution.py:408
  89.1 71.8 %all-to-all-start.3 = ((f32[4,2,256,512]{3,2,1,0:T(8,128)}), f32[4,2,256,512]{3,2,1,0:T(8,128)}, u32[]{:S(2)}, u32[]{:S(2)}) async-start(f32[4,2,256,512]{3,2,1,0:T(8,128)} %get-tuple-element.48), calls=%async_computation.3 | async-start | bytes 8388608 | tf_op jit(solution)/shard_map/all_to_all | solution.py:360
  136.2 22.7 %collective-permute-start.7 = (f32[2,4,128,128]{3,2,1,0:T(8,128)}, f32[2,4,128,128]{3,2,1,0:T(8,128)S(1)}, u32[]{:S(2)}, u32[]{:S(2)}) collective-permute-start(f32[2,4,128,128]{3,2,1,0:T(8,128)} %multiply_add_fusion.3), channel_id=1, source_target_pairs={{4,0},{6,2},{8,12},{10,14},{5,1},{7,3},{9,13},{11,15},{20,16},{22,... | collective-permute-start | bytes 1572872 | tf_op jit(solution)/shard_map/ppermute | solution.py:532
  173.2 32.1 %collective-permute-start.18 = (f32[8,8,32,128]{3,2,1,0:T(8,128)}, f32[8,8,32,128]{3,2,1,0:T(8,128)}, u32[]{:S(2)}, u32[]{:S(2)}) collective-permute-start(f32[8,8,32,128]{3,2,1,0:T(8,128)} %get-tuple-element.62), channel_id=1, source_target_pairs={{0,4},{2,6},{4,0},{6,2},{8,12},{10,14},{12,8},{14,10},{1,5},{3,7},... | collective-permute-start | bytes 3145736 | tf_op jit(solution)/shard_map/ppermute | solution.py:600
  176.2 34.6 %collective-permute-start.11 = (f32[16,128,128]{2,1,0:T(8,128)}, f32[16,128,128]{2,1,0:T(8,128)}, u32[]{:S(2)}, u32[]{:S(2)}) collective-permute-start(f32[16,128,128]{2,1,0:T(8,128)} %get-tuple-element.69), channel_id=1, source_target_pairs={{0,2},{2,0},{4,6},{6,4},{8,10},{10,8},{12,14},{14,12},{1,3},{3,1},... | collective-permute-start | bytes 3145736 | tf_op jit(solution)/shard_map/ppermute | solution.py:349
  190.2 39.0 %collective-permute-start.23 = (f32[8,8,32,128]{3,2,1,0:T(8,128)}, f32[8,8,32,128]{3,2,1,0:T(8,128)}, u32[]{:S(2)}, u32[]{:S(2)}) collective-permute-start(f32[8,8,32,128]{3,2,1,0:T(8,128)} %get-tuple-element.64), channel_id=1, source_target_pairs={{0,4},{2,6},{4,0},{6,2},{8,12},{10,14},{12,8},{14,10},{1,5},{3,7},... | collective-permute-start | bytes 3145736 | tf_op jit(solution)/shard_map/ppermute | solution.py:600
  207.9 33.3 %collective-permute-start.19 = (f32[4,8,32,128]{3,2,1,0:T(8,128)}, f32[4,8,32,128]{3,2,1,0:T(8,128)S(1)}, u32[]{:S(2)}, u32[]{:S(2)}) collective-permute-start(f32[4,8,32,128]{3,2,1,0:T(8,128)} %slice.266), channel_id=1, source_target_pairs={{0,8},{2,10},{4,12},{6,14},{8,0},{10,2},{12,4},{14,6},{1,9},{3,11}... | collective-permute-start | bytes 1572872 | tf_op jit(solution)/shard_map/ppermute | solution.py:600
  207.9 34.9 %collective-permute-start.12 = (f32[4,128,128]{2,1,0:T(8,128)}, f32[4,128,128]{2,1,0:T(8,128)}, u32[]{:S(2)}, u32[]{:S(2)}) collective-permute-start(f32[4,128,128]{2,1,0:T(8,128)} %get-tuple-element.52), channel_id=1, source_target_pairs={{0,2},{2,0},{4,6},{6,4},{8,10},{10,8},{12,14},{14,12},{16,18},{18,... | collective-permute-start | bytes 786440 | tf_op jit(solution)/shard_map/ppermute | solution.py:357
  209.3 35.2 %collective-permute-start.13 = (f32[4,128,128]{2,1,0:T(8,128)}, f32[4,128,128]{2,1,0:T(8,128)}, u32[]{:S(2)}, u32[]{:S(2)}) collective-permute-start(f32[4,128,128]{2,1,0:T(8,128)} %get-tuple-element.53), channel_id=1, source_target_pairs={{0,16},{2,18},{4,20},{6,22},{8,24},{10,26},{12,28},{14,30},{16,0},... | collective-permute-start | bytes 786440 | tf_op jit(solution)/shard_map/ppermute | solution.py:357
  210.8 51.8 %collective-permute-start.14 = (f32[4,128,128]{2,1,0:T(8,128)}, f32[4,128,128]{2,1,0:T(8,128)}, u32[]{:S(2)}, u32[]{:S(2)}) collective-permute-start(f32[4,128,128]{2,1,0:T(8,128)} %get-tuple-element.54), channel_id=1, source_target_pairs={{0,18},{2,16},{4,22},{6,20},{8,26},{10,24},{12,30},{14,28},{16,2},... | collective-permute-start | bytes 786440 | tf_op jit(solution)/shard_map/ppermute | solution.py:357
  231.9 26.4 %collective-permute-start.24 = (f32[4,8,32,128]{3,2,1,0:T(8,128)}, f32[4,8,32,128]{3,2,1,0:T(8,128)}, u32[]{:S(2)}, u32[]{:S(2)}) collective-permute-start(f32[4,8,32,128]{3,2,1,0:T(8,128)} %slice.268), channel_id=1, source_target_pairs={{0,8},{2,10},{4,12},{6,14},{8,0},{10,2},{12,4},{14,6},{1,9},{3,11}... | collective-permute-start | bytes 1572872 | tf_op jit(solution)/shard_map/ppermute | solution.py:600
  234.2 55.0 %all-to-all-start.4 = ((f32[8,64,128]{2,1,0:T(8,128)}), f32[8,64,128]{2,1,0:T(8,128)S(1)}, u32[]{:S(2)}, u32[]{:S(2)}) async-start(f32[8,64,128]{2,1,0:T(8,128)} %broadcast_in_dim.58), calls=%async_computation.4 | async-start | bytes 524288 | tf_op jit(solution)/shard_map/all_to_all | solution.py:374
  241.2 23.6 %collective-permute-start.15 = (f32[4,128,128]{2,1,0:T(8,128)}, f32[4,128,128]{2,1,0:T(8,128)S(1)}, u32[]{:S(2)}, u32[]{:S(2)}) collective-permute-start(f32[4,128,128]{2,1,0:T(8,128)} %get-tuple-element.55), channel_id=1, source_target_pairs={{0,2},{2,0},{4,6},{6,4},{8,10},{10,8},{12,14},{14,12},{16,18},{18,... | collective-permute-start | bytes 786440 | tf_op jit(solution)/shard_map/ppermute | solution.py:357
  242.8 22.0 %collective-permute-start.16 = (f32[4,128,128]{2,1,0:T(8,128)}, f32[4,128,128]{2,1,0:T(8,128)S(1)}, u32[]{:S(2)}, u32[]{:S(2)}) collective-permute-start(f32[4,128,128]{2,1,0:T(8,128)} %get-tuple-element.56), channel_id=1, source_target_pairs={{0,16},{2,18},{4,20},{6,22},{8,24},{10,26},{12,28},{14,30},{16,0},... | collective-permute-start | bytes 786440 | tf_op jit(solution)/shard_map/ppermute | solution.py:357
  244.5 20.6 %collective-permute-start.17 = (f32[4,128,128]{2,1,0:T(8,128)}, f32[4,128,128]{2,1,0:T(8,128)S(1)}, u32[]{:S(2)}, u32[]{:S(2)}) collective-permute-start(f32[4,128,128]{2,1,0:T(8,128)} %get-tuple-element.57), channel_id=1, source_target_pairs={{0,18},{2,16},{4,22},{6,20},{8,26},{10,24},{12,30},{14,28},{16,2},... | collective-permute-start | bytes 786440 | tf_op jit(solution)/shard_map/ppermute | solution.py:357
  262.6 33.0 %collective-permute-start.20 = (f32[2,8,32,128]{3,2,1,0:T(8,128)S(1)}, f32[2,8,32,128]{3,2,1,0:T(8,128)}, u32[]{:S(2)}, u32[]{:S(2)}) collective-permute-start(f32[2,8,32,128]{3,2,1,0:T(8,128)S(1)} %get-tuple-element.87), channel_id=1, source_target_pairs={{0,2},{2,0},{4,6},{6,4},{8,10},{10,8},{12,14},{14,12},{16,18},{18,... | collective-permute-start | bytes 786440 | tf_op jit(solution)/shard_map/ppermute | solution.py:357
  264.7 30.8 %collective-permute-start.27 = (f32[2,8,32,128]{3,2,1,0:T(8,128)}, f32[2,8,32,128]{3,2,1,0:T(8,128)}, u32[]{:S(2)}, u32[]{:S(2)}) collective-permute-start(f32[2,8,32,128]{3,2,1,0:T(8,128)} %get-tuple-element.85), channel_id=1, source_target_pairs={{0,18},{2,16},{4,22},{6,20},{8,26},{10,24},{12,30},{14,28},{16,2},... | collective-permute-start | bytes 786440 | tf_op jit(solution)/shard_map/ppermute | solution.py:357
  264.8 30.8 %collective-permute-start.25 = (f32[2,8,32,128]{3,2,1,0:T(8,128)}, f32[2,8,32,128]{3,2,1,0:T(8,128)}, u32[]{:S(2)}, u32[]{:S(2)}) collective-permute-start(f32[2,8,32,128]{3,2,1,0:T(8,128)} %get-tuple-element.85), channel_id=1, source_target_pairs={{0,2},{2,0},{4,6},{6,4},{8,10},{10,8},{12,14},{14,12},{16,18},{18,... | collective-permute-start | bytes 786440 | tf_op jit(solution)/shard_map/ppermute | solution.py:357
  265.2 30.4 %collective-permute-start.21 = (f32[2,8,32,128]{3,2,1,0:T(8,128)S(1)}, f32[2,8,32,128]{3,2,1,0:T(8,128)}, u32[]{:S(2)}, u32[]{:S(2)}) collective-permute-start(f32[2,8,32,128]{3,2,1,0:T(8,128)S(1)} %get-tuple-element.88.refs_0_), channel_id=1, source_target_pairs={{0,16},{2,18},{4,20},{6,22},{8,24},{10,26},{12,28},{14,30},{16,0},... | collective-permute-start | bytes 786440 | tf_op jit(solution)/shard_map/ppermute | solution.py:357
  268.2 27.4 %collective-permute-start.26 = (f32[2,8,32,128]{3,2,1,0:T(8,128)S(1)}, f32[2,8,32,128]{3,2,1,0:T(8,128)}, u32[]{:S(2)}, u32[]{:S(2)}) collective-permute-start(f32[2,8,32,128]{3,2,1,0:T(8,128)S(1)} %get-tuple-element.86.refs_4_), channel_id=1, source_target_pairs={{0,16},{2,18},{4,20},{6,22},{8,24},{10,26},{12,28},{14,30},{16,0},... | collective-permute-start | bytes 786440 | tf_op jit(solution)/shard_map/ppermute | solution.py:357
  (30 other events, 364.1 us)

commit v4 on v3

--- a/solution.py
+++ b/solution.py
@@ -72,35 +72,43 @@
     return jnp.concatenate([high, low, low2, jnp.zeros((13, n), BF16)], axis=0)
 
 
+def put_message(out, i, vector, total):
+    copies = out.shape[0]
+    out[:, 0, i : i + 1, :] = jnp.broadcast_to(vector[None], (copies, 1, HEAD))
+    out[:, 0, 8 + i : 9 + i, :] = jnp.broadcast_to(total[None], (copies, 1, HEAD))
+
+
 def key_sums_kernel(heads, kw, cum, out):
     for i in range(heads):
         row = cum[0, i : i + 1, :]
         tail = jnp.exp(row[:, -1:] - row)
         k = unpack(kw[i * WORDS : (i + 1) * WORDS, :]).astype(BF16)
-        out[0, i : i + 1, :] = jnp.sum(nt(rows_of(tail), k), axis=0, keepdims=True)
-
-
-def state_kernel(heads, kw, v, cum, y_out, kt_out):
+        vector = jnp.sum(nt(rows_of(tail), k), axis=0, keepdims=True)
+        put_message(out, i, vector, jnp.exp(row[:, -1:]))
+
+
+def state_kernel(heads, kw, v, cum, y_out):
     for i in range(heads):
         row = cum[0, i : i + 1, :]
         k = unpack(kw[i * WORDS : (i + 1) * WORDS, :])
-        kt_out[:, lanes(i)] = jnp.transpose(k).astype(BF16)
         high, low = split(k * jnp.exp(row[:, -1:] - row))
         value = v[:, lanes(i)]
         y_out[i] = nn(high, value) + nn(low, value)
 
 
-def weight_kernel(heads, qw, kt, cum, wt_out, den_out, qt_out):
-    tokens = kt.shape[0]
+def weight_kernel(heads, qw, kw, cum, wt_out, den_out, qt_out, kt_out):
+    tokens = kt_out.shape[0]
     cols = jnp.transpose(cum[0])
     after = causal((tokens, tokens), 1)
     for i in range(heads):
         row = cum[0, i : i + 1, :]
         col = cols[:, i : i + 1]
         q = unpack(qw[i * WORDS : (i + 1) * WORDS, :])
+        kt = jnp.transpose(unpack(kw[i * WORDS : (i + 1) * WORDS, :])).astype(BF16)
+        kt_out[:, lanes(i)] = kt
         qt_out[:, lanes(i)] = jnp.transpose(q).astype(BF16)
         decay = jnp.where(after, jnp.exp(jnp.minimum(row - col, 0.0)), 0.0)
-        w = nn(kt[:, lanes(i)], q.astype(BF16)) * decay
+        w = nn(kt, q.astype(BF16)) * decay
         wt_out[i] = w.astype(BF16)
         den_out[0, i : i + 1, :] = jnp.sum(w, axis=0, keepdims=True)
 
@@ -112,13 +120,32 @@
     send_out[0] = jnp.where(z[0] == 0, up[0], down)
 
 
+def turn_kernel(sizes, z, y, first, decay, order, *refs):
+    hops, (keep_out, send_out) = refs[:-2], refs[-2:]
+    count = len(hops) // CHUNKS
+    for n in range(CHUNKS):
+        for i in range(sizes[n]):
+            at = n * sizes[0] + i
+            reach = jnp.zeros((HEAD, HEAD), F32)
+            for hop in range(count):
+                reach = jnp.where(z[0] == hop + 1, hops[n * count + hop][i], reach)
+            later = decay[at] * reach + first[at]
+            keep_out[at] = jnp.where(y[0] == 0, reach, later)
+            send_out[at] = jnp.where(y[0] == 0, later, reach)
+
+
+def sum_kernel(y, *refs):
+    terms, (own_out, other_out) = refs[:-3], refs[-2:]
+    own_out[...] = sum((term[...] for term in terms[2::2]), terms[0][...])
+    other_out[...] = sum((term[...] for term in terms[3::2]), terms[1][...])
+
+
 def local_kernel(heads, wt, v, out):
     for i in range(heads):
         out[:, lanes(i)] = tn(wt[i], v[:, lanes(i)])
 
 
-def adjoint_kernel(start, heads, qw, do, cum, den_local, z0, wt, *refs):
-    den_out, x_out, dv_out = refs[-3:]
+def adjoint_kernel(start, heads, qw, do, cum, den_local, z0, wt, den_out, x_out, dv_out):
     tokens = do.shape[0]
     rows = []
     qs = []
@@ -139,11 +166,11 @@
         lead = leads[:, start + i : start + i + 1]
         x_out[0, i, :HEAD, :] = fold(nn(qs[i], jnp.concatenate(split(g * lead), axis=1)))
         x_out[0, i, HEAD:, :] = jnp.broadcast_to(lead[-1:, :], (8, HEAD))
-        dv_out[0, 0, :, lanes(i)] = nn(wt[i], g.astype(BF16))
+        dv_out[0, :, lanes(i)] = nn(wt[i], g.astype(BF16))
 
 
 def output_kernel(chunk, heads, y, keep, got, local, qt, do, cum, *refs):
-    dens, (h_out, xv_out) = refs[:-3], refs[-2:]
+    dens, (h_out, xv_out) = refs[:CHUNKS], refs[-2:]
     cols = jnp.transpose(cum[0])
     inverses = [jnp.transpose(1.0 / den[0]) for den in dens]
     kept = pl.program_id(0) // 2 == y[0]
@@ -158,12 +185,12 @@
         o = (local[:, lanes(i)] + lead * carried) * inverse
         h = -jnp.sum(grad * o, axis=1, keepdims=True) * inverse
         h_out[0, :, i : i + 1] = h
-        xv_out[0, i : i + 1, :] = jnp.sum(q.astype(F32) * (lead * h), axis=0, keepdims=True)
-
-
-def token_kernel(chunk, heads, y, quad, keep, got, z0, qt, kt, v, do, cum, slope, h_in, *refs):
+        vector = jnp.sum(q.astype(F32) * (lead * h), axis=0, keepdims=True)
+        put_message(xv_out, i, vector, lead[-1:, :])
+
+
+def token_kernel(chunk, heads, y, keep, got, z0, qt, kt, v, do, cum, slope, h_in, *refs):
     dens, adjoints, (dq_out, dk_out) = refs[:CHUNKS], refs[CHUNKS:-2], refs[-2:]
-    offset = pl.program_id(0) ^ quad[0]
     tokens = v.shape[0]
     cols = jnp.transpose(cum[0])
     inverses = [jnp.transpose(1.0 / den[0]) for den in dens]
@@ -184,9 +211,7 @@
         back = fold(nt(g, jnp.concatenate(split(state), axis=0))) + h * z0[0, i : i + 1, :]
         dq = nn(r, kt[:, lanes(i)]) + lead * back
         dq_out[:, lanes(i)] = (slope[:, lanes(i)].astype(F32) * dq).astype(BF16)
-        adjoint = adjoints[QUAD * (i // chunk)][i % chunk]
-        for at in range(1, QUAD):
-            adjoint = jnp.where(offset == at, adjoints[QUAD * (i // chunk) + at][i % chunk], adjoint)
+        adjoint = adjoints[i // chunk][0, i % chunk]
         carried = fold(nt(value, jnp.concatenate(split(adjoint), axis=0)))
         dk_out[:, lanes(i)] = tn(r, qt[:, lanes(i)]) + tail * carried
 
@@ -200,16 +225,17 @@
         out[:, lanes(i)] = (slope[:, lanes(i)].astype(F32) * total).astype(BF16)
 
 
-def block_kernel(start, quad, core, pattern, *refs):
-    keep_out, send_out, *adjoint_outs = refs[-6 - QUAD : -4]
-    flags, lines, others, found = refs[-4:]
-    pieces, (grads, parts, reach), other_pieces = refs[:QUAD], refs[QUAD : QUAD + 3], refs[QUAD + 3 : -7 - QUAD]
-    tokens = grads.shape[2]
+def block_kernel(start, hops, quad, core, z, pattern, *refs):
+    keep_out, send_out, adjoint_out, flags, lines, others = refs[-6:]
+    pieces, (grads, parts), refs = refs[:QUAD], refs[QUAD : QUAD + 2], refs[QUAD + 2 : -7]
+    reaches, other_pieces = refs[:hops], refs[hops:]
+    tokens = grads.shape[1]
     key_rows = others.shape[1] - 8
     ncore = 1 + len(other_pieces)
     spike_rows = lines.shape[1] // ncore
     step = pl.program_id(0)
-    shifts = 2 * lax.broadcasted_iota(jnp.int32, (8, tokens), 0)
+    tests = jnp.left_shift(1, 2 * lax.broadcasted_iota(jnp.int32, (8, tokens), 0))
+    tests = [tests, 2 * tests]
     low = lax.broadcasted_iota(jnp.int32, (tokens, HEAD), 1) < BLK
 
     @pl.when(step == 0)
@@ -224,18 +250,19 @@
 
     values = []
     for source in range(QUAD):
+        reach = jnp.zeros((HEAD, HEAD), F32)
+        for hop in range(hops):
+            reach = jnp.where(z[0] == hops - 1 - hop, reaches[hop][source // 2, 0], reach)
         if source % 2:
-            adjoint = reach[source // 2, 0]
+            adjoint = reach
         else:
-            adjoint = parts[source + 1, 0, :HEAD, :] + parts[source + 1, 0, HEAD : HEAD + 1, :] * reach[source // 2, 0]
-        found[source] = adjoint
+            adjoint = parts[source + 1, 0, :HEAD, :] + parts[source + 1, 0, HEAD : HEAD + 1, :] * reach
+        adjoint_out[source, 0] = adjoint
         row = others[source, pl.ds(key_rows + start + step, 1), :]
         words = others[source, pl.ds(pl.multiple_of((start + step) * WORDS, WORDS), WORDS), :]
         k = unpack(words.astype(jnp.int32)) * jnp.exp(row[:, -1:] - row)
         carried = fold(tn(k.astype(BF16), jnp.concatenate(split(adjoint), axis=1)))
-        values.append((grads[source, 0] + carried).astype(BF16).astype(F32))
-    for i in range(QUAD):
-        adjoint_outs[i][0] = found[quad[0] ^ i]
+        values.append((grads[source] + carried).astype(BF16).astype(F32))
     for side in range(2):
         total = None
         for source in range(QUAD):
@@ -252,10 +279,11 @@
                     for word in range(BLK // 16):
                         line = lines[source, pl.ds(first + word, 1), :]
                         spread = jnp.broadcast_to(line, (8, tokens))
-                        flag_parts.append(jnp.bitwise_and(jnp.right_shift(spread, shifts + parity), 1))
-                    bits = jnp.concatenate(flag_parts, axis=0).astype(F32).astype(BF16)
-                    flags[s * HALF : (s + 1) * HALF, parity * tokens : (parity + 1) * tokens] = bits
-            part = nn(flags[...], right)
+                        spread = jnp.bitwise_and(spread, tests[parity])
+                        flag_parts.append(jnp.where(spread != 0, 1.0, 0.0))
+                    bits = jnp.concatenate(flag_parts, axis=0).astype(BF16)
+                    flags[source, s * HALF : (s + 1) * HALF, parity * tokens : (parity + 1) * tokens] = bits
+            part = nn(flags[source], right)
             total = part if total is None else total + part
         total = total.reshape(SEL, HALF, HEAD)
         keep_out[:, side] = total[: SEL // 2]
@@ -302,7 +330,6 @@
     planes = [[d * nctx + 2 * c + i for d in range(ndp) for i in range(2)] for c in range(nz)]
 
     gate_sums = jnp.cumsum(log_gate, axis=1)
-    totals = jnp.exp(gate_sums[:, -1])
     cum = gate_sums.reshape(QUAD, heads, tokens)
     cum = jnp.pad(cum, ((0, 0), (0, 8 - heads), (0, 0)))
 
@@ -359,37 +386,30 @@
     def plane(value):
         return lax.all_to_all(value, ("dp", "ctx"), 0, 0, axis_index_groups=planes, tiled=True)
 
-    def vec(a):
-        return jnp.pad(a.reshape(QUAD, heads, HEAD), ((0, 0), (0, 8 - heads), (0, 0)))
-
-    def unvec(a):
-        return a[:, :heads].reshape(heads_here, HEAD)
-
     def ordered(own, got):
         return jnp.where(y == 0, own, got), jnp.where(y == 0, got, own)
 
-    def carried_vectors(vector, forward):
-        message = jnp.concatenate([vector, jnp.broadcast_to(totals[:, None], vector.shape)], axis=0)
-        message = jnp.broadcast_to(message[None], (nctx,) + message.shape)
+    def carried_vectors(message, forward):
         parts = lax.all_to_all(message, "ctx", 0, 0, tiled=True)
-        reach = jnp.zeros_like(vector)
+        reach = jnp.zeros(vecs.shape, F32)
         for at in range(nctx) if forward else range(nctx - 1, -1, -1):
             inside = at < place if forward else at > place
-            reach = jnp.where(inside, parts[at, heads_here:] * reach + parts[at, :heads_here], reach)
-        return reach, parts[:, heads_here:, 0]
-
-    key_sum = call(
+            reach = jnp.where(inside, parts[at, :, 8:] * reach + parts[at, :, :8], reach)
+        return reach, parts[:, :, 8 : 8 + heads, 0].reshape(nctx, heads_here)
+
+    message_spec = spec((nctx, 1, 16, HEAD), lambda j: (0, j, 0, 0))
+    messages = shape(nctx, QUAD, 16, HEAD)
+    message = call(
         "key_sums_kernel",
         lambda *refs: key_sums_kernel(heads, *refs),
         [word_spec, cum_spec],
-        vec_spec,
-        vecs,
+        message_spec,
+        messages,
         cost(1, 1),
         key_spikes,
         cum,
     )
-    z0, decays = carried_vectors(unvec(key_sum), True)
-    z0 = vec(z0)
+    z0, decays = carried_vectors(message, True)
     first_total = lax.dynamic_index_in_dim(decays, 2 * z, 0, keepdims=False)
     second_total = lax.dynamic_index_in_dim(decays, 2 * z + 1, 0, keepdims=False)
 
@@ -409,33 +429,42 @@
         for k in range(1, ncore)
     ]
 
-    state_sum, kt = call(
-        "state_kernel",
-        lambda *refs: state_kernel(heads, *refs),
-        [word_spec, flat_spec, cum_spec],
-        [state_spec, flat_spec],
-        [states, flat16],
-        cost(1, 1),
-        key_spikes,
-        values,
-        cum,
-    )
-    wt, den_local, qt = call(
+    def state_half(side):
+        return pl.pallas_call(
+            lambda side, *refs: state_kernel(heads, *refs),
+            grid_spec=pltpu.PrefetchScalarGridSpec(
+                num_scalar_prefetch=1,
+                grid=(2,),
+                in_specs=[
+                    pl.BlockSpec((heads * WORDS, tokens), lambda j, side: (2 * side[0] + j, 0)),
+                    pl.BlockSpec((tokens, heads * HEAD), lambda j, side: (0, 2 * side[0] + j)),
+                    pl.BlockSpec((1, 8, tokens), lambda j, side: (2 * side[0] + j, 0, 0)),
+                ],
+                out_specs=state_spec,
+            ),
+            out_shape=shape(heads_here // 2, HEAD, HEAD),
+            compiler_params=params(),
+            cost_estimate=cost(1, 1),
+            name="state_kernel",
+        )(side.astype(jnp.int32).reshape(1), key_spikes, values, cum)
+
+    state_other = swap(state_half(1 - y))
+    state_mine = state_half(y)
+    wt, den_local, qt, kt = call(
         "weight_kernel",
         lambda *refs: weight_kernel(heads, *refs),
-        [word_spec, flat_spec, cum_spec],
-        [wt_spec, cum_spec, flat_spec],
-        [shape(heads_here, tokens, tokens, kind=BF16), cums, flat16],
+        [word_spec, word_spec, cum_spec],
+        [wt_spec, cum_spec, flat_spec, flat_spec],
+        [shape(heads_here, tokens, tokens, kind=BF16), cums, flat16, flat16],
         cost(1, 1),
         query_spikes,
-        kt,
+        key_spikes,
         cum,
     )
-    dens, adjoint_sums, value_parts = [], [], None
+    dens, adjoint_sums, value_parts = [], [], []
     anywhere = pl.BlockSpec(memory_space=pl.ANY)
     for n in range(CHUNKS):
-        extra = pieces if n == 0 else [value_parts]
-        den, adjoint_sum, value_parts = call(
+        den, adjoint_sum, value_part = call(
             "adjoint_kernel",
             lambda *refs, n=n: adjoint_kernel(n * chunk, chunk, *refs),
             [
@@ -445,14 +474,13 @@
                 cum_spec,
                 vec_spec,
                 spec((chunk, tokens, tokens), lambda j, n=n: (j * CHUNKS + n, 0, 0)),
-            ]
-            + [anywhere] * len(extra),
+            ],
             [
                 cum_spec,
                 spec((1, chunk, HEAD + 8, HEAD), lambda j: (j, 0, 0, 0)),
-                spec((1, 1, tokens, chunk * HEAD), lambda j, n=n: (j, n, 0, 0)),
+                spec((1, tokens, chunk * HEAD), lambda j: (j, 0, 0)),
             ],
-            [cums, shape(QUAD, chunk, HEAD + 8, HEAD), shape(QUAD, CHUNKS, tokens, chunk * HEAD)],
+            [cums, shape(QUAD, chunk, HEAD + 8, HEAD), shape(QUAD, tokens, chunk * HEAD)],
             cost(1, 1),
             query_spikes,
             grad_out,
@@ -460,11 +488,10 @@
             den_local,
             z0,
             wt,
-            *extra,
-            aliases={6: 2} if n else {},
         )
         dens.append(den)
         adjoint_sums.append(adjoint_sum)
+        value_parts.append(value_part)
 
     local = call(
         "local_kernel",
@@ -480,19 +507,20 @@
     )
 
     half = heads_here // 2
-    mine, other = y * half, (1 - y) * half
+    mine = y * half
 
     def cut(value, start):
         return lax.dynamic_slice_in_dim(value, start, half, 0)
 
-    first, second = ordered(cut(state_sum, mine), swap(cut(state_sum, other)))
+    first, second = ordered(state_mine, state_other)
     first_decay = cut(first_total, mine)[:, None, None]
     second_decay = cut(second_total, mine)[:, None, None]
     state_both = second_decay * first + second
     state_decay = second_decay * first_decay
     part_size = half // CHUNKS
 
-    reaches, adjoint_parts = [], []
+    at_z = z.astype(jnp.int32).reshape(1)
+    hops, adjoint_parts = [], []
     for n in range(CHUNKS):
         received = plane(adjoint_sums[n])
         parts = received.reshape(2, 2, chunk, HEAD + 8, HEAD)
@@ -517,32 +545,21 @@
             compiler_params=params(),
             cost_estimate=cost(1, 1),
             name="start_kernel",
-        )(z.astype(jnp.int32).reshape(1), received, up, local)
+        )(at_z, received, up, local if n else received)
         up_decay = state_decay[n * part_size : (n + 1) * part_size].reshape(down_decay.shape)
-        reach = None
+        got = []
         for hop in range(nz - 1):
-            if reach is not None:
-                send = jnp.where(z == hop, up, down) + jnp.where(z == hop, up_decay, down_decay) * reach
+            if hop:
+                send = jnp.where(z == hop, up, down) + jnp.where(z == hop, up_decay, down_decay) * got[-1]
             pairs = []
             for c in range(nctx):
                 if c // 2 == hop:
                     pairs.append((c, c + 2))
                 elif c // 2 == nz - 1 - hop:
                     pairs.append((c, c - 2))
-            got = lax.ppermute(send, "ctx", pairs)
-            if reach is None:
-                reach = got
-                reach_up = jnp.where(z == hop + 1, got, 0.0)
-                reach_down = jnp.where(z == nz - 2 - hop, got, 0.0)
-            else:
-                reach = got
-                reach_up = jnp.where(z == hop + 1, got, reach_up)
-                reach_down = jnp.where(z == nz - 2 - hop, got, reach_down)
-        reaches.append(reach_up.reshape(part_size, HEAD, HEAD))
-        adjoint_parts.append((received, reach_down))
-    reach = jnp.concatenate(reaches, axis=0)
-    keep, send = ordered(reach, first_decay * reach + first)
-    state = [y.astype(jnp.int32).reshape(1), keep, swap(send)]
+            got.append(lax.ppermute(send, "ctx", pairs))
+        hops.append(got)
+        adjoint_parts.append(received)
 
     columns = pattern.shape[0] // QUAD
     share = SEL // nz
@@ -552,60 +569,152 @@
     order = ((z ^ turned)[:, None] * share + jnp.arange(share, dtype=jnp.int32)[None, :]).reshape(SEL)
     own_pattern = jnp.take(own_pattern, order, axis=1)
     columns = columns // CHUNKS
-    value_parts = plane(value_parts)
-    results, adjoints = [], []
+    terms_of, adjoints = [], []
     for n in range(CHUNKS):
         half_spec = spec((SEL // 2, 2, HALF, HEAD), lambda j: (0, j, 0, 0))
         half_shape = shape(SEL // 2, columns, HALF, HEAD)
-        after = adjoints[-1][0] if adjoints else adjoint_parts[n][1]
-        summed, send, *adjoint = pl.pallas_call(
-            lambda *refs, n=n: block_kernel(n * chunk, *refs),
+        after = state_keep if n else adjoint_parts[n]
+        summed, send, adjoint = pl.pallas_call(
+            lambda *refs, n=n: block_kernel(n * chunk, nz - 1, *refs),
             grid_spec=pltpu.PrefetchScalarGridSpec(
-                num_scalar_prefetch=3,
+                num_scalar_prefetch=4,
                 grid=(chunk,),
                 in_specs=[spec(piece.shape, lambda j: (0, 0)) for piece in pieces]
                 + [
-                    spec((QUAD, 1, tokens, HEAD), lambda j, n=n: (0, n, 0, j)),
+                    spec((QUAD, tokens, HEAD), lambda j: (0, 0, j)),
                     spec((QUAD, 1, HEAD + 8, HEAD), lambda j: (0, j, 0, 0)),
-                    spec((2, 1, HEAD, HEAD), lambda j: (0, j, 0, 0)),
                 ]
+                + [spec((2, 1, HEAD, HEAD), lambda j: (0, j, 0, 0))] * (nz - 1)
                 + [spec(piece.shape, lambda j: (0, 0, 0)) for piece in other_pieces]
                 + [anywhere],
-                out_specs=[half_spec, half_spec] + [spec((1, HEAD, HEAD), lambda j: (j, 0, 0))] * QUAD,
+                out_specs=[half_spec, half_spec, spec((QUAD, 1, HEAD, HEAD), lambda j: (0, j, 0, 0))],
                 scratch_shapes=[
-                    pltpu.VMEM((SEL * HALF, 2 * tokens), BF16),
+                    pltpu.VMEM((QUAD, SEL * HALF, 2 * tokens), BF16),
                     pltpu.VMEM((QUAD, input_spikes.shape[0], tokens), jnp.int32),
                     pltpu.VMEM((QUAD, pieces[0].shape[0] - spike_rows, tokens), F32),
-                    pltpu.VMEM((QUAD, HEAD, HEAD), F32),
                 ],
             ),
-            out_shape=[half_shape, half_shape] + [shape(chunk, HEAD, HEAD)] * QUAD,
+            out_shape=[half_shape, half_shape, shape(QUAD, chunk, HEAD, HEAD)],
             compiler_params=params(),
             cost_estimate=cost(1, 40 * mib),
             name="block_kernel",
         )(
             quad,
             core.astype(jnp.int32).reshape(1),
+            at_z,
             own_pattern,
             *pieces,
-            value_parts,
-            *adjoint_parts[n],
+            plane(value_parts[n]),
+            adjoint_parts[n],
+            *hops[n],
             *other_pieces,
             after,
         )
         adjoints.append(adjoint)
 
+        terms = [summed]
         bit = 1
         while True:
-            summed = summed + lax.ppermute(send, "ctx", [(c, c ^ (2 * bit)) for c in range(nctx)])
+            terms.append(lax.ppermute(send, "ctx", [(c, c ^ (2 * bit)) for c in range(nctx)]))
             bit *= 2
             if bit == nz:
                 break
-            rest = summed.shape[0] // 2
-            summed, send = summed[:rest], summed[rest:]
-        for i in range(QUAD):
-            part = lax.dynamic_slice_in_dim(summed, (y ^ (i % 2)) * (share // 2), share // 2, 0)
-            results.append(across(part, i) if i else part)
+            rest = terms[0].shape[0] // 2
+            send = sum(term[rest:] for term in terms)
+            terms = [term[:rest] for term in terms]
+        terms_of.append(terms)
+        if n == 0:
+            state_keep, state_send = pl.pallas_call(
+                lambda *refs: turn_kernel([part_size] * CHUNKS, *refs),
+                grid_spec=pltpu.PrefetchScalarGridSpec(
+                    num_scalar_prefetch=2,
+                    grid=(1,),
+                    in_specs=[
+                        spec((half, HEAD, HEAD), lambda j: (0, 0, 0)),
+                        spec((half, 1, HEAD), lambda j: (0, 0, 0)),
+                        anywhere,
+                    ]
+                    + [spec((part_size, HEAD, HEAD), lambda j: (0, 0, 0))] * (CHUNKS * (nz - 1)),
+                    out_specs=[spec((half, HEAD, HEAD), lambda j: (0, 0, 0))] * 2,
+                ),
+                out_shape=[shape(half, HEAD, HEAD)] * 2,
+                compiler_params=params(),
+                cost_estimate=cost(1, 6 * mib),
+                name="turn_kernel",
+            )(
+                at_z,
+                y.astype(jnp.int32).reshape(1),
+                first,
+                jnp.broadcast_to(first_decay, (half, 1, HEAD)),
+                adjoints[0],
+                *[got.reshape(part_size, HEAD, HEAD) for n in range(CHUNKS) for got in hops[n]],
+            )
+
+    state = [y.astype(jnp.int32).reshape(1), state_keep, swap(state_send)]
+    returned = [plane(adjoint) for adjoint in adjoints]
+    part_spec = spec((heads, HEAD, HEAD), lambda j: (j % 2, 0, 0))
+    h, xv = call(
+        "output_kernel",
+        lambda *refs: output_kernel(chunk, heads, *refs),
+        [part_spec] * 2 + [flat_spec] * 3 + [cum_spec] * (1 + CHUNKS) + [anywhere],
+        [col_spec, message_spec],
+        [shape(QUAD, tokens, 8), messages],
+        cost(1, 40 * mib),
+        *state,
+        local,
+        qt,
+        grad_out,
+        cum,
+        *dens,
+        returned[0],
+        scalars=1,
+    )
+    cv = carried_vectors(xv, False)[0]
+    dq, dk = call(
+        "token_kernel",
+        lambda *refs: token_kernel(chunk, heads, *refs),
+        [part_spec, part_spec, vec_spec]
+        + [flat_spec] * 4
+        + [cum_spec, flat_spec, col_spec]
+        + [cum_spec] * CHUNKS
+        + [spec((1, chunk, HEAD, HEAD), lambda j: (j, 0, 0, 0))] * CHUNKS,
+        [flat_spec, flat_spec],
+        [flat16, flat32],
+        cost(1, 60 * mib),
+        *state,
+        z0,
+        qt,
+        kt,
+        values,
+        grad_out,
+        cum,
+        query_slope,
+        h,
+        *dens,
+        *returned,
+        scalars=1,
+    )
+    results = []
+    for n in range(CHUNKS):
+        order = dq if n == CHUNKS - 1 else adjoints[-1]
+        half_spec = pl.BlockSpec((share // 2, columns, HALF, HEAD), lambda j, y: (y[0], 0, 0, 0))
+        other_spec = pl.BlockSpec((share // 2, columns, HALF, HEAD), lambda j, y: (1 - y[0], 0, 0, 0))
+        part_shape = shape(share // 2, columns, HALF, HEAD)
+        whole_spec = pl.BlockSpec(part_shape.shape, lambda j, y: (0, 0, 0, 0))
+        own, other = pl.pallas_call(
+            sum_kernel,
+            grid_spec=pltpu.PrefetchScalarGridSpec(
+                num_scalar_prefetch=1,
+                grid=(1,),
+                in_specs=[half_spec, other_spec] * len(terms_of[n]) + [anywhere],
+                out_specs=[whole_spec, whole_spec],
+            ),
+            out_shape=[part_shape, part_shape],
+            compiler_params=params(),
+            cost_estimate=cost(1, 4 * mib),
+            name="sum_kernel",
+        )(y.astype(jnp.int32).reshape(1), *[term for term in terms_of[n] for _ in range(2)], order)
+        results += [own, across(other, 1), across(own, 2), across(other, 3)]
     part_spec = spec((1, columns, HALF, HEAD), lambda j: (j, 0, 0, 0))
     value_grad = pl.pallas_call(
         finish_kernel,
@@ -621,51 +730,6 @@
         name="finish_kernel",
     )(quad, *results)
 
-    part_spec = spec((heads, HEAD, HEAD), lambda j: (j % 2, 0, 0))
-    h, xv = call(
-        "output_kernel",
-        lambda *refs: output_kernel(chunk, heads, *refs),
-        [part_spec] * 2 + [flat_spec] * 3 + [cum_spec] * (1 + CHUNKS) + [anywhere],
-        [col_spec, vec_spec],
-        [shape(QUAD, tokens, 8), vecs],
-        cost(1, 40 * mib),
-        *state,
-        local,
-        qt,
-        grad_out,
-        cum,
-        *dens,
-        adjoints[-1][0],
-        scalars=1,
-    )
-    cv = vec(carried_vectors(unvec(xv), False)[0])
-    returned = [across(adjoint[i], i) if i else adjoint[i] for adjoint in adjoints for i in range(QUAD)]
-    dq, dk = call(
-        "token_kernel",
-        lambda *refs: token_kernel(chunk, heads, *refs),
-        [part_spec, part_spec, vec_spec]
-        + [flat_spec] * 4
-        + [cum_spec, flat_spec, col_spec]
-        + [cum_spec] * CHUNKS
-        + [spec((chunk, HEAD, HEAD), lambda j: (0, 0, 0))] * (CHUNKS * QUAD),
-        [flat_spec, flat_spec],
-        [flat16, flat32],
-        cost(1, 60 * mib),
-        state[0],
-        quad,
-        *state[1:],
-        z0,
-        qt,
-        kt,
-        values,
-        grad_out,
-        cum,
-        query_slope,
-        h,
-        *dens,
-        *returned,
-        scalars=2,
-    )
     key_grad = call(
         "key_kernel",
         lambda *refs: key_kernel(heads, *refs),

time: 304 us -> 288 us (0.947)
  waiting for transfers between devices: 86 us -> 68.8 us
  Pallas kernels: 103 us -> 111 us
  other arithmetic: 25.2 us -> 19.7 us
    ppermute x6, waiting for transfers between devices: 32.7 us -> 9.37 us  [per_device(): got.append(lax.ppermute(send, 'ctx', pairs))]
    pallas_call x2 -> x7, Pallas kernels: 24.6 us -> 38.3 us  [the longest x2 24.3 us: per_device(): pl.pallas_call(lambda *refs, n=n: block_kernel(n * chunk, nz - 1, *refs),...]
    all_to_all x3 -> x6, starting transfers between devices: 12.5 us -> 24.3 us  [plane(): lax.all_to_all(value, ('dp', 'ctx'), 0, 0, axis_index_groups=planes, tile...]
    ppermute x15 -> x9, starting transfers between devices: 22.5 us -> 10.7 us  [across(): return lax.ppermute(value, ('dp', 'ctx'), pairs)]
    ppermute x4, waiting for transfers between devices: 30.8 us -> 22.5 us  [per_device(): lax.ppermute(send, 'ctx', [(c, c ^ 2 * bit) for c in range(nctx)])]
    all_to_all x3 -> x6, waiting for transfers between devices: 22.5 us -> 30 us  [plane(): lax.all_to_all(value, ('dp', 'ctx'), 0, 0, axis_index_groups=planes, tile...]
    ppermute x15 -> x9, waiting for transfers between devices: 0.04 us -> 6.9 us  [across(): return lax.ppermute(value, ('dp', 'ctx'), pairs)]
    select_n x7 -> x4, other arithmetic: 8.13 us -> 1.36 us  [the longest x2 1.35 us: carried_vectors(): jnp.where(inside, parts[at, :, 8:] * reach + parts[at, :, :8], reach)]
  transfers between devices with their start and end apart: 33 -> 30, of which waited for: 9 -> 9; matrix products, arithmetic and copies ran while one was open for 12% -> 10% of each run, Pallas kernels for 28% -> 36%
where the time goes in v4:
time: 288 us; the launch traced here: 284 us
  Pallas kernels  111 us (39%)
  waiting for transfers between devices  68.8 us (24%)
  starting transfers between devices  66.1 us (23%)
  other arithmetic  19.7 us (7%)
  local copies, waits for them, and re-layouts  17.8 us (6%)
    pallas_call x8, Pallas kernels, call(): pl.pallas_call(body, grid_spec=pltpu.PrefetchScalarGridSpec(num_scalar_pr...  64 us
    all_to_all x6, waiting for transfers between devices, plane(): lax.all_to_all(value, ('dp', 'ctx'), 0, 0, axis_index_groups=planes, tile...  30 us
    pallas_call x2, Pallas kernels, per_device(): pl.pallas_call(lambda *refs, n=n: block_kernel(n * chunk, nz - 1, *refs),...  24.3 us
    all_to_all x6, starting transfers between devices, plane(): lax.all_to_all(value, ('dp', 'ctx'), 0, 0, axis_index_groups=planes, tile...  24.3 us
    ppermute x4, waiting for transfers between devices, per_device(): lax.ppermute(send, 'ctx', [(c, c ^ 2 * bit) for c in range(nctx)])  22.5 us
    all_to_all x2, starting transfers between devices, carried_vectors(): parts = lax.all_to_all(message, 'ctx', 0, 0, tiled=True)  12.9 us
    ppermute x9, starting transfers between devices, across(): return lax.ppermute(value, ('dp', 'ctx'), pairs)  10.7 us
    ppermute x6, waiting for transfers between devices, per_device(): got.append(lax.ppermute(send, 'ctx', pairs))  9.37 us
  transfers between devices with their start and end apart: 30, of which 9 were waited for; matrix products, arithmetic and copies ran while one was open for 10% of the time, Pallas kernels for 36%

profile of v4, /device:TPU:24, one launch (start us, length us, event | category | flops | bytes accessed | tf_op | source)
XLA Modules:
  0.0 284.3 jit_solution(13419635073127784337)
XLA Ops:
  2.9 3.6 %key_sums_kernel.1 = f32[8,4,16,128]{3,2,1,0:T(8,128)} custom-call(s32[256,256]{1,0:T(8,128)} %refs_1_.8, f32[4,8,256]{2,1,0:T(8,128)} %reduce_window_sum.16.refs_2_.refs_1_.refs_6_.refs_8_), custom_call_target="tpu_custom_call" | custom-call | flops 1 | bytes 1 | tf_op jit(solution)/shard_map/key_sums_kernel/pallas_call | solution.py:363
  6.6 6.1 %all-to-all-start = ((f32[8,4,16,128]{3,2,1,0:T(8,128)}), f32[8,4,16,128]{3,2,1,0:T(8,128)S(1)}, u32[]{:S(2)}, u32[]{:S(2)}) async-start(f32[8,4,16,128]{3,2,1,0:T(8,128)} %key_sums_kernel.1), calls=%async_computation | async-start | bytes 524288 | tf_op jit(solution)/shard_map/all_to_all | solution.py:393
  24.0 6.3 %weight_kernel.1 = (bf16[32,256,256]{2,1,0:T(8,128)(2,1)}, f32[4,8,256]{2,1,0:T(8,128)}, bf16[256,4096]{1,0:T(8,128)(2,1)}, bf16[256,4096]{1,0:T(8,128)(2,1)}) custom-call(s32[256,256]{1,0:T(8,128)} %refs_0_.11, s32[256,256]{1,0:T(8,128)} %refs_1_.8, f32[4,8,256]{2,1,0:T(8,128)} %reduce_window_sum.16.refs_2_.refs_1_.refs_6_.refs_8_), custom_call_target="tpu_custom_call" | custom-call | flops 1 | bytes 1 | tf_op jit(solution)/shard_map/weight_kernel/pallas_call | solution.py:363
  31.0 6.4 %adjoint_kernel.3 = (f32[4,8,256]{2,1,0:T(8,128)}, f32[4,4,136,128]{3,2,1,0:T(8,128)}, f32[4,256,512]{2,1,0:T(8,128)}) custom-call(s32[256,256]{1,0:T(8,128)} %refs_0_.11, bf16[256,4096]{1,0:T(8,128)(2,1)} %refs_7_.1, f32[4,8,256]{2,1,0:T(8,128)} %reduce_window_sum.16.refs_2_.refs_1_.refs_6_.refs_8_, f32[4,8,256]{2,1,0:T(8,128)} %get-tuple-element.33.refs_3_, ...), custom_call_target="tpu_custom_call" | custom-call | flops 1 | bytes 1 | tf_op jit(solution)/shard_map/adjoint_kernel/pallas_call | solution.py:363
  46.6 6.3 %adjoint_kernel.2 = (f32[4,8,256]{2,1,0:T(8,128)}, f32[4,4,136,128]{3,2,1,0:T(8,128)}, f32[4,256,512]{2,1,0:T(8,128)}) custom-call(s32[256,256]{1,0:T(8,128)} %refs_0_.11, bf16[256,4096]{1,0:T(8,128)(2,1)} %refs_7_.1, f32[4,8,256]{2,1,0:T(8,128)} %reduce_window_sum.16.refs_2_.refs_1_.refs_6_.refs_8_, f32[4,8,256]{2,1,0:T(8,128)} %get-tuple-element.33.refs_3_, ...), custom_call_target="tpu_custom_call" | custom-call | flops 1 | bytes 1 | tf_op jit(solution)/shard_map/adjoint_kernel/pallas_call | solution.py:363
  52.9 15.0 %all-to-all-done.3.received.refs_9_ = f32[4,4,136,128]{3,2,1,0:T(8,128)S(1)} async-done(((f32[4,4,136,128]{3,2,1,0:T(8,128)}), f32[4,4,136,128]{3,2,1,0:T(8,128)S(1)}, u32[]{:S(2)}, u32[]{:S(2)}) %all-to-all-start.3) | async-done | bytes 1114144 | tf_op jit(solution)/shard_map/all_to_all | solution.py:387
  68.9 3.7 %all-to-all-start.2 = ((f32[4,4,136,128]{3,2,1,0:T(8,128)}), f32[4,4,136,128]{3,2,1,0:T(8,128)S(1)}, u32[]{:S(2)}, u32[]{:S(2)}) async-start(f32[4,4,136,128]{3,2,1,0:T(8,128)} %get-tuple-element.36), calls=%async_computation.2 | async-start | bytes 2228224 | tf_op jit(solution)/shard_map/all_to_all | solution.py:387
  75.3 11.8 %all-to-all-done.2.received.order.refs_9_.refs_14_ = f32[4,4,136,128]{3,2,1,0:T(8,128)S(1)} async-done(((f32[4,4,136,128]{3,2,1,0:T(8,128)}), f32[4,4,136,128]{3,2,1,0:T(8,128)S(1)}, u32[]{:S(2)}, u32[]{:S(2)}) %all-to-all-start.2) | async-done | bytes 1114144 | tf_op jit(solution)/shard_map/all_to_all | solution.py:387
  88.2 4.5 %all-to-all-start.1 = ((f32[4,256,512]{2,1,0:T(8,128)}), f32[4,256,512]{2,1,0:T(8,128)}, u32[]{:S(2)}, u32[]{:S(2)}) async-start(f32[4,256,512]{2,1,0:T(8,128)} %get-tuple-element.35), calls=%async_computation.1 | async-start | bytes 4194304 | tf_op jit(solution)/shard_map/all_to_all | solution.py:387
  103.0 6.0 %local_kernel.1.order.refs_3_ = f32[256,4096]{1,0:T(8,128)} custom-call(bf16[32,256,256]{2,1,0:T(8,128)(2,1)} %get-tuple-element.34.refs_5_.refs_0_, bf16[256,4096]{1,0:T(8,128)(2,1)} %refs_6_.1, f32[4,4,136,128]{3,2,1,0:T(8,128)} %get-tuple-element.40.refs_2_, f32[4,256,256]{2,1,0:T(8,128)} %collective-permute-done.7.refs_13_.refs_3_), custom_call_target="tpu_custom_call" | custom-call | flops 1 | bytes 1 | tf_op jit(solution)/shard_map/local_kernel/pallas_call | solution.py:363
  117.7 4.6 %all-to-all-start.5 = ((f32[4,256,512]{2,1,0:T(8,128)}), f32[4,256,512]{2,1,0:T(8,128)}, u32[]{:S(2)}, u32[]{:S(2)}) async-start(f32[4,256,512]{2,1,0:T(8,128)} %get-tuple-element.50), calls=%async_computation.5 | async-start | bytes 4194304 | tf_op jit(solution)/shard_map/all_to_all | solution.py:387
  134.7 8.2 %collective-permute-done.6.refs_12_ = f32[2,4,128,128]{3,2,1,0:T(8,128)S(1)} collective-permute-done((f32[2,4,128,128]{3,2,1,0:T(8,128)}, f32[2,4,128,128]{3,2,1,0:T(8,128)S(1)}, u32[]{:S(2)}, u32[]{:S(2)}) %collective-permute-start.6) | collective-permute-done | bytes 524320 | tf_op jit(solution)/shard_map/ppermute | solution.py:560
  143.7 12.1 %block_kernel.2 = (f32[8,8,32,128]{3,2,1,0:T(8,128)}, f32[8,8,32,128]{3,2,1,0:T(8,128)}, f32[4,4,128,128]{3,2,1,0:T(8,128)}) custom-call(s32[1]{0:T(128)} %bitcast.4.refs_0_.quad, s32[1]{0:T(128)} %bitcast.5.refs_1_, s32[1]{0:T(128)} %bitcast.1.z.refs_2_.refs_0_, s32[16,16]{1,0:T(8,128)} %select_bitcast_fusion.refs_3_, ...), custom_call_target="tpu_custom_call" | custom-call | flops 1 | bytes 41943040 | tf_op jit(solution)/shard_map/block_kernel/pallas_call | solution.py:577
  158.8 3.8 %all-to-all-start.4 = ((f32[4,4,128,128]{3,2,1,0:T(8,128)}), f32[4,4,128,128]{3,2,1,0:T(8,128)S(1)}, u32[]{:S(2)}, u32[]{:S(2)}) async-start(f32[4,4,128,128]{3,2,1,0:T(8,128)} %get-tuple-element.39.refs_4_), calls=%async_computation.4 | async-start | bytes 2097152 | tf_op jit(solution)/shard_map/all_to_all | solution.py:387
  163.4 3.7 %turn_kernel.1 = (f32[16,128,128]{2,1,0:T(8,128)}, f32[16,128,128]{2,1,0:T(8,128)}) custom-call(s32[1]{0:T(128)} %bitcast.1.z.refs_2_.refs_0_, s32[1]{0:T(128)} %bitcast.side.refs_1_.refs_0_.y, f32[16,128,128]{2,1,0:T(8,128)} %get-tuple-element.66.refs_2_, f32[16,1,128]{2,1,0:T(1,128)} %broadcast_in_dim.28.refs_3_, ...), custom_call_target="tpu_custom_call" | custom-call | flops 1 | bytes 6291456 | tf_op jit(solution)/shard_map/turn_kernel/pallas_call | solution.py:627
  167.1 12.2 %block_kernel.3 = (f32[8,8,32,128]{3,2,1,0:T(8,128)}, f32[8,8,32,128]{3,2,1,0:T(8,128)}, f32[4,4,128,128]{3,2,1,0:T(8,128)}) custom-call(s32[1]{0:T(128)} %bitcast.4.refs_0_.quad, s32[1]{0:T(128)} %bitcast.5.refs_1_, s32[1]{0:T(128)} %bitcast.1.z.refs_2_.refs_0_, s32[16,16]{1,0:T(8,128)} %select_bitcast_fusion.refs_3_, ...), custom_call_target="tpu_custom_call" | custom-call | flops 1 | bytes 41943040 | tf_op jit(solution)/shard_map/block_kernel/pallas_call | solution.py:577
  181.5 4.3 %all-to-all-start.6 = ((f32[4,4,128,128]{3,2,1,0:T(8,128)}), f32[4,4,128,128]{3,2,1,0:T(8,128)}, u32[]{:S(2)}, u32[]{:S(2)}) async-start(f32[4,4,128,128]{3,2,1,0:T(8,128)} %get-tuple-element.51.refs_6_), calls=%async_computation.6 | async-start | bytes 2097152 | tf_op jit(solution)/shard_map/all_to_all | solution.py:387
  191.0 22.5 %collective-permute-done.17 = f32[8,8,32,128]{3,2,1,0:T(8,128)} collective-permute-done((f32[8,8,32,128]{3,2,1,0:T(8,128)}, f32[8,8,32,128]{3,2,1,0:T(8,128)}, u32[]{:S(2)}, u32[]{:S(2)}) %collective-permute-start.17) | collective-permute-done | bytes 1048608 | tf_op jit(solution)/shard_map/ppermute | solution.py:618
  216.7 12.9 %output_kernel.1 = (f32[4,256,8]{2,1,0:T(8,128)}, f32[8,4,16,128]{3,2,1,0:T(8,128)}) custom-call(s32[1]{0:T(128)} %bitcast.side.refs_1_.refs_0_.y, f32[16,128,128]{2,1,0:T(8,128)} %get-tuple-element.43.refs_1_.refs_14_, f32[16,128,128]{2,1,0:T(8,128)} %collective-permute-done.11.refs_2_, f32[256,4096]{1,0:T(8,128)} %local_kernel.1.order.refs_3_, ...), custom_call_target="tpu_custom_call" | custom-call | flops 1 | bytes 41943040 | tf_op jit(solution)/shard_map/output_kernel/pallas_call | solution.py:363
  229.7 6.8 %all-to-all-start.7 = ((f32[8,4,16,128]{3,2,1,0:T(8,128)}), f32[8,4,16,128]{3,2,1,0:T(8,128)S(1)}, u32[]{:S(2)}, u32[]{:S(2)}) async-start(f32[8,4,16,128]{3,2,1,0:T(8,128)} %get-tuple-element.54), calls=%async_computation.7 | async-start | bytes 524288 | tf_op jit(solution)/shard_map/all_to_all | solution.py:393
  240.9 16.7 %token_kernel.1 = (bf16[256,4096]{1,0:T(8,128)(2,1)}, f32[256,4096]{1,0:T(8,128)}) custom-call(s32[1]{0:T(128)} %bitcast.side.refs_1_.refs_0_.y, f32[16,128,128]{2,1,0:T(8,128)} %get-tuple-element.43.refs_1_.refs_14_, f32[16,128,128]{2,1,0:T(8,128)} %collective-permute-done.11.refs_2_, f32[4,8,128]{2,1,0:T(8,128)} %fusion.24.refs_4_.refs_3_, ...), custom_call_target="tpu_custom_call" | custom-call | flops 1 | bytes 62914560 | tf_op jit(solution)/shard_map/token_kernel/pallas_call | solution.py:363
  267.1 5.7 %key_kernel.1 = bf16[256,4096]{1,0:T(8,128)(2,1)} custom-call(f32[256,4096]{1,0:T(8,128)} %get-tuple-element.53.refs_0_, f32[4,8,128]{2,1,0:T(8,128)} %fusion.1.refs_1_, f32[4,8,256]{2,1,0:T(8,128)} %reduce_window_sum.16.refs_2_.refs_1_.refs_6_.refs_8_, bf16[256,4096]{1,0:T(8,128)(2,1)} %refs_3_.1), custom_call_target="tpu_custom_call" | custom-call | flops 1 | bytes 8388608 | tf_op jit(solution)/shard_map/key_kernel/pallas_call | solution.py:363
  273.1 3.8 %collective-permute-done.20.refs_6_ = f32[2,8,32,128]{3,2,1,0:T(8,128)S(1)} collective-permute-done((f32[2,8,32,128]{3,2,1,0:T(8,128)}, f32[2,8,32,128]{3,2,1,0:T(8,128)S(1)}, u32[]{:S(2)}, u32[]{:S(2)}) %collective-permute-start.20) | collective-permute-done | bytes 262176 | tf_op jit(solution)/shard_map/ppermute | solution.py:384
  280.4 3.7 %finish_kernel.1 = f32[2,64,4096]{2,1,0:T(8,128)} custom-call(s32[1]{0:T(128)} %bitcast.4.refs_0_.quad, f32[2,8,32,128]{3,2,1,0:T(8,128)} %get-tuple-element.57.refs_0_, f32[2,8,32,128]{3,2,1,0:T(8,128)} %copy-done.28, f32[2,8,32,128]{3,2,1,0:T(8,128)} %collective-permute-done.15.refs_2_, f32[2,8,32,128]{3,2,1,0:T(8,128)} %collective-permute-done.16.refs_3_, ...), custom_call_target="tpu_custom_call" | custom-call | flops 1 | bytes 4194304 | tf_op jit(solution)/shard_map/finish_kernel/pallas_call | solution.py:719
  (176 shorter events, 92.3 us)
Async XLA Ops:
  6.6 23.7 %all-to-all-start = ((f32[8,4,16,128]{3,2,1,0:T(8,128)}), f32[8,4,16,128]{3,2,1,0:T(8,128)S(1)}, u32[]{:S(2)}, u32[]{:S(2)}) async-start(f32[8,4,16,128]{3,2,1,0:T(8,128)} %key_sums_kernel.1), calls=%async_computation | async-start | bytes 524288 | tf_op jit(solution)/shard_map/all_to_all | solution.py:393
  16.1 29.7 %collective-permute-start.3 = (f32[328,256]{1,0:T(8,128)}, f32[328,256]{1,0:T(8,128)S(1)}, u32[]{:S(2)}, u32[]{:S(2)}) collective-permute-start(f32[328,256]{1,0:T(8,128)} %get-tuple-element.67), channel_id=1, source_target_pairs={{0,18},{2,16},{4,22},{6,20},{8,26},{10,24},{12,30},{14,28},{16,2},... | collective-permute-start | bytes 1007624 | tf_op jit(solution)/shard_map/ppermute | solution.py:384
  18.5 54.0 %collective-permute-start.2 = (f32[328,256]{1,0:T(8,128)}, f32[328,256]{1,0:T(8,128)S(1)}, u32[]{:S(2)}, u32[]{:S(2)}) collective-permute-start(f32[328,256]{1,0:T(8,128)} %get-tuple-element.68), channel_id=1, source_target_pairs={{0,16},{2,18},{4,20},{6,22},{8,24},{10,26},{12,28},{14,30},{16,0},... | collective-permute-start | bytes 1007624 | tf_op jit(solution)/shard_map/ppermute | solution.py:384
  19.0 53.5 %collective-permute-start.1 = (f32[328,256]{1,0:T(8,128)}, f32[328,256]{1,0:T(8,128)}, u32[]{:S(2)}, u32[]{:S(2)}) collective-permute-start(f32[328,256]{1,0:T(8,128)} %get-tuple-element.69), channel_id=1, source_target_pairs={{0,2},{2,0},{4,6},{6,4},{8,10},{10,8},{12,14},{14,12},{16,18},{18,... | collective-permute-start | bytes 1007624 | tf_op jit(solution)/shard_map/ppermute | solution.py:384
  22.6 70.1 %collective-permute-start = (f32[16,128,128]{2,1,0:T(8,128)}, f32[16,128,128]{2,1,0:T(8,128)}, u32[]{:S(2)}, u32[]{:S(2)}) collective-permute-start(f32[16,128,128]{2,1,0:T(8,128)} %state_kernel.3), channel_id=1, source_target_pairs={{0,2},{2,0},{4,6},{6,4},{8,10},{10,8},{12,14},{14,12},{1,3},{3,1},... | collective-permute-start | bytes 3145736 | tf_op jit(solution)/shard_map/ppermute | solution.py:376
  37.4 30.5 %all-to-all-start.3 = ((f32[4,4,136,128]{3,2,1,0:T(8,128)}), f32[4,4,136,128]{3,2,1,0:T(8,128)S(1)}, u32[]{:S(2)}, u32[]{:S(2)}) async-start(f32[4,4,136,128]{3,2,1,0:T(8,128)} %get-tuple-element.40.refs_2_), calls=%async_computation.3 | async-start | bytes 2228224 | tf_op jit(solution)/shard_map/all_to_all | solution.py:387
  68.9 18.3 %all-to-all-start.2 = ((f32[4,4,136,128]{3,2,1,0:T(8,128)}), f32[4,4,136,128]{3,2,1,0:T(8,128)S(1)}, u32[]{:S(2)}, u32[]{:S(2)}) async-start(f32[4,4,136,128]{3,2,1,0:T(8,128)} %get-tuple-element.36), calls=%async_computation.2 | async-start | bytes 2228224 | tf_op jit(solution)/shard_map/all_to_all | solution.py:387
  74.8 28.2 %collective-permute-start.7 = (f32[4,256,256]{2,1,0:T(8,128)}, f32[4,256,256]{2,1,0:T(8,128)}, u32[]{:S(2)}, u32[]{:S(2)}) collective-permute-start(f32[4,256,256]{2,1,0:T(8,128)} %pad_maximum_fusion.1), channel_id=1, source_target_pairs={{0,1},{1,0},{2,3},{3,2},{4,5},{5,4},{6,7},{7,6},{8,9},{9,8},{10,11... | collective-permute-start | bytes 3145736 | tf_op jit(solution)/shard_map/ppermute | solution.py:428
  88.2 29.6 %all-to-all-start.1 = ((f32[4,256,512]{2,1,0:T(8,128)}), f32[4,256,512]{2,1,0:T(8,128)}, u32[]{:S(2)}, u32[]{:S(2)}) async-start(f32[4,256,512]{2,1,0:T(8,128)} %get-tuple-element.35), calls=%async_computation.1 | async-start | bytes 4194304 | tf_op jit(solution)/shard_map/all_to_all | solution.py:387
  98.3 14.5 %collective-permute-start.4 = (f32[2,4,128,128]{3,2,1,0:T(8,128)}, f32[2,4,128,128]{3,2,1,0:T(8,128)S(1)}, u32[]{:S(2)}, u32[]{:S(2)}) collective-permute-start(f32[2,4,128,128]{3,2,1,0:T(8,128)} %get-tuple-element.37), channel_id=1, source_target_pairs={{0,4},{2,6},{12,8},{14,10},{1,5},{3,7},{13,9},{15,11},{16,20},{18,... | collective-permute-start | bytes 1572872 | tf_op jit(solution)/shard_map/ppermute | solution.py:560
  117.7 41.1 %all-to-all-start.5 = ((f32[4,256,512]{2,1,0:T(8,128)}), f32[4,256,512]{2,1,0:T(8,128)}, u32[]{:S(2)}, u32[]{:S(2)}) async-start(f32[4,256,512]{2,1,0:T(8,128)} %get-tuple-element.50), calls=%async_computation.5 | async-start | bytes 4194304 | tf_op jit(solution)/shard_map/all_to_all | solution.py:387
  128.7 14.2 %collective-permute-start.6 = (f32[2,4,128,128]{3,2,1,0:T(8,128)}, f32[2,4,128,128]{3,2,1,0:T(8,128)S(1)}, u32[]{:S(2)}, u32[]{:S(2)}) collective-permute-start(f32[2,4,128,128]{3,2,1,0:T(8,128)} %multiply_add_fusion.2), channel_id=1, source_target_pairs={{4,0},{6,2},{8,12},{10,14},{5,1},{7,3},{9,13},{11,15},{20,16},{22,... | collective-permute-start | bytes 1572872 | tf_op jit(solution)/shard_map/ppermute | solution.py:560
  132.1 30.5 %collective-permute-start.10 = (f32[2,4,128,128]{3,2,1,0:T(8,128)}, f32[2,4,128,128]{3,2,1,0:T(8,128)S(1)}, u32[]{:S(2)}, u32[]{:S(2)}) collective-permute-start(f32[2,4,128,128]{3,2,1,0:T(8,128)} %multiply_add_fusion), channel_id=1, source_target_pairs={{4,0},{6,2},{8,12},{10,14},{5,1},{7,3},{9,13},{11,15},{20,16},{22,... | collective-permute-start | bytes 1572872 | tf_op jit(solution)/shard_map/ppermute | solution.py:560
  155.8 29.9 %collective-permute-start.12 = (f32[8,8,32,128]{3,2,1,0:T(8,128)}, f32[8,8,32,128]{3,2,1,0:T(8,128)}, u32[]{:S(2)}, u32[]{:S(2)}) collective-permute-start(f32[8,8,32,128]{3,2,1,0:T(8,128)} %get-tuple-element.56), channel_id=1, source_target_pairs={{0,4},{2,6},{4,0},{6,2},{8,12},{10,14},{12,8},{14,10},{1,5},{3,7},... | collective-permute-start | bytes 3145736 | tf_op jit(solution)/shard_map/ppermute | solution.py:618
  158.8 22.7 %all-to-all-start.4 = ((f32[4,4,128,128]{3,2,1,0:T(8,128)}), f32[4,4,128,128]{3,2,1,0:T(8,128)S(1)}, u32[]{:S(2)}, u32[]{:S(2)}) async-start(f32[4,4,128,128]{3,2,1,0:T(8,128)} %get-tuple-element.39.refs_4_), calls=%async_computation.4 | async-start | bytes 2097152 | tf_op jit(solution)/shard_map/all_to_all | solution.py:387
  179.3 34.3 %collective-permute-start.17 = (f32[8,8,32,128]{3,2,1,0:T(8,128)}, f32[8,8,32,128]{3,2,1,0:T(8,128)}, u32[]{:S(2)}, u32[]{:S(2)}) collective-permute-start(f32[8,8,32,128]{3,2,1,0:T(8,128)} %get-tuple-element.60), channel_id=1, source_target_pairs={{0,4},{2,6},{4,0},{6,2},{8,12},{10,14},{12,8},{14,10},{1,5},{3,7},... | collective-permute-start | bytes 3145736 | tf_op jit(solution)/shard_map/ppermute | solution.py:618
  179.4 37.3 %collective-permute-start.11 = (f32[16,128,128]{2,1,0:T(8,128)}, f32[16,128,128]{2,1,0:T(8,128)}, u32[]{:S(2)}, u32[]{:S(2)}) collective-permute-start(f32[16,128,128]{2,1,0:T(8,128)} %get-tuple-element.44), channel_id=1, source_target_pairs={{0,2},{2,0},{4,6},{6,4},{8,10},{10,8},{12,14},{14,12},{1,3},{3,1},... | collective-permute-start | bytes 3145736 | tf_op jit(solution)/shard_map/ppermute | solution.py:376
  181.5 48.2 %all-to-all-start.6 = ((f32[4,4,128,128]{3,2,1,0:T(8,128)}), f32[4,4,128,128]{3,2,1,0:T(8,128)}, u32[]{:S(2)}, u32[]{:S(2)}) async-start(f32[4,4,128,128]{3,2,1,0:T(8,128)} %get-tuple-element.51.refs_6_), calls=%async_computation.6 | async-start | bytes 2097152 | tf_op jit(solution)/shard_map/all_to_all | solution.py:387
  188.2 48.2 %collective-permute-start.13 = (f32[4,8,32,128]{3,2,1,0:T(8,128)}, f32[4,8,32,128]{3,2,1,0:T(8,128)S(1)}, u32[]{:S(2)}, u32[]{:S(2)}) collective-permute-start(f32[4,8,32,128]{3,2,1,0:T(8,128)} %get-tuple-element.78), channel_id=1, source_target_pairs={{0,8},{2,10},{4,12},{6,14},{8,0},{10,2},{12,4},{14,6},{1,9},{3,11}... | collective-permute-start | bytes 1572872 | tf_op jit(solution)/shard_map/ppermute | solution.py:618
  215.9 44.1 %collective-permute-start.18 = (f32[4,8,32,128]{3,2,1,0:T(8,128)S(1)}, f32[4,8,32,128]{3,2,1,0:T(8,128)S(1)}, u32[]{:S(2)}, u32[]{:S(2)}) collective-permute-start(f32[4,8,32,128]{3,2,1,0:T(8,128)S(1)} %get-tuple-element.75), channel_id=1, source_target_pairs={{0,8},{2,10},{4,12},{6,14},{8,0},{10,2},{12,4},{14,6},{1,9},{3,11}... | collective-permute-start | bytes 1572872 | tf_op jit(solution)/shard_map/ppermute | solution.py:618
  229.7 36.8 %all-to-all-start.7 = ((f32[8,4,16,128]{3,2,1,0:T(8,128)}), f32[8,4,16,128]{3,2,1,0:T(8,128)S(1)}, u32[]{:S(2)}, u32[]{:S(2)}) async-start(f32[8,4,16,128]{3,2,1,0:T(8,128)} %get-tuple-element.54), calls=%async_computation.7 | async-start | bytes 524288 | tf_op jit(solution)/shard_map/all_to_all | solution.py:393
  239.5 26.9 %collective-permute-start.14 = (f32[2,8,32,128]{3,2,1,0:T(8,128)}, f32[2,8,32,128]{3,2,1,0:T(8,128)S(1)}, u32[]{:S(2)}, u32[]{:S(2)}) collective-permute-start(f32[2,8,32,128]{3,2,1,0:T(8,128)} %get-tuple-element.58), channel_id=1, source_target_pairs={{0,2},{2,0},{4,6},{6,4},{8,10},{10,8},{12,14},{14,12},{16,18},{18,... | collective-permute-start | bytes 786440 | tf_op jit(solution)/shard_map/ppermute | solution.py:384
  257.7 15.4 %collective-permute-start.16 = (f32[2,8,32,128]{3,2,1,0:T(8,128)}, f32[2,8,32,128]{3,2,1,0:T(8,128)}, u32[]{:S(2)}, u32[]{:S(2)}) collective-permute-start(f32[2,8,32,128]{3,2,1,0:T(8,128)} %get-tuple-element.58), channel_id=1, source_target_pairs={{0,18},{2,16},{4,22},{6,20},{8,26},{10,24},{12,30},{14,28},{16,2},... | collective-permute-start | bytes 786440 | tf_op jit(solution)/shard_map/ppermute | solution.py:384
  266.4 13.3 %collective-permute-start.21 = (f32[2,8,32,128]{3,2,1,0:T(8,128)}, f32[2,8,32,128]{3,2,1,0:T(8,128)S(1)}, u32[]{:S(2)}, u32[]{:S(2)}) collective-permute-start(f32[2,8,32,128]{3,2,1,0:T(8,128)} %get-tuple-element.62), channel_id=1, source_target_pairs={{0,18},{2,16},{4,22},{6,20},{8,26},{10,24},{12,30},{14,28},{16,2},... | collective-permute-start | bytes 786440 | tf_op jit(solution)/shard_map/ppermute | solution.py:384
  (40 other events, 296.6 us)

commit v5 on v4

--- a/solution.py
+++ b/solution.py
@@ -132,6 +132,11 @@
             later = decay[at] * reach + first[at]
             keep_out[at] = jnp.where(y[0] == 0, reach, later)
             send_out[at] = jnp.where(y[0] == 0, later, reach)
+
+
+def half_kernel(*refs):
+    terms, out = refs[:-2], refs[-1]
+    out[...] = sum((term[...] for term in terms[1:]), terms[0][...])
 
 
 def sum_kernel(y, *refs):
@@ -613,15 +618,7 @@
         adjoints.append(adjoint)
 
         terms = [summed]
-        bit = 1
-        while True:
-            terms.append(lax.ppermute(send, "ctx", [(c, c ^ (2 * bit)) for c in range(nctx)]))
-            bit *= 2
-            if bit == nz:
-                break
-            rest = terms[0].shape[0] // 2
-            send = sum(term[rest:] for term in terms)
-            terms = [term[:rest] for term in terms]
+        terms.append(lax.ppermute(send, "ctx", [(c, c ^ 2) for c in range(nctx)]))
         terms_of.append(terms)
         if n == 0:
             state_keep, state_send = pl.pallas_call(
@@ -669,6 +666,26 @@
         returned[0],
         scalars=1,
     )
+    bit, rest, order = 2, SEL // 4, terms_of[1][0]
+    while bit < nz:
+        for n in range(CHUNKS):
+            part_shape = (rest, columns, HALF, HEAD)
+            send = pl.pallas_call(
+                half_kernel,
+                grid=(1,),
+                in_specs=[spec(part_shape, lambda j: (1, 0, 0, 0))] * len(terms_of[n]) + [anywhere],
+                out_specs=spec(part_shape, lambda j: (0, 0, 0, 0)),
+                out_shape=shape(*part_shape),
+                compiler_params=params(),
+                cost_estimate=cost(1, 1),
+                name="half_kernel",
+            )(*terms_of[n], order)
+            order = h
+            terms_of[n].append(
+                lax.ppermute(send, "ctx", [(c, c ^ (2 * bit)) for c in range(nctx)])
+            )
+        bit *= 2
+        rest //= 2
     cv = carried_vectors(xv, False)[0]
     dq, dk = call(
         "token_kernel",

time: 288 us -> 286 us (level)
  other arithmetic: 19.7 us -> 13.6 us
  Pallas kernels: 111 us -> 115 us
    ppermute x4 -> x2, waiting for transfers between devices: 22.5 us -> 0.01 us  [per_device(): lax.ppermute(send, 'ctx', [(c, c ^ 2 * bit) for c in range(nctx)])]
    ppermute x6, waiting for transfers between devices: 9.37 us -> 18.9 us  [per_device(): got.append(lax.ppermute(send, 'ctx', pairs))]
    ppermute x2, waiting for transfers between devices: 0.01 us -> 9.01 us  [swap(): return lax.ppermute(value, 'ctx', [(c, c ^ 1) for c in range(nctx)])]
    add x2 -> x0, other arithmetic: 4.83 us -> none  [per_device(): send = sum((term[rest:] for term in terms))]
    pallas_call x0 -> x2, Pallas kernels: none -> 4.12 us  [per_device(): pl.pallas_call(half_kernel, grid=(1,), in_specs=[spec(part_shape, lambda...]
    ppermute x4 -> x2, starting transfers between devices: 6.62 us -> 2.98 us  [per_device(): lax.ppermute(send, 'ctx', [(c, c ^ 2 * bit) for c in range(nctx)])]
    unnamed x72 -> x70, local copies, waits for them, and re-layouts: 7.4 us -> 7.68 us
  transfers between devices with their start and end apart: 30 -> 30, of which waited for: 9 -> 9; matrix products, arithmetic and copies ran while one was open for 10% -> 8% of each run, Pallas kernels for 36% -> 38%
where the time goes in v5:
time: 286 us; the launch traced here: 283 us
  Pallas kernels  115 us (40%)
  waiting for transfers between devices  69.5 us (24%)
  starting transfers between devices  65.6 us (23%)
  local copies, waits for them, and re-layouts  18.1 us (6%)
  other arithmetic  13.6 us (5%)
    pallas_call x8, Pallas kernels, call(): pl.pallas_call(body, grid_spec=pltpu.PrefetchScalarGridSpec(num_scalar_pr...  63.9 us
    all_to_all x6, waiting for transfers between devices, plane(): lax.all_to_all(value, ('dp', 'ctx'), 0, 0, axis_index_groups=planes, tile...  31.8 us
    all_to_all x6, starting transfers between devices, plane(): lax.all_to_all(value, ('dp', 'ctx'), 0, 0, axis_index_groups=planes, tile...  24.9 us
    pallas_call x2, Pallas kernels, per_device(): pl.pallas_call(lambda *refs, n=n: block_kernel(n * chunk, nz - 1, *refs),...  24.4 us
    ppermute x6, waiting for transfers between devices, per_device(): got.append(lax.ppermute(send, 'ctx', pairs))  18.9 us
    all_to_all x2, starting transfers between devices, carried_vectors(): parts = lax.all_to_all(message, 'ctx', 0, 0, tiled=True)  13.1 us
    ppermute x9, starting transfers between devices, across(): return lax.ppermute(value, ('dp', 'ctx'), pairs)  10.5 us
    ppermute x2, waiting for transfers between devices, swap(): return lax.ppermute(value, 'ctx', [(c, c ^ 1) for c in range(nctx)])  9.01 us
  transfers between devices with their start and end apart: 30, of which 9 were waited for; matrix products, arithmetic and copies ran while one was open for 8% of the time, Pallas kernels for 38%

profile of v5, /device:TPU:24, one launch (start us, length us, event | category | flops | bytes accessed | tf_op | source)
XLA Modules:
  0.0 282.5 jit_solution(9867870725713347068)
XLA Ops:
  2.9 3.6 %key_sums_kernel.1 = f32[8,4,16,128]{3,2,1,0:T(8,128)} custom-call(s32[256,256]{1,0:T(8,128)} %refs_1_.8, f32[4,8,256]{2,1,0:T(8,128)} %reduce_window_sum.16.refs_2_.refs_1_.refs_6_.refs_8_), custom_call_target="tpu_custom_call" | custom-call | flops 1 | bytes 1 | tf_op jit(solution)/shard_map/key_sums_kernel/pallas_call | solution.py:368
  6.6 6.1 %all-to-all-start = ((f32[8,4,16,128]{3,2,1,0:T(8,128)}), f32[8,4,16,128]{3,2,1,0:T(8,128)S(1)}, u32[]{:S(2)}, u32[]{:S(2)}) async-start(f32[8,4,16,128]{3,2,1,0:T(8,128)} %key_sums_kernel.1), calls=%async_computation | async-start | bytes 524288 | tf_op jit(solution)/shard_map/all_to_all | solution.py:398
  24.0 6.3 %weight_kernel.1 = (bf16[32,256,256]{2,1,0:T(8,128)(2,1)}, f32[4,8,256]{2,1,0:T(8,128)}, bf16[256,4096]{1,0:T(8,128)(2,1)}, bf16[256,4096]{1,0:T(8,128)(2,1)}) custom-call(s32[256,256]{1,0:T(8,128)} %refs_0_.11, s32[256,256]{1,0:T(8,128)} %refs_1_.8, f32[4,8,256]{2,1,0:T(8,128)} %reduce_window_sum.16.refs_2_.refs_1_.refs_6_.refs_8_), custom_call_target="tpu_custom_call" | custom-call | flops 1 | bytes 1 | tf_op jit(solution)/shard_map/weight_kernel/pallas_call | solution.py:368
  30.9 6.4 %adjoint_kernel.3 = (f32[4,8,256]{2,1,0:T(8,128)}, f32[4,4,136,128]{3,2,1,0:T(8,128)}, f32[4,256,512]{2,1,0:T(8,128)}) custom-call(s32[256,256]{1,0:T(8,128)} %refs_0_.11, bf16[256,4096]{1,0:T(8,128)(2,1)} %refs_7_.1, f32[4,8,256]{2,1,0:T(8,128)} %reduce_window_sum.16.refs_2_.refs_1_.refs_6_.refs_8_, f32[4,8,256]{2,1,0:T(8,128)} %get-tuple-element.33.refs_3_, ...), custom_call_target="tpu_custom_call" | custom-call | flops 1 | bytes 1 | tf_op jit(solution)/shard_map/adjoint_kernel/pallas_call | solution.py:368
  46.5 6.3 %adjoint_kernel.2 = (f32[4,8,256]{2,1,0:T(8,128)}, f32[4,4,136,128]{3,2,1,0:T(8,128)}, f32[4,256,512]{2,1,0:T(8,128)}) custom-call(s32[256,256]{1,0:T(8,128)} %refs_0_.11, bf16[256,4096]{1,0:T(8,128)(2,1)} %refs_7_.1, f32[4,8,256]{2,1,0:T(8,128)} %reduce_window_sum.16.refs_2_.refs_1_.refs_6_.refs_8_, f32[4,8,256]{2,1,0:T(8,128)} %get-tuple-element.33.refs_3_, ...), custom_call_target="tpu_custom_call" | custom-call | flops 1 | bytes 1 | tf_op jit(solution)/shard_map/adjoint_kernel/pallas_call | solution.py:368
  52.8 15.0 %all-to-all-done.3.received.refs_9_ = f32[4,4,136,128]{3,2,1,0:T(8,128)S(1)} async-done(((f32[4,4,136,128]{3,2,1,0:T(8,128)}), f32[4,4,136,128]{3,2,1,0:T(8,128)S(1)}, u32[]{:S(2)}, u32[]{:S(2)}) %all-to-all-start.3) | async-done | bytes 1114144 | tf_op jit(solution)/shard_map/all_to_all | solution.py:392
  68.9 3.7 %all-to-all-start.2 = ((f32[4,4,136,128]{3,2,1,0:T(8,128)}), f32[4,4,136,128]{3,2,1,0:T(8,128)S(1)}, u32[]{:S(2)}, u32[]{:S(2)}) async-start(f32[4,4,136,128]{3,2,1,0:T(8,128)} %get-tuple-element.36), calls=%async_computation.2 | async-start | bytes 2228224 | tf_op jit(solution)/shard_map/all_to_all | solution.py:392
  75.1 12.1 %all-to-all-done.2.received.order.refs_9_.refs_14_ = f32[4,4,136,128]{3,2,1,0:T(8,128)S(1)} async-done(((f32[4,4,136,128]{3,2,1,0:T(8,128)}), f32[4,4,136,128]{3,2,1,0:T(8,128)S(1)}, u32[]{:S(2)}, u32[]{:S(2)}) %all-to-all-start.2) | async-done | bytes 1114144 | tf_op jit(solution)/shard_map/all_to_all | solution.py:392
  88.1 4.4 %all-to-all-start.1 = ((f32[4,256,512]{2,1,0:T(8,128)}), f32[4,256,512]{2,1,0:T(8,128)}, u32[]{:S(2)}, u32[]{:S(2)}) async-start(f32[4,256,512]{2,1,0:T(8,128)} %get-tuple-element.35), calls=%async_computation.1 | async-start | bytes 4194304 | tf_op jit(solution)/shard_map/all_to_all | solution.py:392
  103.2 6.0 %local_kernel.1.order.refs_3_ = f32[256,4096]{1,0:T(8,128)} custom-call(bf16[32,256,256]{2,1,0:T(8,128)(2,1)} %get-tuple-element.34.refs_5_.refs_0_, bf16[256,4096]{1,0:T(8,128)(2,1)} %refs_6_.1, f32[4,4,136,128]{3,2,1,0:T(8,128)} %get-tuple-element.40.refs_2_, f32[4,256,256]{2,1,0:T(8,128)} %collective-permute-done.7.refs_13_.refs_3_), custom_call_target="tpu_custom_call" | custom-call | flops 1 | bytes 1 | tf_op jit(solution)/shard_map/local_kernel/pallas_call | solution.py:368
  112.9 4.7 %all-to-all-done.1.refs_8_ = f32[4,256,512]{2,1,0:T(8,128)} async-done(((f32[4,256,512]{2,1,0:T(8,128)}), f32[4,256,512]{2,1,0:T(8,128)}, u32[]{:S(2)}, u32[]{:S(2)}) %all-to-all-start.1) | async-done | bytes 2097184 | tf_op jit(solution)/shard_map/all_to_all | solution.py:392
  117.7 4.6 %all-to-all-start.5 = ((f32[4,256,512]{2,1,0:T(8,128)}), f32[4,256,512]{2,1,0:T(8,128)}, u32[]{:S(2)}, u32[]{:S(2)}) async-start(f32[4,256,512]{2,1,0:T(8,128)} %get-tuple-element.50), calls=%async_computation.5 | async-start | bytes 4194304 | tf_op jit(solution)/shard_map/all_to_all | solution.py:392
  134.6 18.9 %collective-permute-done.6.refs_12_ = f32[2,4,128,128]{3,2,1,0:T(8,128)S(1)} collective-permute-done((f32[2,4,128,128]{3,2,1,0:T(8,128)}, f32[2,4,128,128]{3,2,1,0:T(8,128)S(1)}, u32[]{:S(2)}, u32[]{:S(2)}) %collective-permute-start.6) | collective-permute-done | bytes 524320 | tf_op jit(solution)/shard_map/ppermute | solution.py:565
  154.4 12.2 %block_kernel.2 = (f32[8,8,32,128]{3,2,1,0:T(8,128)}, f32[8,8,32,128]{3,2,1,0:T(8,128)}, f32[4,4,128,128]{3,2,1,0:T(8,128)}) custom-call(s32[1]{0:T(128)} %bitcast.4.refs_0_.quad, s32[1]{0:T(128)} %bitcast.5.refs_1_, s32[1]{0:T(128)} %bitcast.1.z.refs_2_.refs_0_, s32[16,16]{1,0:T(8,128)} %select_bitcast_fusion.refs_3_, ...), custom_call_target="tpu_custom_call" | custom-call | flops 1 | bytes 41943040 | tf_op jit(solution)/shard_map/block_kernel/pallas_call | solution.py:582
  166.5 4.5 %all-to-all-start.4 = ((f32[4,4,128,128]{3,2,1,0:T(8,128)}), f32[4,4,128,128]{3,2,1,0:T(8,128)}, u32[]{:S(2)}, u32[]{:S(2)}) async-start(f32[4,4,128,128]{3,2,1,0:T(8,128)} %get-tuple-element.39.refs_4_), calls=%async_computation.4 | async-start | bytes 2097152 | tf_op jit(solution)/shard_map/all_to_all | solution.py:392
  171.9 3.7 %turn_kernel.1 = (f32[16,128,128]{2,1,0:T(8,128)}, f32[16,128,128]{2,1,0:T(8,128)}) custom-call(s32[1]{0:T(128)} %bitcast.1.z.refs_2_.refs_0_, s32[1]{0:T(128)} %bitcast.side.refs_1_.refs_0_.y, f32[16,128,128]{2,1,0:T(8,128)} %get-tuple-element.66.refs_2_, f32[16,1,128]{2,1,0:T(1,128)} %broadcast_in_dim.28.refs_3_, ...), custom_call_target="tpu_custom_call" | custom-call | flops 1 | bytes 6291456 | tf_op jit(solution)/shard_map/turn_kernel/pallas_call | solution.py:624
  177.3 12.2 %block_kernel.3 = (f32[8,8,32,128]{3,2,1,0:T(8,128)}, f32[8,8,32,128]{3,2,1,0:T(8,128)}, f32[4,4,128,128]{3,2,1,0:T(8,128)}) custom-call(s32[1]{0:T(128)} %bitcast.4.refs_0_.quad, s32[1]{0:T(128)} %bitcast.5.refs_1_, s32[1]{0:T(128)} %bitcast.1.z.refs_2_.refs_0_, s32[16,16]{1,0:T(8,128)} %select_bitcast_fusion.refs_3_, ...), custom_call_target="tpu_custom_call" | custom-call | flops 1 | bytes 41943040 | tf_op jit(solution)/shard_map/block_kernel/pallas_call | solution.py:582
  191.5 4.3 %all-to-all-start.6 = ((f32[4,4,128,128]{3,2,1,0:T(8,128)}), f32[4,4,128,128]{3,2,1,0:T(8,128)}, u32[]{:S(2)}, u32[]{:S(2)}) async-start(f32[4,4,128,128]{3,2,1,0:T(8,128)} %get-tuple-element.51.refs_6_), calls=%async_computation.6 | async-start | bytes 2097152 | tf_op jit(solution)/shard_map/all_to_all | solution.py:392
  201.1 9.0 %collective-permute-done.11.refs_2_ = f32[16,128,128]{2,1,0:T(8,128)} collective-permute-done((f32[16,128,128]{2,1,0:T(8,128)}, f32[16,128,128]{2,1,0:T(8,128)}, u32[]{:S(2)}, u32[]{:S(2)}) %collective-permute-start.11) | collective-permute-done | bytes 1048608 | tf_op jit(solution)/shard_map/ppermute | solution.py:381
  210.1 13.0 %output_kernel.1 = (f32[4,256,8]{2,1,0:T(8,128)}, f32[8,4,16,128]{3,2,1,0:T(8,128)}) custom-call(s32[1]{0:T(128)} %bitcast.side.refs_1_.refs_0_.y, f32[16,128,128]{2,1,0:T(8,128)} %get-tuple-element.43.refs_1_.refs_14_, f32[16,128,128]{2,1,0:T(8,128)} %collective-permute-done.11.refs_2_, f32[256,4096]{1,0:T(8,128)} %local_kernel.1.order.refs_3_, ...), custom_call_target="tpu_custom_call" | custom-call | flops 1 | bytes 41943040 | tf_op jit(solution)/shard_map/output_kernel/pallas_call | solution.py:368
  228.7 7.0 %all-to-all-start.7 = ((f32[8,4,16,128]{3,2,1,0:T(8,128)}), f32[8,4,16,128]{3,2,1,0:T(8,128)S(1)}, u32[]{:S(2)}, u32[]{:S(2)}) async-start(f32[8,4,16,128]{3,2,1,0:T(8,128)} %get-tuple-element.54), calls=%async_computation.7 | async-start | bytes 524288 | tf_op jit(solution)/shard_map/all_to_all | solution.py:398
  240.2 16.7 %token_kernel.1 = (bf16[256,4096]{1,0:T(8,128)(2,1)}, f32[256,4096]{1,0:T(8,128)}) custom-call(s32[1]{0:T(128)} %bitcast.side.refs_1_.refs_0_.y, f32[16,128,128]{2,1,0:T(8,128)} %get-tuple-element.43.refs_1_.refs_14_, f32[16,128,128]{2,1,0:T(8,128)} %collective-permute-done.11.refs_2_, f32[4,8,128]{2,1,0:T(8,128)} %fusion.24.refs_4_.refs_3_, ...), custom_call_target="tpu_custom_call" | custom-call | flops 1 | bytes 62914560 | tf_op jit(solution)/shard_map/token_kernel/pallas_call | solution.py:368
  266.1 5.7 %key_kernel.1 = bf16[256,4096]{1,0:T(8,128)(2,1)} custom-call(f32[256,4096]{1,0:T(8,128)} %get-tuple-element.53.refs_0_, f32[4,8,128]{2,1,0:T(8,128)} %fusion.1.refs_1_, f32[4,8,256]{2,1,0:T(8,128)} %reduce_window_sum.16.refs_2_.refs_1_.refs_6_.refs_8_, bf16[256,4096]{1,0:T(8,128)(2,1)} %refs_3_.1), custom_call_target="tpu_custom_call" | custom-call | flops 1 | bytes 8388608 | tf_op jit(solution)/shard_map/key_kernel/pallas_call | solution.py:368
  278.7 3.7 %finish_kernel.1 = f32[2,64,4096]{2,1,0:T(8,128)} custom-call(s32[1]{0:T(128)} %bitcast.4.refs_0_.quad, f32[2,8,32,128]{3,2,1,0:T(8,128)} %get-tuple-element.58.refs_0_, f32[2,8,32,128]{3,2,1,0:T(8,128)} %copy-done.26, f32[2,8,32,128]{3,2,1,0:T(8,128)} %copy-done.28, f32[2,8,32,128]{3,2,1,0:T(8,128)} %copy-done.27, ...), custom_call_target="tpu_custom_call" | custom-call | flops 1 | bytes 4194304 | tf_op jit(solution)/shard_map/finish_kernel/pallas_call | solution.py:736
  (174 shorter events, 91.4 us)
Async XLA Ops:
  6.6 23.7 %all-to-all-start = ((f32[8,4,16,128]{3,2,1,0:T(8,128)}), f32[8,4,16,128]{3,2,1,0:T(8,128)S(1)}, u32[]{:S(2)}, u32[]{:S(2)}) async-start(f32[8,4,16,128]{3,2,1,0:T(8,128)} %key_sums_kernel.1), calls=%async_computation | async-start | bytes 524288 | tf_op jit(solution)/shard_map/all_to_all | solution.py:398
  16.1 29.7 %collective-permute-start.3 = (f32[328,256]{1,0:T(8,128)}, f32[328,256]{1,0:T(8,128)S(1)}, u32[]{:S(2)}, u32[]{:S(2)}) collective-permute-start(f32[328,256]{1,0:T(8,128)} %get-tuple-element.67), channel_id=1, source_target_pairs={{0,18},{2,16},{4,22},{6,20},{8,26},{10,24},{12,30},{14,28},{16,2},... | collective-permute-start | bytes 1007624 | tf_op jit(solution)/shard_map/ppermute | solution.py:389
  18.5 54.1 %collective-permute-start.2 = (f32[328,256]{1,0:T(8,128)}, f32[328,256]{1,0:T(8,128)S(1)}, u32[]{:S(2)}, u32[]{:S(2)}) collective-permute-start(f32[328,256]{1,0:T(8,128)} %get-tuple-element.68), channel_id=1, source_target_pairs={{0,16},{2,18},{4,20},{6,22},{8,24},{10,26},{12,28},{14,30},{16,0},... | collective-permute-start | bytes 1007624 | tf_op jit(solution)/shard_map/ppermute | solution.py:389
  19.0 53.6 %collective-permute-start.1 = (f32[328,256]{1,0:T(8,128)}, f32[328,256]{1,0:T(8,128)}, u32[]{:S(2)}, u32[]{:S(2)}) collective-permute-start(f32[328,256]{1,0:T(8,128)} %get-tuple-element.69), channel_id=1, source_target_pairs={{0,2},{2,0},{4,6},{6,4},{8,10},{10,8},{12,14},{14,12},{16,18},{18,... | collective-permute-start | bytes 1007624 | tf_op jit(solution)/shard_map/ppermute | solution.py:389
  22.5 70.4 %collective-permute-start = (f32[16,128,128]{2,1,0:T(8,128)}, f32[16,128,128]{2,1,0:T(8,128)}, u32[]{:S(2)}, u32[]{:S(2)}) collective-permute-start(f32[16,128,128]{2,1,0:T(8,128)} %state_kernel.3), channel_id=1, source_target_pairs={{0,2},{2,0},{4,6},{6,4},{8,10},{10,8},{12,14},{14,12},{1,3},{3,1},... | collective-permute-start | bytes 3145736 | tf_op jit(solution)/shard_map/ppermute | solution.py:381
  37.4 30.5 %all-to-all-start.3 = ((f32[4,4,136,128]{3,2,1,0:T(8,128)}), f32[4,4,136,128]{3,2,1,0:T(8,128)S(1)}, u32[]{:S(2)}, u32[]{:S(2)}) async-start(f32[4,4,136,128]{3,2,1,0:T(8,128)} %get-tuple-element.40.refs_2_), calls=%async_computation.3 | async-start | bytes 2228224 | tf_op jit(solution)/shard_map/all_to_all | solution.py:392
  68.9 18.3 %all-to-all-start.2 = ((f32[4,4,136,128]{3,2,1,0:T(8,128)}), f32[4,4,136,128]{3,2,1,0:T(8,128)S(1)}, u32[]{:S(2)}, u32[]{:S(2)}) async-start(f32[4,4,136,128]{3,2,1,0:T(8,128)} %get-tuple-element.36), calls=%async_computation.2 | async-start | bytes 2228224 | tf_op jit(solution)/shard_map/all_to_all | solution.py:392
  74.8 28.4 %collective-permute-start.7 = (f32[4,256,256]{2,1,0:T(8,128)}, f32[4,256,256]{2,1,0:T(8,128)}, u32[]{:S(2)}, u32[]{:S(2)}) collective-permute-start(f32[4,256,256]{2,1,0:T(8,128)} %pad_maximum_fusion.1), channel_id=1, source_target_pairs={{0,1},{1,0},{2,3},{3,2},{4,5},{5,4},{6,7},{7,6},{8,9},{9,8},{10,11... | collective-permute-start | bytes 3145736 | tf_op jit(solution)/shard_map/ppermute | solution.py:433
  88.1 29.5 %all-to-all-start.1 = ((f32[4,256,512]{2,1,0:T(8,128)}), f32[4,256,512]{2,1,0:T(8,128)}, u32[]{:S(2)}, u32[]{:S(2)}) async-start(f32[4,256,512]{2,1,0:T(8,128)} %get-tuple-element.35), calls=%async_computation.1 | async-start | bytes 4194304 | tf_op jit(solution)/shard_map/all_to_all | solution.py:392
  98.6 23.7 %collective-permute-start.4 = (f32[2,4,128,128]{3,2,1,0:T(8,128)}, f32[2,4,128,128]{3,2,1,0:T(8,128)S(1)}, u32[]{:S(2)}, u32[]{:S(2)}) collective-permute-start(f32[2,4,128,128]{3,2,1,0:T(8,128)} %get-tuple-element.37), channel_id=1, source_target_pairs={{0,4},{2,6},{12,8},{14,10},{1,5},{3,7},{13,9},{15,11},{16,20},{18,... | collective-permute-start | bytes 1572872 | tf_op jit(solution)/shard_map/ppermute | solution.py:565
  117.7 48.8 %all-to-all-start.5 = ((f32[4,256,512]{2,1,0:T(8,128)}), f32[4,256,512]{2,1,0:T(8,128)}, u32[]{:S(2)}, u32[]{:S(2)}) async-start(f32[4,256,512]{2,1,0:T(8,128)} %get-tuple-element.50), calls=%async_computation.5 | async-start | bytes 4194304 | tf_op jit(solution)/shard_map/all_to_all | solution.py:392
  128.6 24.9 %collective-permute-start.6 = (f32[2,4,128,128]{3,2,1,0:T(8,128)}, f32[2,4,128,128]{3,2,1,0:T(8,128)S(1)}, u32[]{:S(2)}, u32[]{:S(2)}) collective-permute-start(f32[2,4,128,128]{3,2,1,0:T(8,128)} %multiply_add_fusion.2), channel_id=1, source_target_pairs={{4,0},{6,2},{8,12},{10,14},{5,1},{7,3},{9,13},{11,15},{20,16},{22,... | collective-permute-start | bytes 1572872 | tf_op jit(solution)/shard_map/ppermute | solution.py:565
  132.7 38.4 %collective-permute-start.10 = (f32[2,4,128,128]{3,2,1,0:T(8,128)}, f32[2,4,128,128]{3,2,1,0:T(8,128)S(1)}, u32[]{:S(2)}, u32[]{:S(2)}) collective-permute-start(f32[2,4,128,128]{3,2,1,0:T(8,128)} %multiply_add_fusion), channel_id=1, source_target_pairs={{4,0},{6,2},{8,12},{10,14},{5,1},{7,3},{9,13},{11,15},{20,16},{22,... | collective-permute-start | bytes 1572872 | tf_op jit(solution)/shard_map/ppermute | solution.py:565
  166.5 25.0 %all-to-all-start.4 = ((f32[4,4,128,128]{3,2,1,0:T(8,128)}), f32[4,4,128,128]{3,2,1,0:T(8,128)}, u32[]{:S(2)}, u32[]{:S(2)}) async-start(f32[4,4,128,128]{3,2,1,0:T(8,128)} %get-tuple-element.39.refs_4_), calls=%async_computation.4 | async-start | bytes 2097152 | tf_op jit(solution)/shard_map/all_to_all | solution.py:392
  171.0 24.8 %collective-permute-start.12 = (f32[8,8,32,128]{3,2,1,0:T(8,128)}, f32[8,8,32,128]{3,2,1,0:T(8,128)S(1)}, u32[]{:S(2)}, u32[]{:S(2)}) collective-permute-start(f32[8,8,32,128]{3,2,1,0:T(8,128)} %get-tuple-element.56), channel_id=1, source_target_pairs={{0,4},{2,6},{4,0},{6,2},{8,12},{10,14},{12,8},{14,10},{1,5},{3,7},... | collective-permute-start | bytes 3145736 | tf_op jit(solution)/shard_map/ppermute | solution.py:621
  175.6 34.5 %collective-permute-start.11 = (f32[16,128,128]{2,1,0:T(8,128)}, f32[16,128,128]{2,1,0:T(8,128)}, u32[]{:S(2)}, u32[]{:S(2)}) collective-permute-start(f32[16,128,128]{2,1,0:T(8,128)} %get-tuple-element.44), channel_id=1, source_target_pairs={{0,2},{2,0},{4,6},{6,4},{8,10},{10,8},{12,14},{14,12},{1,3},{3,1},... | collective-permute-start | bytes 3145736 | tf_op jit(solution)/shard_map/ppermute | solution.py:381
  189.5 36.4 %collective-permute-start.17 = (f32[8,8,32,128]{3,2,1,0:T(8,128)}, f32[8,8,32,128]{3,2,1,0:T(8,128)}, u32[]{:S(2)}, u32[]{:S(2)}) collective-permute-start(f32[8,8,32,128]{3,2,1,0:T(8,128)} %get-tuple-element.60), channel_id=1, source_target_pairs={{0,4},{2,6},{4,0},{6,2},{8,12},{10,14},{12,8},{14,10},{1,5},{3,7},... | collective-permute-start | bytes 3145736 | tf_op jit(solution)/shard_map/ppermute | solution.py:621
  191.5 37.1 %all-to-all-start.6 = ((f32[4,4,128,128]{3,2,1,0:T(8,128)}), f32[4,4,128,128]{3,2,1,0:T(8,128)}, u32[]{:S(2)}, u32[]{:S(2)}) async-start(f32[4,4,128,128]{3,2,1,0:T(8,128)} %get-tuple-element.51.refs_6_), calls=%async_computation.6 | async-start | bytes 2097152 | tf_op jit(solution)/shard_map/all_to_all | solution.py:392
  198.9 36.8 %collective-permute-start.13 = (f32[4,8,32,128]{3,2,1,0:T(8,128)}, f32[4,8,32,128]{3,2,1,0:T(8,128)S(1)}, u32[]{:S(2)}, u32[]{:S(2)}) collective-permute-start(f32[4,8,32,128]{3,2,1,0:T(8,128)} %half_kernel.2), channel_id=1, source_target_pairs={{0,8},{2,10},{4,12},{6,14},{8,0},{10,2},{12,4},{14,6},{1,9},{3,11}... | collective-permute-start | bytes 1572872 | tf_op jit(solution)/shard_map/ppermute | solution.py:685
  228.0 30.9 %collective-permute-start.18 = (f32[4,8,32,128]{3,2,1,0:T(8,128)}, f32[4,8,32,128]{3,2,1,0:T(8,128)S(1)}, u32[]{:S(2)}, u32[]{:S(2)}) collective-permute-start(f32[4,8,32,128]{3,2,1,0:T(8,128)} %half_kernel.3), channel_id=1, source_target_pairs={{0,8},{2,10},{4,12},{6,14},{8,0},{10,2},{12,4},{14,6},{1,9},{3,11}... | collective-permute-start | bytes 1572872 | tf_op jit(solution)/shard_map/ppermute | solution.py:685
  228.7 36.8 %all-to-all-start.7 = ((f32[8,4,16,128]{3,2,1,0:T(8,128)}), f32[8,4,16,128]{3,2,1,0:T(8,128)S(1)}, u32[]{:S(2)}, u32[]{:S(2)}) async-start(f32[8,4,16,128]{3,2,1,0:T(8,128)} %get-tuple-element.54), calls=%async_computation.7 | async-start | bytes 524288 | tf_op jit(solution)/shard_map/all_to_all | solution.py:398
  238.7 26.2 %collective-permute-start.14 = (f32[2,8,32,128]{3,2,1,0:T(8,128)}, f32[2,8,32,128]{3,2,1,0:T(8,128)S(1)}, u32[]{:S(2)}, u32[]{:S(2)}) collective-permute-start(f32[2,8,32,128]{3,2,1,0:T(8,128)} %get-tuple-element.59), channel_id=1, source_target_pairs={{0,2},{2,0},{4,6},{6,4},{8,10},{10,8},{12,14},{14,12},{16,18},{18,... | collective-permute-start | bytes 786440 | tf_op jit(solution)/shard_map/ppermute | solution.py:389
  256.8 15.1 %collective-permute-start.16 = (f32[2,8,32,128]{3,2,1,0:T(8,128)}, f32[2,8,32,128]{3,2,1,0:T(8,128)S(1)}, u32[]{:S(2)}, u32[]{:S(2)}) collective-permute-start(f32[2,8,32,128]{3,2,1,0:T(8,128)} %get-tuple-element.59), channel_id=1, source_target_pairs={{0,18},{2,16},{4,22},{6,20},{8,26},{10,24},{12,30},{14,28},{16,2},... | collective-permute-start | bytes 786440 | tf_op jit(solution)/shard_map/ppermute | solution.py:389
  264.9 13.7 %collective-permute-start.21 = (f32[2,8,32,128]{3,2,1,0:T(8,128)}, f32[2,8,32,128]{3,2,1,0:T(8,128)}, u32[]{:S(2)}, u32[]{:S(2)}) collective-permute-start(f32[2,8,32,128]{3,2,1,0:T(8,128)} %get-tuple-element.62), channel_id=1, source_target_pairs={{0,18},{2,16},{4,22},{6,20},{8,26},{10,24},{12,30},{14,28},{16,2},... | collective-permute-start | bytes 786440 | tf_op jit(solution)/shard_map/ppermute | solution.py:389
  (39 other events, 263.5 us)
